TPU v7x, 32 devices: a whole 2x2x4 slice. The times are simulated.
32 devices in a mesh: dp: 4 (over z), tensor: 8 (over y, x, core).
Axes of the slice: x: 2, y: 2, z: 4, core: 2. Of those that a mesh axis runs over, the one named last changes fastest.
Arguments:
- hidden_in: bfloat16 [6144, 2048], P(('dp', 'tensor')), may hold values from -6 to 6
- doc_ids: int32 [4, 1536], P('dp'), may hold values from 0 to 11, never falling along the last dimension, each value on 1 to 384 neighbouring positions
- query_weight: bfloat16 [2048, 2048], P(None, 'tensor'), may hold values from -1 to 1
- key_weight: bfloat16 [2048, 2048], P(None, 'tensor'), may hold values from -1 to 1
- value_weight: bfloat16 [2048, 2048], P(None, 'tensor'), may hold values from -0.125 to 0.125
- output_weight: bfloat16 [2048, 2048], P('tensor'), may hold values from -0.125 to 0.125
- gate_weight: bfloat16 [2048, 8192], P(None, 'tensor'), may hold values from -0.125 to 0.125
- up_weight: bfloat16 [2048, 8192], P(None, 'tensor'), may hold values from -0.125 to 0.125
- down_weight: bfloat16 [8192, 2048], P('tensor'), may hold values from -0.0625 to 0.0625
- query_gain: float32 [2048], P('tensor'), may hold values from 0.1 to 1.9
- key_gain: float32 [2048], P('tensor'), may hold values from 0.1 to 1.9
- attention_gain: float32 [2048], replicated, may hold values from 0.5 to 1.5
- feedforward_gain: float32 [2048], replicated, may hold values from 0.5 to 1.5
- out_grad: bfloat16 [6144, 2048], P(('dp', 'tensor')), may hold values from -6 to 6
Outputs:
- result: float32 [6144, 2048], P(('dp', 'tensor'))
- input_grad: float32 [6144, 2048], P(('dp', 'tensor'))
- query_weight_grad: float32 [2048, 2048], P('dp', 'tensor')
- key_weight_grad: float32 [2048, 2048], P('dp', 'tensor')
- value_weight_grad: float32 [2048, 2048], P('dp', 'tensor')
- output_weight_grad: float32 [2048, 2048], P('tensor', 'dp')
- gate_weight_grad: float32 [2048, 8192], P('dp', 'tensor')
- up_weight_grad: float32 [2048, 8192], P('dp', 'tensor')
- down_weight_grad: float32 [8192, 2048], P('tensor', 'dp')
- query_gain_grad: float32 [2048], replicated
- key_gain_grad: float32 [2048], replicated
- attention_gain_grad: float32 [2048], replicated
- feedforward_gain_grad: float32 [2048], replicated
All inputs are finite; a program needn't handle non-finite values.
Results may differ from a plain program's by a relative error of at most 0.015.
The roundings to bfloat16 on the way count: a program that leaves them out, or rounds other values in their place, can miss the bound.
Values may be sent and summed in bfloat16 or wider, within the bound.
No kernel may reach another device: no remote copies, remote signals or barrier semaphores. Data moves between devices by JAX's collectives and lax.ppermute only.
A program may use at most 256 MiB of HBM per device.

v0:
```python
import jax
import jax.numpy as jnp
from jax import lax
from jax.sharding import PartitionSpec as P

HEAD_DIM = 128


norm_eps = 1e-06
rope_base = 500000.0


def contract_rows(left, right):
    return lax.dot_general(
        left, right, (((0,), (0,)), ((), ())), preferred_element_type=jnp.float32
    )


def times_transposed(left, right):
    return lax.dot_general(
        left, right, (((1,), (1,)), ((), ())), preferred_element_type=jnp.float32
    )


def rope_tables(length, head_dim):
    half = head_dim // 2
    freq = rope_base ** (-(2.0 * jnp.arange(half, dtype=jnp.float32)) / head_dim)
    angle = jnp.arange(length, dtype=jnp.float32)[:, None] * freq[None, :]
    cosine = jnp.concatenate([jnp.cos(angle), jnp.cos(angle)], axis=1)
    sine = jnp.concatenate([jnp.sin(angle), jnp.sin(angle)], axis=1)
    return (cosine[:, None, :], sine[:, None, :])


def rotate(value, cosine, sine):
    half = value.shape[-1] // 2
    turned = jnp.concatenate([-value[..., half:], value[..., :half]], axis=-1)
    return value * cosine + turned * sine


def rotate_back(grad, cosine, sine):
    moved = grad * sine
    half = grad.shape[-1] // 2
    turned = jnp.concatenate([moved[..., half:], -moved[..., :half]], axis=-1)
    return grad * cosine + turned


def norm_back(grad, unit, inverse, gain):
    inner = grad * gain
    return inverse * (inner - unit * jnp.mean(inner * unit, axis=1, keepdims=True))


def masked_scores(query_block, key, rows, doc_block, documents, scale):
    scores = (
        jnp.einsum("bhd,lhd->hbl", query_block, key, preferred_element_type=jnp.float32) * scale
    )
    columns = jnp.arange(key.shape[0])
    allowed = (columns[None, :] <= rows[:, None]) & (documents[None, :] == doc_block[:, None])
    return jnp.where(allowed[None], scores, -1e30)


def body(
    hidden_in,
    doc_ids,
    query_weight,
    key_weight,
    value_weight,
    output_weight,
    gate_weight,
    up_weight,
    down_weight,
    query_gain,
    key_gain,
    attention_gain,
    feedforward_gain,
    out_grad,
):
    width = hidden_in.shape[1]
    head_dim = HEAD_DIM
    local_width = query_weight.shape[1]
    local_heads = local_width // head_dim
    documents = doc_ids[0]
    length = documents.shape[0]
    span = min(512, length)
    count = length // span
    scale = head_dim ** (-0.5)
    cosine, sine = rope_tables(length, head_dim)
    gathered = lax.all_gather(hidden_in, "tensor", axis=0, tiled=True)
    query_raw = jnp.dot(gathered, query_weight, preferred_element_type=jnp.float32)
    key_raw = jnp.dot(gathered, key_weight, preferred_element_type=jnp.float32)
    value = jnp.dot(gathered, value_weight, preferred_element_type=jnp.float32).astype(jnp.bfloat16)
    squares = lax.psum(
        (jnp.sum(query_raw * query_raw, axis=1), jnp.sum(key_raw * key_raw, axis=1)), "tensor"
    )
    query_scale = lax.rsqrt(squares[0] / width + norm_eps)[:, None]
    key_scale = lax.rsqrt(squares[1] / width + norm_eps)[:, None]
    query_unit = query_raw * query_scale
    key_unit = key_raw * key_scale
    query = rotate(
        (query_unit * query_gain).reshape(length, local_heads, head_dim), cosine, sine
    ).astype(jnp.bfloat16)
    key = rotate((key_unit * key_gain).reshape(length, local_heads, head_dim), cosine, sine).astype(
        jnp.bfloat16
    )
    value_heads = value.reshape(length, local_heads, head_dim)

    def forward_block(index):
        start = index * span
        query_block = lax.dynamic_slice_in_dim(query, start, span, 0)
        rows = start + jnp.arange(span)
        doc_block = lax.dynamic_slice_in_dim(documents, start, span, 0)
        scores = masked_scores(query_block, key, rows, doc_block, documents, scale)
        top = jnp.max(scores, axis=-1, keepdims=True)
        weights = jnp.exp(scores - top)
        total = jnp.sum(weights, axis=-1, keepdims=True)
        shares = (weights / total).astype(jnp.bfloat16)
        output = jnp.einsum("hbl,lhd->bhd", shares, value_heads, preferred_element_type=jnp.float32)
        return (output.astype(jnp.bfloat16), (top + jnp.log(total))[..., 0])

    attended_blocks, logsum = lax.map(forward_block, jnp.arange(count))
    attended = attended_blocks.reshape(length, local_width)
    part = attended
    attn_proj = lax.psum_scatter(
        jnp.dot(part, output_weight, preferred_element_type=jnp.float32),
        "tensor",
        scatter_dimension=0,
        tiled=True,
    )
    attn_scale = lax.rsqrt(jnp.mean(attn_proj * attn_proj, axis=1, keepdims=True) + norm_eps)
    attn_unit = attn_proj * attn_scale
    middle = hidden_in.astype(jnp.float32) + attn_unit * attention_gain
    middle_all = lax.all_gather(middle.astype(jnp.bfloat16), "tensor", axis=0, tiled=True)
    gate = jnp.dot(middle_all, gate_weight, preferred_element_type=jnp.float32)
    up = jnp.dot(middle_all, up_weight, preferred_element_type=jnp.float32)
    sigma = jax.nn.sigmoid(gate)
    silu_gate = gate * sigma
    activated = (silu_gate * up).astype(jnp.bfloat16)
    part = activated
    mlp_proj = lax.psum_scatter(
        jnp.dot(part, down_weight, preferred_element_type=jnp.float32),
        "tensor",
        scatter_dimension=0,
        tiled=True,
    )
    mlp_scale = lax.rsqrt(jnp.mean(mlp_proj * mlp_proj, axis=1, keepdims=True) + norm_eps)
    mlp_unit = mlp_proj * mlp_scale
    result = middle + mlp_unit * feedforward_gain
    grad_out = out_grad.astype(jnp.float32)
    grad_mlp = norm_back(grad_out, mlp_unit, mlp_scale, feedforward_gain).astype(jnp.bfloat16)
    feedforward_part = jnp.sum(grad_out * mlp_unit, axis=0)
    grad_mlp_all = lax.all_gather(grad_mlp, "tensor", axis=0, tiled=True)
    down_grad = contract_rows(activated, grad_mlp_all)
    grad_act = times_transposed(grad_mlp_all, down_weight)
    grad_gate = (grad_act * up * sigma * (1.0 + gate * (1.0 - sigma))).astype(jnp.bfloat16)
    grad_up = (grad_act * silu_gate).astype(jnp.bfloat16)
    gate_grad = contract_rows(middle_all, grad_gate)
    up_grad = contract_rows(middle_all, grad_up)
    grad_middle = grad_out + lax.psum_scatter(
        times_transposed(grad_gate, gate_weight) + times_transposed(grad_up, up_weight),
        "tensor",
        scatter_dimension=0,
        tiled=True,
    )
    grad_proj = norm_back(grad_middle, attn_unit, attn_scale, attention_gain).astype(jnp.bfloat16)
    attention_part = jnp.sum(grad_middle * attn_unit, axis=0)
    grad_proj_all = lax.all_gather(grad_proj, "tensor", axis=0, tiled=True)
    output_grad = contract_rows(attended, grad_proj_all)
    grad_attended = times_transposed(grad_proj_all, output_weight).astype(jnp.bfloat16)
    grad_attended_heads = grad_attended.reshape(length, local_heads, head_dim)

    def backward_block(carry, inputs):
        grad_key_sum, grad_value_sum = carry
        index, block_logsum = inputs
        start = index * span
        query_block = lax.dynamic_slice_in_dim(query, start, span, 0)
        rows = start + jnp.arange(span)
        doc_block = lax.dynamic_slice_in_dim(documents, start, span, 0)
        scores = masked_scores(query_block, key, rows, doc_block, documents, scale)
        chances = jnp.exp(scores - block_logsum[..., None])
        shares = chances.astype(jnp.bfloat16)
        grad_block = lax.dynamic_slice_in_dim(grad_attended_heads, start, span, 0)
        grad_shares = jnp.einsum(
            "bhd,lhd->hbl", grad_block, value_heads, preferred_element_type=jnp.float32
        )
        offset = jnp.sum(chances * grad_shares, axis=-1, keepdims=True)
        grad_scores = (chances * (grad_shares - offset)).astype(jnp.bfloat16)
        grad_query_block = (
            jnp.einsum("hbl,lhd->bhd", grad_scores, key, preferred_element_type=jnp.float32) * scale
        )
        grad_key_sum = (
            grad_key_sum
            + jnp.einsum(
                "hbl,bhd->lhd", grad_scores, query_block, preferred_element_type=jnp.float32
            )
            * scale
        )
        grad_value_sum = grad_value_sum + jnp.einsum(
            "hbl,bhd->lhd", shares, grad_block, preferred_element_type=jnp.float32
        )
        return ((grad_key_sum, grad_value_sum), grad_query_block)

    zero_heads = jnp.zeros((length, local_heads, head_dim), jnp.float32)
    (grad_key_rot, grad_value_sum), grad_query_blocks = lax.scan(
        backward_block, (zero_heads, zero_heads), (jnp.arange(count), logsum)
    )
    grad_query_rot = grad_query_blocks.reshape(length, local_heads, head_dim)
    grad_value = grad_value_sum.reshape(length, local_width).astype(jnp.bfloat16)
    grad_query_norm = rotate_back(grad_query_rot, cosine, sine).reshape(length, local_width)
    grad_key_norm = rotate_back(grad_key_rot, cosine, sine).reshape(length, local_width)
    query_gain_part = jnp.sum(grad_query_norm * query_unit, axis=0)
    key_gain_part = jnp.sum(grad_key_norm * key_unit, axis=0)
    inner_query = grad_query_norm * query_gain
    inner_key = grad_key_norm * key_gain
    products = lax.psum(
        (jnp.sum(inner_query * query_unit, axis=1), jnp.sum(inner_key * key_unit, axis=1)), "tensor"
    )
    grad_query = (query_scale * (inner_query - query_unit * (products[0] / width)[:, None])).astype(
        jnp.bfloat16
    )
    grad_key = (key_scale * (inner_key - key_unit * (products[1] / width)[:, None])).astype(
        jnp.bfloat16
    )
    query_grad = contract_rows(gathered, grad_query)
    key_grad = contract_rows(gathered, grad_key)
    value_grad = contract_rows(gathered, grad_value)
    input_grad = grad_middle + lax.psum_scatter(
        times_transposed(grad_query, query_weight)
        + times_transposed(grad_key, key_weight)
        + times_transposed(grad_value, value_weight),
        "tensor",
        scatter_dimension=0,
        tiled=True,
    )
    reduced = (
        lax.psum_scatter(query_grad, "dp", scatter_dimension=0, tiled=True),
        lax.psum_scatter(key_grad, "dp", scatter_dimension=0, tiled=True),
        lax.psum_scatter(value_grad, "dp", scatter_dimension=0, tiled=True),
        lax.psum_scatter(output_grad, "dp", scatter_dimension=1, tiled=True),
        lax.psum_scatter(gate_grad, "dp", scatter_dimension=0, tiled=True),
        lax.psum_scatter(up_grad, "dp", scatter_dimension=0, tiled=True),
        lax.psum_scatter(down_grad, "dp", scatter_dimension=1, tiled=True),
    )
    place = lax.axis_index("tensor") * local_width
    zero_width = jnp.zeros((width,), jnp.float32)
    query_gain_full = lax.dynamic_update_slice_in_dim(zero_width, query_gain_part, place, 0)
    key_gain_full = lax.dynamic_update_slice_in_dim(zero_width, key_gain_part, place, 0)
    gains = lax.psum(
        (query_gain_full, key_gain_full, attention_part, feedforward_part), ("dp", "tensor")
    )
    return (
        result,
        input_grad,
        reduced[0],
        reduced[1],
        reduced[2],
        reduced[3],
        reduced[4],
        reduced[5],
        reduced[6],
        gains[0],
        gains[1],
        gains[2],
        gains[3],
    )


def solution(mesh):
    in_specs = (
        P(("dp", "tensor"), None),
        P("dp", None),
        P(None, "tensor"),
        P(None, "tensor"),
        P(None, "tensor"),
        P("tensor", None),
        P(None, "tensor"),
        P(None, "tensor"),
        P("tensor", None),
        P("tensor"),
        P("tensor"),
        P(),
        P(),
        P(("dp", "tensor"), None),
    )
    out_specs = (
        P(("dp", "tensor"), None),
        P(("dp", "tensor"), None),
        P("dp", "tensor"),
        P("dp", "tensor"),
        P("dp", "tensor"),
        P("tensor", "dp"),
        P("dp", "tensor"),
        P("dp", "tensor"),
        P("tensor", "dp"),
        P(),
        P(),
        P(),
        P(),
    )
    return jax.shard_map(body, mesh=mesh, in_specs=in_specs, out_specs=out_specs, check_vma=False)
```

profile of v0, /device:TPU:0, one launch (start us, length us, event | category | flops | bytes accessed | tf_op | source)
XLA Modules:
  0.0 1458.1 jit_solution(6248746526958268343)
XLA Ops:
  14.0 44.2 %all-gather.5.cloned.1.call-done = bf16[1536,2048]{1,0:T(8,128)(2,1)} async-done(((bf16[192,2048]{1,0:T(8,128)(2,1)}), bf16[1536,2048]{1,0:T(8,128)(2,1)}) %all-gather.5.cloned.1.call-update) | async-done | bytes 6291472 | tf_op jit(solution)/shard_map/all_gather | solution.py:87
  58.2 5.5 convolution_convert_fusion.1
  65.2 4.9 multiply_reduce_fusion.8
  70.1 6.3 multiply_reduce_fusion.9
  76.4 23.9 %all-reduce.2 = (f32[1536]{0:T(1024)S(1)}, f32[1536]{0:T(1024)S(1)}) all-reduce(f32[1536]{0:T(1024)S(1)} %get-tuple-element.318, f32[1536]{0:T(1024)S(1)} %get-tuple-element.320), channel_id=1, replica_groups=mesh['dp'=4,'tensor'=8] {'tensor'}, use_global_device_ids=true, to_apply=%region_1.0 | all-reduce | flops 3072 | bytes 24576 | tf_op jit(solution)/shard_map/psum | solution.py:91
  103.7 3.3 multiply_multiply_fusion.1
  107.0 3.0 copy.42
  116.6 27.2 %while.27 = (s32[]{:T(128)}, bf16[3,512,2,128]{3,2,1,0:T(2,128)(2,1)}, f32[3,2,512]{2,1,0:T(2,128)S(1)}, s32[3]{0:T(128)S(1)}, s32[1,1536]{1,0:T(1,128)S(1)}, /*...) while((s32[]{:T(128)}, ...), condition=%wide.region_7.8_spmd, body=%wide.region_4.7_spmd.sunk | while | flops 826670592 | bytes 24703192 | solution.py:119
  143.8 8.4 fusion.48
  152.2 92.5 %reduce-scatter.12.cloned.1.call-done = f32[192,2048]{1,0:T(8,128)} async-done(((f32[1536,2048]{1,0:T(8,128)}), f32[192,2048]{1,0:T(8,128)}) %reduce-scatter.12.cloned.1.call-update) | async-done | bytes 1572880 | tf_op jit(solution)/shard_map/reduce_scatter | solution.py:122
  249.6 45.1 %all-gather.7.cloned.1.call-done = bf16[1536,2048]{1,0:T(8,128)(2,1)} async-done(((bf16[192,2048]{1,0:T(8,128)(2,1)}), bf16[1536,2048]{1,0:T(8,128)(2,1)}) %all-gather.7.cloned.1.call-update) | async-done | bytes 6291472 | tf_op jit(solution)/shard_map/all_gather | solution.py:131
  294.7 10.1 fusion.57
  304.8 9.0 multiply_convert_fusion.3
  315.5 9.1 fusion.58
  324.7 92.5 %reduce-scatter.14.cloned.1.call-done = f32[192,2048]{1,0:T(8,128)} async-done(((f32[1536,2048]{1,0:T(8,128)}), f32[192,2048]{1,0:T(8,128)}) %reduce-scatter.14.cloned.1.call-update) | async-done | bytes 1572880 | tf_op jit(solution)/shard_map/reduce_scatter | solution.py:138
  423.0 45.4 %all-gather.9.cloned.1.call-done = bf16[1536,2048]{1,0:T(8,128)(2,1)} async-done(((bf16[192,2048]{1,0:T(8,128)(2,1)}), bf16[1536,2048]{1,0:T(8,128)(2,1)}) %all-gather.9.cloned.1.call-update) | async-done | bytes 6291472 | tf_op jit(solution)/shard_map/all_gather | solution.py:150
  468.4 17.2 %multiply_convert_fusion.1 = (bf16[1536,1024]{1,0:T(8,128)(2,1)}, bf16[1536,1024]{1,0:T(8,128)(2,1)}) fusion(f32[1536,1024]{1,0:T(8,128)} %copy-done.54, f32[1536,1024]{1,0:T(8,128)} %get-tuple-element.323, bf16[1536,2048]{1,0:T(8,128)(2,1)} %all-gather.9.cloned.1.call-done, bf16[1024,2048]{1,0:T(8,128)(2,1)} %param.26), kind=kOutput, calls=%fused_computation.46 | convolution fusion | flops 6462898176 | bytes 29360128 | tf_op jit(solution)/shard_map/dot_general | solution.py:20
  485.6 11.7 fusion.59
  497.3 13.4 convolution_add_fusion
  510.8 92.5 %reduce-scatter.16.cloned.1.call-done = f32[192,2048]{1,0:T(8,128)} async-done(((f32[1536,2048]{1,0:T(8,128)}), f32[192,2048]{1,0:T(8,128)}) %reduce-scatter.16.cloned.1.call-update) | async-done | bytes 1572880 | tf_op jit(solution)/shard_map/reduce_scatter | solution.py:157
  603.3 2.9 multiply_reduce_fusion.1
  606.2 3.2 multiply_convert_fusion.6
  612.0 43.1 %all-gather.11.cloned.1.call-done = bf16[1536,2048]{1,0:T(8,128)(2,1)} async-done(((bf16[192,2048]{1,0:T(8,128)(2,1)}), bf16[1536,2048]{1,0:T(8,128)(2,1)}) %all-gather.11.cloned.1.call-update) | async-done | bytes 6291472 | tf_op jit(solution)/shard_map/all_gather | solution.py:165
  655.1 5.7 convolution_convert_fusion
  660.9 45.8 %while.28 = (s32[]{:T(128)}, f32[1536,2,128]{0,2,1:T(8,128)}, f32[1536,2,128]{0,2,1:T(8,128)S(1)}, f32[3,512,2,128]{3,1,2,0:T(8,128)}, s32[3]{0:T(128)S(1)}, /*i...) while((s32[]{:T(128)}, f32[1536,2,128]{0,2,1:T(8,128)}, ...), condition=%wide.region_17.18_spmd.clone, body=%wide.region_15.17_spmd.clone.sunk | while | flops 2031877632 | bytes 87343480 | solution.py:202
  665.4 3.1 multiply_reduce_fusion.11
  680.6 3.1 multiply_reduce_fusion.11
  695.9 3.1 multiply_reduce_fusion.11
  709.3 2.9 copy.65
  712.2 3.0 copy.57
  718.9 6.0 convolution_bitcast_fusion
  732.0 3.1 copy.59
  737.8 4.1 multiply_reduce_fusion.2
  742.4 25.2 %all-reduce.1 = (f32[1536]{0:T(1024)S(1)}, f32[1536]{0:T(1024)S(1)}) all-reduce(f32[1536]{0:T(1024)S(1)} %get-tuple-element.242, f32[1536]{0:T(1024)S(1)} %get-tuple-element.240), channel_id=1, replica_groups=mesh['dp'=4,'tensor'=8] {'tensor'}, use_global_device_ids=true, to_apply=%region_19.20 | all-reduce | flops 3072 | bytes 24576 | tf_op jit(solution)/shard_map/psum | solution.py:213
  769.8 5.9 convolution_bitcast_fusion.2
  778.5 6.0 convolution_bitcast_fusion.1
  786.7 6.4 fusion.61
  793.0 11.4 add_add_fusion
  804.5 11.9 fusion.64
  816.5 11.8 fusion.63
  828.6 11.9 fusion.62
  841.6 5.9 fusion.46
  848.3 39.1 %all-reduce = (f32[2048]{0:T(1024)}, f32[2048]{0:T(1024)}, f32[2048]{0:T(1024)}, f32[2048]{0:T(1024)}) all-reduce(f32[2048]{0:T(1024)S(1)} %dynamic_update_slice.18, f32[2048]{0:T(1024)S(1)} %dynamic_update_slice.19, f32[2048]{0:T(1024)S(1)} %copy-done.43, f32[2048]{0:T(1024)S(1)} %copy-done.42), channel_id=1, replica_groups=mesh['dp'=4,'tensor'=8] {'dp','tensor'}, use_global_device_ids=true, to_apply=%region_31.32 | all-reduce | flops 8192 | bytes 65536 | tf_op jit(solution)/shard_map/psum | solution.py:246
  893.7 66.4 %reduce-scatter.18.cloned.1.call-done = f32[192,2048]{1,0:T(8,128)} async-done(((f32[1536,2048]{1,0:T(8,128)}), f32[192,2048]{1,0:T(8,128)}) %reduce-scatter.18.cloned.1.call-update) | async-done | bytes 1572880 | tf_op jit(solution)/shard_map/reduce_scatter | solution.py:225
  962.9 144.5 %reduce-scatter.32.cloned.1.call-done = f32[1024,512]{1,0:T(8,128)} async-done(((f32[1024,2048]{1,0:T(8,128)}), f32[1024,512]{1,0:T(8,128)}) %reduce-scatter.32.cloned.1.call-update) | async-done | bytes 2097168 | tf_op jit(solution)/shard_map/reduce_scatter | solution.py:240
  1107.5 148.3 %reduce-scatter.30.cloned.1.call-done = f32[512,1024]{1,0:T(8,128)} async-done(((f32[2048,1024]{1,0:T(8,128)}), f32[512,1024]{1,0:T(8,128)}) %reduce-scatter.30.cloned.1.call-update) | async-done | bytes 2097168 | tf_op jit(solution)/shard_map/reduce_scatter | solution.py:239
  1255.7 148.1 %reduce-scatter.28.cloned.1.call-done = f32[512,1024]{1,0:T(8,128)} async-done(((f32[2048,1024]{1,0:T(8,128)}), f32[512,1024]{1,0:T(8,128)}) %reduce-scatter.28.cloned.1.call-update) | async-done | bytes 2097168 | tf_op jit(solution)/shard_map/reduce_scatter | solution.py:238
  1403.9 47.4 %reduce-scatter.26.cloned.1.call-done = f32[256,512]{1,0:T(8,128)} async-done(((f32[256,2048]{1,0:T(8,128)}), f32[256,512]{1,0:T(8,128)}) %reduce-scatter.26.cloned.1.call-update) | async-done | bytes 524304 | tf_op jit(solution)/shard_map/reduce_scatter | solution.py:237
  (274 shorter events, 127.1 us)
Async XLA Ops:
  7.2 62.9 %copy-start = (bf16[2048,256]{1,0:T(8,128)(2,1)S(1)}, bf16[2048,256]{1,0:T(8,128)(2,1)}, u32[]{:S(2)}) copy-start(bf16[2048,256]{1,0:T(8,128)(2,1)} %param.20) | copy-start | bytes 3145732
  7.2 51.0 %all-gather.5.cloned.1.call-start = ((), (), s32[]{:S(2)}) async-start(), calls=%async_computation.11 | async-start | bytes 7077888 | tf_op jit(solution)/shard_map/all_gather | solution.py:87
  7.9 236.8 %reduce-scatter.12.cloned.1.call-start = ((), (), s32[]{:S(2)}) async-start(), calls=%async_computation.12 | async-start | bytes 14155776 | tf_op jit(solution)/shard_map/reduce_scatter | solution.py:122
  11.6 46.5 %copy-start.34 = (bf16[2048,256]{1,0:T(8,128)(2,1)S(1)}, bf16[2048,256]{1,0:T(8,128)(2,1)}, u32[]{:S(2)}) copy-start(bf16[2048,256]{1,0:T(8,128)(2,1)} %param.22) | copy-start | bytes 3145732
  70.1 30.3 %copy-start.19 = (f32[1536,256]{0,1:T(8,128)}, f32[1536,256]{0,1:T(8,128)S(1)}, u32[]{:S(2)}) copy-start(f32[1536,256]{0,1:T(8,128)S(1)} %get-tuple-element.321) | copy-start | bytes 4718596
  70.1 30.3 %copy-start.46 = (f32[256]{0:T(256)S(1)}, f32[256]{0:T(256)}, u32[]{:S(2)}) copy-start(f32[256]{0:T(256)} %param.28) | copy-start | bytes 3076
  100.4 3.3 copy-start.38
  103.6 8.8 copy-start.8
  143.8 8.4 copy-start.4
  143.8 8.4 copy-start.6
  152.2 94.3 %copy-start.40 = (f32[2048]{0:T(1024)S(1)}, f32[2048]{0:T(1024)}, u32[]{:S(2)}) copy-start(f32[2048]{0:T(1024)} %param.29) | copy-start | bytes 24580
  152.2 142.5 %all-gather.7.cloned.1.call-start = ((), (), s32[]{:S(2)}) async-start(), calls=%async_computation.13 | async-start | bytes 7077888 | tf_op jit(solution)/shard_map/all_gather | solution.py:131
  249.0 168.2 %reduce-scatter.14.cloned.1.call-start = ((), (), s32[]{:S(2)}) async-start(), calls=%async_computation.14 | async-start | bytes 14155776 | tf_op jit(solution)/shard_map/reduce_scatter | solution.py:138
  294.7 10.1 copy-start.48
  294.7 10.1 copy-start.51
  304.8 9.0 copy-start.54
  304.8 10.7 copy-start.49
  324.6 94.3 %copy-start.41 = (f32[2048]{0:T(1024)S(1)}, f32[2048]{0:T(1024)}, u32[]{:S(2)}) copy-start(f32[2048]{0:T(1024)} %param.30) | copy-start | bytes 24580
  324.6 143.8 %all-gather.9.cloned.1.call-start = ((), (), s32[]{:S(2)}) async-start(), calls=%async_computation.15 | async-start | bytes 7077888 | tf_op jit(solution)/shard_map/all_gather | solution.py:150
  418.9 2.6 copy-start.12
  422.8 180.5 %reduce-scatter.16.cloned.1.call-start = ((), (), s32[]{:S(2)}) async-start(), calls=%async_computation.16 | async-start | bytes 14155776 | tf_op jit(solution)/shard_map/reduce_scatter | solution.py:157
  468.4 17.2 %copy-start.50 = (bf16[2048,1024]{1,0:T(8,128)(2,1)S(1)}, bf16[2048,1024]{1,0:T(8,128)(2,1)}, u32[]{:S(2)}) copy-start(bf16[2048,1024]{1,0:T(8,128)(2,1)} %param.24) | copy-start | bytes 12582916
  485.6 11.7 copy-start.52
  510.7 144.4 %all-gather.11.cloned.1.call-start = ((), (), s32[]{:S(2)}) async-start(), calls=%async_computation.17 | async-start | bytes 7077888 | tf_op jit(solution)/shard_map/all_gather | solution.py:165
  603.3 3.0 copy-start.11
  603.3 3.0 copy-start.13
  603.3 3.0 copy-start.16
  609.5 277.9 %reduce-scatter.24.cloned.1.call-start = ((), (), s32[]{:S(2)}) async-start(), calls=%async_computation.21 | async-start | bytes 2621440 | tf_op jit(solution)/shard_map/reduce_scatter | solution.py:236
  670.9 2.4 copy-start.2
  686.1 2.4 copy-start.2
  701.4 2.4 copy-start.2
  715.3 3.6 copy-start.31
  718.9 6.5 copy-start.26
  725.0 164.6 %reduce-scatter.20.cloned.1.call-start = ((), (), s32[]{:S(2)}) async-start(), calls=%async_computation.19 | async-start | bytes 2621440 | tf_op jit(solution)/shard_map/reduce_scatter | solution.py:234
  732.0 3.2 copy-start.18
  737.8 4.1 copy-start.20
  737.8 4.1 copy-start.21
  737.8 4.1 copy-start.37
  737.8 4.1 copy-start.47
  775.8 115.8 %reduce-scatter.22.cloned.1.call-start = ((), (), s32[]{:S(2)}) async-start(), calls=%async_computation.20 | async-start | bytes 2621440 | tf_op jit(solution)/shard_map/reduce_scatter | solution.py:235
  784.5 175.5 %reduce-scatter.18.cloned.1.call-start = ((), (), s32[]{:S(2)}) async-start(), calls=%async_computation.18 | async-start | bytes 14155776 | tf_op jit(solution)/shard_map/reduce_scatter | solution.py:225
  786.7 6.4 copy-start.32
  804.4 303.0 %reduce-scatter.32.cloned.1.call-start = ((), (), s32[]{:S(2)}) async-start(), calls=%async_computation.25 | async-start | bytes 10485760 | tf_op jit(solution)/shard_map/reduce_scatter | solution.py:240
  816.4 439.3 %reduce-scatter.30.cloned.1.call-start = ((), (), s32[]{:S(2)}) async-start(), calls=%async_computation.24 | async-start | bytes 10485760 | tf_op jit(solution)/shard_map/reduce_scatter | solution.py:239
  828.3 575.5 %reduce-scatter.28.cloned.1.call-start = ((), (), s32[]{:S(2)}) async-start(), calls=%async_computation.23 | async-start | bytes 10485760 | tf_op jit(solution)/shard_map/reduce_scatter | solution.py:238
  840.5 610.8 %reduce-scatter.26.cloned.1.call-start = ((), (), s32[]{:S(2)}) async-start(), calls=%async_computation.22 | async-start | bytes 2621440 | tf_op jit(solution)/shard_map/reduce_scatter | solution.py:237
  887.4 72.7 %copy-start.14 = (bf16[192,2048]{1,0:T(8,128)(2,1)S(1)}, bf16[192,2048]{1,0:T(8,128)(2,1)}, u32[]{:S(2)}) copy-start(bf16[192,2048]{1,0:T(8,128)(2,1)} %param.31) | copy-start | bytes 2359300
  887.4 72.7 %copy-start.17 = (f32[192,2048]{1,0:T(8,128)S(1)}, f32[192,2048]{1,0:T(8,128)}, u32[]{:S(2)}) copy-start(f32[192,2048]{1,0:T(8,128)} %reduce-scatter.16.cloned.1.call-done) | copy-start | bytes 4718596
  (30 other events, 50.8 us)
Sparse Core Ops, SparseCore 0:
  9.9 48.2 all-gather.4
  152.3 92.4 reduce-scatter.11
  249.1 45.5 all-gather.6
  324.7 92.3 reduce-scatter.13
  422.9 45.5 all-gather.8
  510.8 92.3 reduce-scatter.15
  609.6 45.4 all-gather.10
  725.1 43.8 reduce-scatter.23
  775.9 43.0 reduce-scatter.19
  821.1 43.1 reduce-scatter.21
  868.3 91.7 reduce-scatter.17
  963.0 144.4 reduce-scatter.31
  1110.5 145.1 reduce-scatter.29
  1258.6 145.1 reduce-scatter.27
  1406.7 44.5 reduce-scatter.25
where the time goes:
time: 1470 us; the launch traced here: 1460 us
  waiting for transfers between devices  1010 us (69%)
  matrix products  223 us (15%)
  blocking collectives  88.2 us (6%)
  other arithmetic  66.8 us (5%)
  local copies, waits for them, and re-layouts  47.8 us (3%)
    reduce_scatter x1, waiting for transfers between devices, body(): lax.psum_scatter(up_grad, 'dp', scatter_dimension=0, tiled=True)  148 us
    reduce_scatter x1, waiting for transfers between devices, body(): lax.psum_scatter(gate_grad, 'dp', scatter_dimension=0, tiled=True)  148 us
    reduce_scatter x1, waiting for transfers between devices, body(): lax.psum_scatter(down_grad, 'dp', scatter_dimension=1, tiled=True)  145 us
    reduce_scatter x1, waiting for transfers between devices, body(): lax.psum_scatter(jnp.dot(part, output_weight, preferred_element_type=jnp....  92.5 us
    reduce_scatter x1, waiting for transfers between devices, body(): lax.psum_scatter(times_transposed(grad_gate, gate_weight) + times_transpo...  92.5 us
    reduce_scatter x1, waiting for transfers between devices, body(): lax.psum_scatter(jnp.dot(part, down_weight, preferred_element_type=jnp.fl...  92.5 us
    dot_general x7, matrix products, times_transposed(): lax.dot_general(left, right, (((1,), (1,)), ((), ())), preferred_element_...  67.6 us
    reduce_scatter x1, waiting for transfers between devices, body(): lax.psum_scatter(times_transposed(grad_query, query_weight) + times_trans...  66.4 us
  transfers between devices with their start and end apart: 15, of which 12 were waited for; matrix products, arithmetic and copies ran while one was open for 8% of the time, Pallas kernels for 0%

commit v1 on v0

v1 whole, which is shorter than its diff:
```python
import functools

import jax
import jax.numpy as jnp
from jax import lax
from jax.experimental import pallas as pl
from jax.experimental.pallas import tpu as pltpu
from jax.sharding import PartitionSpec as P

HEAD_DIM = 128
BF16 = jnp.bfloat16
F32 = jnp.float32

norm_eps = 1e-06
rope_base = 500000.0


def contract_rows(left, right):
    return lax.dot_general(left, right, (((0,), (0,)), ((), ())), preferred_element_type=F32)


def times_transposed(left, right):
    return lax.dot_general(left, right, (((1,), (1,)), ((), ())), preferred_element_type=F32)


def times(left, right):
    return jnp.dot(left, right, preferred_element_type=F32)


def rope_tables(length, head_dim):
    half = head_dim // 2
    freq = rope_base ** (-(2.0 * jnp.arange(half, dtype=F32)) / head_dim)
    angle = jnp.arange(length, dtype=F32)[:, None] * freq[None, :]
    cosine, sine = jnp.cos(angle), jnp.sin(angle)
    return (
        jnp.concatenate([cosine, cosine], axis=1),
        jnp.concatenate([-sine, sine], axis=1),
    )


def norm_back(grad, unit, inverse, gain):
    inner = grad * gain
    return inverse * (inner - unit * jnp.mean(inner * unit, axis=1, keepdims=True))


class PairedCores:
    def __init__(self):
        turn = lambda low, high: [(i, i ^ (low if i % 2 == 0 else high)) for i in range(8)]
        self.first, self.second, self.core = turn(2, 4), turn(4, 2), turn(1, 1)

    def send(self, value, way):
        return lax.ppermute(value, "tensor", way)

    def order(self):
        me = lax.axis_index("tensor")
        near = jnp.where(me % 2 == 0, 2, 4)
        far = 6 - near
        return jnp.stack([me ^ near, me ^ far, me, me ^ 6, me ^ 1 ^ far, me ^ 1 ^ near, me ^ 1, me ^ 7])

    def gather(self, own, meanwhile=None, early=None):
        first, second = self.send(own, self.first), self.send(own, self.second)
        other = self.send(own, self.core)
        if meanwhile is not None:
            second, meanwhile = lax.optimization_barrier((second, meanwhile))
        opposite = self.send(second, self.first)
        first_other, second_other = self.send(first, self.core), self.send(second, self.core)
        groups = [[own, other], [first, second, first_other, second_other]]
        made = None
        if early is not None:
            opposite, made = lax.optimization_barrier((opposite, early(*groups)))
        groups.append([opposite, self.send(opposite, self.core)])
        return groups, meanwhile, made

    def whole(self, groups):
        near, middle, last = groups
        if not isinstance(near, list):
            near, middle, last = jnp.split(near, 2), jnp.split(middle, 4), jnp.split(last, 2)
        first, second, first_other, second_other = middle
        return [first, second, near[0], last[0], first_other, second_other, near[1], last[1]]

    def groups(self, whole):
        first, second, own, opposite, first_other, second_other, other, opposite_other = jnp.split(whole, 8)
        groups = [[own, other], [first, second, first_other, second_other], [opposite, opposite_other]]
        return [jnp.concatenate(group, axis=0) for group in groups]

    def scatter(self, halves, product, meanwhile=None, late=None):
        mine, others = halves
        from_core = self.send(product(others).astype(BF16), self.core)
        total = product(mine) + from_core.astype(F32)
        first, second, own, opposite = jnp.split(total, 4)
        sent = opposite.astype(BF16), first.astype(BF16)
        passing, from_first = (self.send(part, self.first) for part in sent)
        if meanwhile is not None:
            passing, meanwhile = lax.optimization_barrier((passing, meanwhile(sent)))
        from_second = self.send((second + passing.astype(F32)).astype(BF16), self.second)
        if late is not None:
            from_second, late = lax.optimization_barrier((from_second, late(passing)))
        return own + from_first.astype(F32) + from_second.astype(F32), meanwhile, late

    def add(self, value):
        for bit in (1, 2, 4):
            value = value + self.send(value, [(i, i ^ bit) for i in range(8)])
        return value


class AnyDevices:
    def __init__(self, size):
        self.size = size

    def order(self):
        return jnp.arange(self.size)

    def gather(self, own, meanwhile=None, early=None):
        return [[lax.all_gather(own, "tensor", axis=0, tiled=True)]], meanwhile, []

    def groups(self, whole):
        return [whole]

    def whole(self, groups):
        return groups[0] if isinstance(groups[0], list) else groups

    def scatter(self, halves, product, meanwhile=None, late=None):
        part = product(jnp.concatenate(halves, axis=0)).astype(BF16)
        total = lax.psum_scatter(part, "tensor", scatter_dimension=0, tiled=True).astype(F32)
        return total, meanwhile, late

    def add(self, value):
        return lax.psum(value, "tensor")


def in_pairs(step):
    return [(i, i ^ step) for i in range(4)]


def scatter_rows(part, dimension):
    return lax.psum_scatter(part, "dp", scatter_dimension=dimension, tiled=True).astype(F32)


def from_neighbour(part):
    both = lax.all_gather(part, "dp", axis_index_groups=[[0, 1], [2, 3]])
    return lax.dynamic_index_in_dim(both, 1 - lax.axis_index("dp") % 2, 0, keepdims=False)


def piece_of(part, dimension, place):
    size = part.shape[dimension] // 4
    return lax.dynamic_slice_in_dim(part, place * size, size, dimension)


def add_rows(value, count):
    if count != 4:
        return lax.psum(value, "dp")
    one, two, three = (lax.ppermute(value, "dp", in_pairs(step)) for step in (1, 2, 3))
    return value + one, two, three


def turned(value):
    return pltpu.roll(value, HEAD_DIM // 2, 1)


def scale_of(sums, at, width):
    return lax.rsqrt(sums[:, at : at + 1] * (1.0 / width) + norm_eps)


def allowed_in(docs_col, docs_row, block, back):
    window = (back + 1) * block
    rows = lax.broadcasted_iota(jnp.int32, (block, window), 0)
    columns = lax.broadcasted_iota(jnp.int32, (block, window), 1)
    return (docs_col == docs_row) & (columns <= rows + back * block)


def places_of(b, block, back):
    start = pl.multiple_of(b * block, block)
    return pl.ds(start, block), pl.ds(start + back * block, block), pl.ds(start, (back + 1) * block)


def attend_kernel(
    shape, order, raw, sums, gains, cosine, sine, docs_col, docs_row, attended, query, key, value, logsum
):
    blocks, block, width, local, back, scale = shape
    heads = local // HEAD_DIM
    for ref in (key, value):
        ref[: back * block, :] = jnp.zeros((back * block, local), BF16)

    def step(b, carry):
        at = order[b]
        rows, later, window = places_of(b, block, back)
        total = sums[b]
        cos, sin = cosine[rows, :], sine[rows, :]
        for which in range(2):
            inverse = scale_of(total, which, width)
            for h in range(heads):
                lanes = slice(h * HEAD_DIM, (h + 1) * HEAD_DIM)
                own = slice(which * local + h * HEAD_DIM, which * local + (h + 1) * HEAD_DIM)
                v = raw[at, :, own] * inverse * gains[which : which + 1, lanes]
                v = (v * cos + turned(v) * sin).astype(BF16)
                if which == 0:
                    query[rows, lanes] = v
                else:
                    key[later, lanes] = v
        value[later, :] = raw[at, :, 2 * local :].astype(BF16)
        allowed = allowed_in(docs_col[rows, :], docs_row[b], block, back)
        for h in range(heads):
            lanes = slice(h * HEAD_DIM, (h + 1) * HEAD_DIM)
            scores = times_transposed(query[rows, lanes], key[window, lanes]) * scale
            scores = jnp.where(allowed, scores, -1e30)
            top = jnp.max(scores, axis=1, keepdims=True)
            weights = jnp.exp(scores - top)
            mass = jnp.sum(weights, axis=1, keepdims=True)
            shares = (weights * (1.0 / mass)).astype(BF16)
            attended[at, :, lanes] = times(shares, value[window, lanes]).astype(BF16)
            logsum[h, rows, :] = top + jnp.log(mass)
        return carry

    lax.fori_loop(0, blocks, step, 0)


def attend_back_kernel(
    shape,
    order,
    raw,
    sums,
    gains,
    cosine,
    sine,
    docs_col,
    docs_row,
    query,
    key,
    value,
    logsum,
    grad,
    inner,
    grad_value,
    products,
    gain_parts,
    grad_query_sum,
    grad_key_sum,
    grad_value_sum,
):
    blocks, block, width, local, back, scale = shape
    heads = local // HEAD_DIM
    grad_key_sum[...] = jnp.zeros(grad_key_sum.shape, F32)
    grad_value_sum[...] = jnp.zeros(grad_value_sum.shape, F32)
    gain_parts[...] = jnp.zeros(gain_parts.shape, F32)

    def step(b, carry):
        at = order[b]
        rows, later, window = places_of(b, block, back)
        allowed = allowed_in(docs_col[rows, :], docs_row[b], block, back)
        for h in range(heads):
            lanes = slice(h * HEAD_DIM, (h + 1) * HEAD_DIM)
            q, k, v, g = query[rows, lanes], key[window, lanes], value[window, lanes], grad[at, :, lanes]
            scores = times_transposed(q, k) * scale
            chances = jnp.exp(jnp.where(allowed, scores, -1e30) - logsum[h, rows, :])
            grad_shares = times_transposed(g, v)
            offset = jnp.sum(chances * grad_shares, axis=1, keepdims=True)
            grad_scores = (chances * (grad_shares - offset)).astype(BF16)
            grad_query_sum[rows, lanes] = times(grad_scores, k) * scale
            grad_key_sum[window, lanes] += contract_rows(grad_scores, q) * scale
            grad_value_sum[window, lanes] += contract_rows(chances.astype(BF16), g)
        return carry

    lax.fori_loop(0, blocks, step, 0)

    def finish(b, carry):
        at = order[b]
        rows, later, window = places_of(b, block, back)
        total = sums[b]
        cos, sin = cosine[rows, :], sine[rows, :]
        grad_value[at] = grad_value_sum[later, :].astype(BF16)
        for which in range(2):
            inverse = scale_of(total, which, width)
            dots = jnp.zeros((8, block), F32)
            ones = jnp.ones((8, HEAD_DIM), F32)
            for h in range(heads):
                lanes = slice(h * HEAD_DIM, (h + 1) * HEAD_DIM)
                own = slice(which * local + h * HEAD_DIM, which * local + (h + 1) * HEAD_DIM)
                unit = raw[at, :, own] * inverse
                g = grad_query_sum[rows, lanes] if which == 0 else grad_key_sum[later, lanes]
                g = g * cos + turned(g * sin)
                gain_parts[which : which + 1, lanes] += jnp.sum(g * unit, axis=0, keepdims=True)
                c = g * gains[which : which + 1, lanes]
                inner[at, :, own] = c
                dots = dots + lax.dot_general(
                    ones, c * unit, (((1,), (1,)), ((), ())), precision=lax.Precision.HIGHEST,
                    preferred_element_type=F32,
                )
            products[b, which : which + 1, :] = dots[:1]
        return carry

    lax.fori_loop(0, blocks, finish, 0)


def whole_specs(count):
    return [pl.BlockSpec(memory_space=pltpu.SMEM)] + [pl.BlockSpec(memory_space=pltpu.VMEM)] * count


def attend(shape, order, raw, sums, gains, cosine, sine, docs_col, docs_row):
    blocks, block, width, local, back, scale = shape
    heads, length = local // HEAD_DIM, blocks * block
    padded = length + back * block
    return pl.pallas_call(
        functools.partial(attend_kernel, shape),
        out_shape=(
            jax.ShapeDtypeStruct((blocks, block, local), BF16),
            jax.ShapeDtypeStruct((length, local), BF16),
            jax.ShapeDtypeStruct((padded, local), BF16),
            jax.ShapeDtypeStruct((padded, local), BF16),
            jax.ShapeDtypeStruct((heads, length, 1), F32),
        ),
        in_specs=whole_specs(7),
        out_specs=(pl.BlockSpec(memory_space=pltpu.VMEM),) * 5,
        compiler_params=pltpu.CompilerParams(vmem_limit_bytes=24 * 2**20),
        cost_estimate=pl.CostEstimate(flops=4 * 10**9, bytes_accessed=10**7, transcendentals=2 * 10**6),
    )(order, raw, sums, gains, cosine, sine, docs_col, docs_row)


def attend_back(shape, order, raw, sums, gains, cosine, sine, docs_col, docs_row, query, key, value, logsum, grad):
    blocks, block, width, local, back, scale = shape
    length = blocks * block
    padded = length + back * block
    return pl.pallas_call(
        functools.partial(attend_back_kernel, shape),
        out_shape=(
            jax.ShapeDtypeStruct((blocks, block, 2 * local), F32),
            jax.ShapeDtypeStruct((blocks, block, local), BF16),
            jax.ShapeDtypeStruct((blocks, 2, block), F32),
            jax.ShapeDtypeStruct((2, local), F32),
        ),
        in_specs=whole_specs(12),
        out_specs=(pl.BlockSpec(memory_space=pltpu.VMEM),) * 4,
        scratch_shapes=[
            pltpu.VMEM((length, local), F32),
            pltpu.VMEM((padded, local), F32),
            pltpu.VMEM((padded, local), F32),
        ],
        compiler_params=pltpu.CompilerParams(vmem_limit_bytes=36 * 2**20),
        cost_estimate=pl.CostEstimate(flops=8 * 10**9, bytes_accessed=2 * 10**7, transcendentals=2 * 10**6),
    )(order, raw, sums, gains, cosine, sine, docs_col, docs_row, query, key, value, logsum, grad)


TILE = 256


def gated_grad(grad_act, gate, up):
    sigma = jax.nn.sigmoid(gate)
    grad_gate = grad_act * up * sigma * (1.0 + gate * (1.0 - sigma))
    return grad_gate.astype(BF16), (grad_act * gate * sigma).astype(BF16)


def feed_back_kernel(count, *refs):
    grads, (weight, gate, up) = refs[:count], refs[count : count + 3]
    *_, mine, others, rows = refs
    block, tile = grads[0].shape[0], weight.shape[0]
    units, half = mine.shape[-1] // 2, rows.shape[0] // 2
    j = pl.program_id(0)

    @pl.when(j == 0)
    def _():
        for at, grad in enumerate(grads):
            rows[at * block : (at + 1) * block, :] = grad[...]

    grad_act = times_transposed(rows[...], weight[...])
    start = pl.multiple_of(j * tile, tile)
    for at, part in zip((start, start + units), gated_grad(grad_act, gate[...], up[...])):
        for out, own in ((mine, part[:half]), (others, part[half:])):
            out[:, :, pl.ds(at, tile)] = own.reshape(out.shape[:2] + (tile,))


def feed_back(grads, down_weight, both, slot, slots, before=()):
    count, width = len(grads), grads[0].shape[1]
    units, tile = down_weight.shape[0], min(TILE, down_weight.shape[0])
    tiles, rows = units // tile, sum(grad.shape[0] for grad in grads)
    in_specs = [pl.BlockSpec(grad.shape, lambda j: (0, 0)) for grad in grads] + [
        pl.BlockSpec((tile, width), lambda j: (j, 0)),
        pl.BlockSpec((rows, tile), lambda j: (0, j)),
        pl.BlockSpec((rows, tile), lambda j: (0, j + tiles)),
    ]
    in_specs += [pl.BlockSpec(memory_space=pl.ANY)] * len(before)
    args = [*grads, down_weight, both, both, *before]
    part = rows // (2 * slots)
    return pl.pallas_call(
        functools.partial(feed_back_kernel, count),
        grid=(tiles,),
        out_shape=(jax.ShapeDtypeStruct((4, part, 2 * units), BF16),) * 2,
        in_specs=in_specs,
        out_specs=(pl.BlockSpec((slots, part, 2 * units), lambda j: (slot // slots, 0, 0)),) * 2,
        scratch_shapes=[pltpu.VMEM((rows, width), BF16)],
        input_output_aliases={count + 3 + at: at for at in range(len(before))},
        compiler_params=pltpu.CompilerParams(vmem_limit_bytes=(8 + 7 * rows // 192) * 2**20),
        cost_estimate=pl.CostEstimate(
            flops=2 * rows * width * units,
            bytes_accessed=2 * units * width + 12 * rows * units + 2 * rows * width,
            transcendentals=rows * units,
        ),
    )(*args)


def pieces_kernel(plan, count, place, *refs):
    sources, outs, sems = refs[:count], refs[count:-1], refs[-1]
    copies = []
    for out, parts in zip(outs, plan):
        size = out.shape[1]
        columns = pl.ds(pl.multiple_of(place[0] * size, size), size)
        at = 0
        for source, start, rows in parts:
            copies.append(
                pltpu.make_async_copy(
                    sources[source].at[pl.ds(start, rows), columns],
                    out.at[pl.ds(at, rows), :],
                    sems.at[len(copies)],
                )
            )
            at += rows
    for copy in copies:
        copy.start()
    for copy in copies:
        copy.wait()


def pieces_of(sources, plan, place, count=4):
    size = sources[0].shape[1] // count
    shapes = [(sum(rows for _, _, rows in parts), size) for parts in plan]
    return pl.pallas_call(
        functools.partial(pieces_kernel, plan, len(sources)),
        out_shape=[jax.ShapeDtypeStruct(shape, BF16) for shape in shapes],
        in_specs=[pl.BlockSpec(memory_space=pltpu.SMEM)] + [pl.BlockSpec(memory_space=pltpu.HBM)] * len(sources),
        out_specs=[pl.BlockSpec(memory_space=pltpu.HBM)] * len(plan),
        scratch_shapes=[pltpu.SemaphoreType.DMA((sum(len(parts) for parts in plan),))],
        compiler_params=pltpu.CompilerParams(vmem_limit_bytes=2**20),
        cost_estimate=pl.CostEstimate(
            flops=0, bytes_accessed=sum(4 * rows * columns for rows, columns in shapes), transcendentals=0
        ),
    )(jnp.reshape(place, (1,)).astype(jnp.int32), *sources)


def joined_rows(blocks):
    return pieces_of(blocks, [[(at, 0, block.shape[0]) for at, block in enumerate(blocks)]], 0, 1)[0]


def body(
    sizes,
    hidden_in,
    doc_ids,
    query_weight,
    key_weight,
    value_weight,
    output_weight,
    gate_weight,
    up_weight,
    down_weight,
    query_gain,
    key_gain,
    attention_gain,
    feedforward_gain,
    out_grad,
):
    tensor, rows = sizes["tensor"], sizes["dp"]
    moves = PairedCores() if tensor == 8 else AnyDevices(tensor)
    width = hidden_in.shape[1]
    local = query_weight.shape[1]
    hidden_units = gate_weight.shape[1]
    documents = doc_ids[0]
    length = documents.shape[0]
    block = length // tensor
    most = length // 4
    back = -(-(most - 1) // block)
    shape = (tensor, block, width, local, back, HEAD_DIM ** (-0.5))

    places = moves.order()
    steps = jnp.arange(tensor, dtype=jnp.int32)
    meets = places[None, :] == steps[:, None]
    order = jnp.sum(jnp.where(meets, steps[None, :], 0), axis=1)

    def in_row(value):
        parts = value.reshape(2, 1, tensor, block)
        return jnp.sum(jnp.where(meets[None, :, :, None], parts, 0.0), axis=2).reshape(2, length)

    def as_arrived(value):
        parts = value.reshape(2, tensor, 1, block)
        return jnp.sum(jnp.where(meets[None, :, :, None], parts, 0.0), axis=1).reshape(2, length)

    cosine, sine = rope_tables(length, HEAD_DIM)
    docs_col = documents[:, None]
    padded = jnp.concatenate([jnp.full((back * block,), -1, jnp.int32), documents])
    docs_row = jnp.stack([padded[b * block : (b + back + 1) * block] for b in range(tensor)])[:, None, :]
    gains = jnp.stack([query_gain, key_gain])

    def row_of(groups):
        return jnp.concatenate(moves.whole(groups), axis=0)

    def joined(group):
        return jnp.concatenate(group, axis=0)

    weight_qkv = jnp.concatenate([query_weight, key_weight, value_weight], axis=1)
    weight_gate_up = jnp.concatenate([gate_weight, up_weight], axis=1)
    paired = rows == 4 and tensor == 8

    def halves_of(whole):
        return jnp.split(whole, 2)

    def raw_of(*groups):
        return [times(joined(group), weight_qkv) for group in groups]

    hidden_groups, _, raw = moves.gather(hidden_in, early=raw_of)
    raw = row_of(raw + raw_of(hidden_groups[-1]))
    squares = jnp.stack(
        [
            jnp.sum(jnp.square(raw[:, :local]), axis=1),
            jnp.sum(jnp.square(raw[:, local : 2 * local]), axis=1),
        ]
    )
    sums = moves.add(in_row(squares))
    raw_blocks = raw.reshape(tensor, block, 3 * local)
    tables = (order, raw_blocks, sums.T.reshape(tensor, block, 2), gains, cosine, sine, docs_col, docs_row)
    attended_blocks, query, key, value, logsum = attend(shape, *tables)
    attended = attended_blocks.reshape(length, local)
    attn_proj, _, _ = moves.scatter(halves_of(attended), lambda part: times(part, output_weight))
    attn_scale = lax.rsqrt(jnp.mean(attn_proj * attn_proj, axis=1, keepdims=True) + norm_eps)
    attn_unit = attn_proj * attn_scale
    middle = hidden_in.astype(F32) + attn_unit * attention_gain
    middle_low = middle.astype(BF16)

    def activate(both):
        gate, up = both[:, :hidden_units], both[:, hidden_units:]
        return (gate * jax.nn.sigmoid(gate) * up).astype(BF16)

    def both_of(*groups):
        both = [times(joined(group), weight_gate_up) for group in groups]
        return both, [activate(part) for part in both]

    def to_pair(value):
        return lax.ppermute(value, "dp", in_pairs(2))

    hidden_all = joined_rows(moves.whole(hidden_groups)) if tensor == 8 else hidden_groups[0][0]
    middle_groups, hidden_all, made = moves.gather(middle_low, hidden_all, both_of)
    if paired:
        middle_groups[-1], pair_middle = lax.optimization_barrier((middle_groups[-1], to_pair(middle_low)))
        pair_middle_all = lax.all_gather(pair_middle, "tensor", axis=0, tiled=True)
    both_groups, activated = (early + late for early, late in zip(made or ([], []), both_of(middle_groups[-1])))
    activated = row_of(activated)
    mlp_proj, _, _ = moves.scatter(halves_of(activated), lambda part: times(part, down_weight))
    mlp_scale = lax.rsqrt(jnp.mean(mlp_proj * mlp_proj, axis=1, keepdims=True) + norm_eps)
    mlp_unit = mlp_proj * mlp_scale
    result = middle + mlp_unit * feedforward_gain

    grad_out = out_grad.astype(F32)
    grad_mlp = norm_back(grad_out, mlp_unit, mlp_scale, feedforward_gain).astype(BF16)
    feedforward_part = jnp.sum(grad_out * mlp_unit, axis=0)
    pair_both = None
    if paired:
        pair_middle_all, grad_mlp = lax.optimization_barrier((pair_middle_all, grad_mlp))
        pair_both = times(pair_middle_all, weight_gate_up)

    def back_early(near, beside):
        part = feed_back(near, down_weight, both_groups[0], 2, 1)
        part = feed_back(beside, down_weight, both_groups[1], 0, 2, part)
        return part, to_pair(grad_mlp) if paired else None

    grad_mlp_groups, pair_both, made = moves.gather(grad_mlp, pair_both, back_early)
    if tensor == 8:
        made, pair_grad_mlp = made
        grad_gate_up = feed_back(grad_mlp_groups[-1], down_weight, both_groups[2], 3, 1, made)
        grad_gate_up = [half.reshape(length // 2, 2 * hidden_units) for half in grad_gate_up]
    else:
        grad_act = times_transposed(grad_mlp_groups[0][0], down_weight)
        both = both_groups[0]
        grad_gate_up = gated_grad(grad_act, both[:, :hidden_units], both[:, hidden_units:])
        grad_gate_up = halves_of(jnp.concatenate(grad_gate_up, axis=1))
    if paired:
        grad_gate_up, pair_activated = lax.optimization_barrier((grad_gate_up, activate(pair_both)))
        pair_grad_mlp_all = lax.all_gather(pair_grad_mlp, "tensor", axis=0, tiled=True)

    me = lax.axis_index("dp")
    half_rows = length // 2

    def own_weight_pieces(place):
        blocks = moves.whole(middle_groups) + moves.whole(grad_mlp_groups)
        part = [(at, 0, block) for at in range(16)]
        mine, others, grads = pieces_of(blocks, [part[:4], part[4:8], part[8:]], place)
        return [
            contract_rows(activated, grads),
            contract_rows(mine, grad_gate_up[0]) + contract_rows(others, grad_gate_up[1]),
        ]

    def pair_weight_pieces(place):
        plan = [[(0, 0, half_rows)], [(0, half_rows, half_rows)], [(1, 0, length)]]
        first, second, grads = pieces_of([pair_middle_all, pair_grad_mlp_all], plan, place)
        return [
            contract_rows(pair_activated, grads),
            contract_rows(first, pair_gate_up[0]) + contract_rows(second, pair_gate_up[1]),
        ]

    def own_away(sent):
        nonlocal grad_mlp_groups, middle_groups
        grad_mlp_groups, middle_groups, _ = lax.optimization_barrier((grad_mlp_groups, middle_groups, sent))
        return own_weight_pieces(me ^ 1)

    def pair_back(passing):
        grads, _ = lax.optimization_barrier((pair_grad_mlp_all, passing))
        pair_gate_up = feed_back([grads], down_weight, pair_both, 0, 4)
        return [half.reshape(half_rows, 2 * hidden_units) for half in pair_gate_up]

    back_part, away, pair_gate_up = moves.scatter(
        grad_gate_up,
        lambda part: times_transposed(part, weight_gate_up),
        own_away if paired else None,
        pair_back if paired else None,
    )
    grad_middle = grad_out + back_part

    grad_proj = norm_back(grad_middle, attn_unit, attn_scale, attention_gain).astype(BF16)
    attention_part = jnp.sum(grad_middle * attn_unit, axis=0)
    if paired:
        pair_gate_up, grad_proj = lax.optimization_barrier((pair_gate_up, grad_proj))
        away = [(own + pair).astype(BF16) for own, pair in zip(away, pair_weight_pieces(me ^ 1))]

    def attended_early(*groups):
        return [times_transposed(joined(group), output_weight).astype(BF16) for group in groups]

    grad_proj_groups, away, made = moves.gather(grad_proj, away, attended_early)
    if paired:
        got = [from_neighbour(part) for part in away]
    else:
        down_grad = scatter_rows(contract_rows(activated, row_of(grad_mlp_groups)).astype(BF16), 1)
        back = contract_rows(row_of(middle_groups), jnp.concatenate(grad_gate_up, axis=0))
        gate_up_grad = scatter_rows(back.astype(BF16), 0)
    grad_attended = row_of(made + attended_early(grad_proj_groups[-1]))
    output_part = sum(
        contract_rows(left, joined(right)) for left, right in zip(moves.groups(attended), grad_proj_groups)
    ).astype(BF16)
    output_grad = scatter_rows(output_part, 1)
    inner, grad_value, products, gain_parts = attend_back(
        shape, *tables, query, key, value, logsum, grad_attended.reshape(tensor, block, local)
    )
    place = lax.axis_index("tensor") * local
    spread = lax.dynamic_update_slice(jnp.zeros((2, width), F32), gain_parts, (0, place))
    spread = jnp.concatenate([spread, attention_part[None], feedforward_part[None]], axis=0)
    products = products.transpose(1, 0, 2).reshape(-1)
    packed = moves.add(jnp.concatenate([products, spread.reshape(-1)]).reshape(-1, 256)).reshape(-1)
    products = as_arrived(packed[: 2 * length].reshape(2, length)).T * (1.0 / width)
    gain_sums = add_rows(packed[2 * length :], rows)
    inner = inner.reshape(length, 2 * local)
    grad_qkv = [None, None, grad_value.reshape(length, local)]
    flat = as_arrived(sums).T
    for which in range(2):
        own = slice(which * local, (which + 1) * local)
        inverse = lax.rsqrt(flat[:, which : which + 1] * (1.0 / width) + norm_eps)
        unit = raw[:, own] * inverse
        grad_qkv[which] = (inverse * (inner[:, own] - unit * products[:, which : which + 1])).astype(BF16)
    grad_qkv = jnp.concatenate(grad_qkv, axis=1)
    qkv_part = contract_rows(hidden_all, grad_qkv).astype(BF16)
    grad_qkv, qkv_part = lax.optimization_barrier((grad_qkv, qkv_part))
    qkv_grad = scatter_rows(qkv_part, 0)

    def here(sent):
        nonlocal grad_mlp_groups, middle_groups, pair_grad_mlp_all, pair_middle_all, gain_sums
        grad_mlp_groups, middle_groups, pair_grad_mlp_all, pair_middle_all, gain_sums, _ = lax.optimization_barrier(
            (grad_mlp_groups, middle_groups, pair_grad_mlp_all, pair_middle_all, gain_sums, sent)
        )
        return [own + pair for own, pair in zip(own_weight_pieces(me), pair_weight_pieces(me))]

    input_part, kept, _ = moves.scatter(
        halves_of(grad_qkv), lambda part: times_transposed(part, weight_qkv), here if paired else None
    )
    input_grad = grad_middle + input_part
    if paired:
        got, output_grad, qkv_grad, input_grad = lax.optimization_barrier((got, output_grad, qkv_grad, input_grad))
        down_grad = kept[0] + got[0].astype(F32)
        gate_up_grad = kept[1] + got[1].astype(F32)
        near, two, three = gain_sums
        gain_sums = near + (two + three)
    gate_grad, up_grad = gate_up_grad[:, :hidden_units], gate_up_grad[:, hidden_units:]
    summed = gain_sums.reshape(4, width)
    return (
        result,
        input_grad,
        qkv_grad[:, :local],
        qkv_grad[:, local : 2 * local],
        qkv_grad[:, 2 * local :],
        output_grad,
        gate_grad,
        up_grad,
        down_grad,
        summed[0],
        summed[1],
        summed[2],
        summed[3],
    )


def solution(mesh):
    in_specs = (
        P(("dp", "tensor"), None),
        P("dp", None),
        P(None, "tensor"),
        P(None, "tensor"),
        P(None, "tensor"),
        P("tensor", None),
        P(None, "tensor"),
        P(None, "tensor"),
        P("tensor", None),
        P("tensor"),
        P("tensor"),
        P(),
        P(),
        P(("dp", "tensor"), None),
    )
    out_specs = (
        P(("dp", "tensor"), None),
        P(("dp", "tensor"), None),
        P("dp", "tensor"),
        P("dp", "tensor"),
        P("dp", "tensor"),
        P("tensor", "dp"),
        P("dp", "tensor"),
        P("dp", "tensor"),
        P("tensor", "dp"),
        P(),
        P(),
        P(),
        P(),
    )
    sizes = {axis: mesh.shape[axis] for axis in ("dp", "tensor")}
    return jax.shard_map(
        functools.partial(body, sizes), mesh=mesh, in_specs=in_specs, out_specs=out_specs, check_vma=False
    )
```

time: 1470 us -> 624 us (0.42)
  waiting for transfers between devices: 1010 us -> 198 us
  blocking collectives: 88.2 us -> 0 us
  matrix products: 223 us -> 140 us
  Pallas kernels: 0 us -> 72.9 us
  starting transfers between devices: 2.32 us -> 52.3 us
  local copies, waits for them, and re-layouts: 47.8 us -> 85.9 us
  other arithmetic: 66.8 us -> 49.5 us
    reduce_scatter x11 -> x2, waiting for transfers between devices: 832 us -> 44.9 us  [scatter_rows(): lax.psum_scatter(part, 'dp', scatter_dimension=dimension, tiled=True)]
    all_gather x4, waiting for transfers between devices: 178 us -> 0.01 us  [the longest x2 0.01 us: from_neighbour(): both = lax.all_gather(part, 'dp', axis_index_groups=[[0, 1], [2, 3]])]
    ppermute x0 -> x55, waiting for transfers between devices: none -> 153 us  [the longest x50 121 us: send(): return lax.ppermute(value, 'tensor', way)]
    psum x3 -> x0, blocking collectives: 88.2 us -> none  [the longest x1 39.1 us: body(): lax.psum((query_gain_full, key_gain_full, attention_part, feedforward_par...]
    pallas_call x0 -> x11, Pallas kernels: none -> 72.9 us  [the longest x4 32.8 us: feed_back(): pl.pallas_call(functools.partial(feed_back_kernel, count), grid=(tiles,),...]
    ppermute x0 -> x55, starting transfers between devices: none -> 52 us  [the longest x50 44.5 us: send(): return lax.ppermute(value, 'tensor', way)]
    unnamed x107 -> x350, local copies, waits for them, and re-layouts: 19.1 us -> 64.3 us
    dot_general x28 -> x11, matrix products: 95.8 us -> 56.2 us  [times(): return jnp.dot(left, right, preferred_element_type=F32)]
  transfers between devices with their start and end apart: 15 -> 61, of which waited for: 12 -> 27; matrix products, arithmetic and copies ran while one was open for 8% -> 33% of each run, Pallas kernels for 0% -> 10%
where the time goes in v1:
time: 624 us; the launch traced here: 616 us
  waiting for transfers between devices  198 us (32%)
  matrix products  140 us (22%)
  local copies, waits for them, and re-layouts  85.9 us (14%)
  Pallas kernels  72.9 us (12%)
  starting transfers between devices  52.3 us (8%)
  other arithmetic  49.5 us (8%)
  between operations  16.7 us (3%)
    ppermute x50, waiting for transfers between devices, send(): return lax.ppermute(value, 'tensor', way)  121 us
    unnamed x350, local copies, waits for them, and re-layouts  64.3 us
    dot_general x11, matrix products, times(): return jnp.dot(left, right, preferred_element_type=F32)  56.2 us
    dot_general x16, matrix products, contract_rows(): lax.dot_general(left, right, (((0,), (0,)), ((), ())), preferred_element_...  45.8 us
    reduce_scatter x2, waiting for transfers between devices, scatter_rows(): lax.psum_scatter(part, 'dp', scatter_dimension=dimension, tiled=True)  44.9 us
    ppermute x50, starting transfers between devices, send(): return lax.ppermute(value, 'tensor', way)  44.5 us
    dot_general x7, matrix products, times_transposed(): lax.dot_general(left, right, (((1,), (1,)), ((), ())), preferred_element_...  38 us
    pallas_call x4, Pallas kernels, feed_back(): pl.pallas_call(functools.partial(feed_back_kernel, count), grid=(tiles,),...  32.8 us
  transfers between devices with their start and end apart: 61, of which 27 were waited for; matrix products, arithmetic and copies ran while one was open for 33% of the time, Pallas kernels for 10%

profile of v1, /device:TPU:0, one launch (start us, length us, event | category | flops | bytes accessed | tf_op | source)
XLA Modules:
  0.0 615.5 jit_solution(16406864202607439998)
XLA Ops:
  7.2 3.0 collective-permute-start
  11.8 3.9 fusion.85
  17.1 11.3 %collective-permute-done.refs_1_ = bf16[192,2048]{1,0:T(8,128)(2,1)S(1)} collective-permute-done((bf16[192,2048]{1,0:T(8,128)(2,1)}, bf16[192,2048]{1,0:T(8,128)(2,1)S(1)}, u32[]{:S(2)}, u32[]{:S(2)}) %collective-permute-start) | collective-permute-done | bytes 786464 | tf_op jit(solution)/shard_map/ppermute | solution.py:52
  30.8 3.6 pad_maximum_fusion.1
  38.5 5.4 fusion.1
  49.3 2.9 fusion.44
  74.0 11.7 %shard_map.237 = (bf16[8,192,256]{2,1,0:T(8,128)(2,1)S(1)}, bf16[1536,256]{1,0:T(8,128)(2,1)S(1)}, bf16[1920,256]{1,0:T(8,128)(2,1)S(1)}, bf16[1920,256]{1,0:T(8,128)(2,1)S(1)}, f32[2,1536,1]{2,1,0:T(8,128)S(1)}) custom-call(s32[8]{0:T(128)S(1)} %select_reduce_fusion.3.order, f32[8,192,768]{2,1,0:T(8,128)S(1)} %bitcast.126, f32[8,192,2]{2,1,0:T(8,128)S(1)} %bitcast.131, ...), custom_call_target="tpu_custom_call" | custom-call | flops 4000000000 | bytes 10000000 | tf_op jit(solution)/shard_map/pallas_call | solution.py:302
  88.1 5.7 collective-permute-done.10
  97.0 10.0 %collective-permute-done.12 = bf16[192,2048]{1,0:T(8,128)(2,1)S(1)} collective-permute-done((bf16[192,2048]{1,0:T(8,128)(2,1)S(1)}, bf16[192,2048]{1,0:T(8,128)(2,1)S(1)}, u32[]{:S(2)}, u32[]{:S(2)}) %collective-permute-start.12) | collective-permute-done | bytes 786464 | tf_op jit(solution)/shard_map/ppermute | solution.py:52
  109.3 12.0 %collective-permute-done.11 = bf16[192,2048]{1,0:T(8,128)(2,1)S(1)} collective-permute-done((bf16[192,2048]{1,0:T(8,128)(2,1)S(1)}, bf16[192,2048]{1,0:T(8,128)(2,1)S(1)}, u32[]{:S(2)}, u32[]{:S(2)}) %collective-permute-start.11) | collective-permute-done | bytes 786464 | tf_op jit(solution)/shard_map/ppermute | solution.py:52
  129.4 4.4 shard_map.238
  136.6 7.7 %collective-permute-done.14.refs_1_ = bf16[192,2048]{1,0:T(8,128)(2,1)S(1)} collective-permute-done((bf16[192,2048]{1,0:T(8,128)(2,1)S(1)}, bf16[192,2048]{1,0:T(8,128)(2,1)S(1)}, u32[]{:S(2)}, u32[]{:S(2)}) %collective-permute-start.14) | collective-permute-done | bytes 786464 | tf_op jit(solution)/shard_map/ppermute | solution.py:52
  147.1 3.5 fusion.48.refs_3_.refs_4_
  152.8 6.7 %fusion.9.refs_5_.refs_6_ = f32[768,2048]{1,0:T(8,128)S(1)} fusion(bf16[2048,2048]{1,0:T(8,128)(2,1)S(1)} %constant_dynamic-update-slice_fusion.3, bf16[192,2048]{1,0:T(8,128)(2,1)S(1)} %collective-permute-done.19.refs_5_, bf16[192,2048]{1,0:T(8,128)(2,1)S(1)} %collective-permute-done.18.refs_4_, bf16[192,2048]{1,0:T(8,128)(2,1)S(1)} %collective-permute-done.14.refs_1_, ...), kind=kOutput, calls=%fused_computation.23 | convolution fusion | flops 6455033856 | bytes 17825792 | tf_op jit(solution)/shard_map/dot_general | solution.py:27
  164.1 7.6 %collective-permute-done.21 = bf16[192,2048]{1,0:T(8,128)(2,1)} collective-permute-done((bf16[192,2048]{1,0:T(8,128)(2,1)S(1)}, bf16[192,2048]{1,0:T(8,128)(2,1)}, u32[]{:S(2)}, u32[]{:S(2)}) %collective-permute-start.21) | collective-permute-done | bytes 786464 | tf_op jit(solution)/shard_map/ppermute | solution.py:533
  171.8 6.0 fusion.52.refs_3_.refs_4_
  182.4 4.8 convolution_convert_fusion.2
  187.3 5.6 collective-permute-done.22
  193.0 3.4 fusion.123
  198.6 25.3 %collective-permute-done.24 = bf16[192,2048]{1,0:T(8,128)(2,1)S(1)} collective-permute-done((bf16[192,2048]{1,0:T(8,128)(2,1)S(1)}, bf16[192,2048]{1,0:T(8,128)(2,1)S(1)}, u32[]{:S(2)}, u32[]{:S(2)}) %collective-permute-start.24) | collective-permute-done | bytes 786464 | tf_op jit(solution)/shard_map/ppermute | solution.py:52
  225.7 11.9 %collective-permute-done.23 = bf16[192,2048]{1,0:T(8,128)(2,1)S(1)} collective-permute-done((bf16[192,2048]{1,0:T(8,128)(2,1)S(1)}, bf16[192,2048]{1,0:T(8,128)(2,1)S(1)}, u32[]{:S(2)}, u32[]{:S(2)}) %collective-permute-start.23) | collective-permute-done | bytes 786464 | tf_op jit(solution)/shard_map/ppermute | solution.py:52
  237.6 3.2 collective-permute-done.25
  245.8 19.1 %fusion.125.refs_2_.refs_3_ = f32[1536,2048]{1,0:T(8,128)} fusion(bf16[1536,2048]{1,0:T(8,128)(2,1)} %all-gather.7.cloned.1.call-done.refs_0_, bf16[2048,2048]{1,0:T(8,128)(2,1)} %copy-done.115), kind=kOutput, calls=%fused_computation.234 | convolution fusion | flops 12884901888 | bytes 27262976 | tf_op jit(solution)/shard_map/dot_general | solution.py:27
  266.6 4.4 shard_map.239
  271.1 7.3 %shard_map.240 = (bf16[4,192,2048]{2,1,0:T(8,128)(2,1)S(1)}, bf16[4,192,2048]{2,1,0:T(8,128)(2,1)S(1)}) custom-call(bf16[192,2048]{1,0:T(8,128)(2,1)S(1)} %collective-permute-done.28.refs_0_.refs_8_, bf16[192,2048]{1,0:T(8,128)(2,1)} %collective-permute-done.26.refs_1_.refs_9_, ...), custom_call_target="tpu_custom_call", output_to_operand_aliasing={{0}: (7, {}), {1}: (8, {})} | custom-call | flops 3221225472 | bytes 16777216 | tf_op jit(solution)/shard_map/pallas_call | solution.py:382
  280.0 23.3 %collective-permute-done.32 = bf16[192,2048]{1,0:T(8,128)(2,1)} collective-permute-done((bf16[192,2048]{1,0:T(8,128)(2,1)}, bf16[192,2048]{1,0:T(8,128)(2,1)}, u32[]{:S(2)}, u32[]{:S(2)}) %collective-permute-start.32) | collective-permute-done | bytes 786464 | tf_op jit(solution)/shard_map/ppermute | solution.py:533
  303.5 7.1 %multiply_convert_fusion = bf16[1536,1024]{1,0:T(8,128)(2,1)} fusion(f32[1536,2048]{1,0:T(8,128)} %fusion.125.refs_2_.refs_3_), kind=kLoop, calls=%fused_computation.2 | loop fusion | flops 9437184 | bytes 15728640 | tf_op jit(solution)/shard_map/convert_element_type | solution.py:526
  312.7 4.4 shard_map.241
  317.1 12.6 %convolution_convert_fusion = bf16[768,2048]{1,0:T(8,128)(2,1)} fusion(bf16[768,2048]{1,0:T(8,128)(2,1)S(1)} %bitcast.117, bf16[2048,2048]{1,0:T(8,128)(2,1)} %copy-done.115), kind=kOutput, calls=%fused_computation.8 | convolution fusion | flops 6444023808 | bytes 14680064 | tf_op jit(solution)/shard_map/dot_general | solution.py:23
  329.7 6.7 %collective-permute-done.34 = bf16[768,2048]{1,0:T(8,128)(2,1)} collective-permute-done((bf16[768,2048]{1,0:T(8,128)(2,1)}, bf16[768,2048]{1,0:T(8,128)(2,1)}, u32[]{:S(2)}, u32[]{:S(2)}) %collective-permute-start.34) | collective-permute-done | bytes 3145760 | tf_op jit(solution)/shard_map/ppermute | solution.py:52
  336.5 12.8 %fusion.110 = (bf16[768,2048]{1,0:T(8,128)(2,1)}, f32[768,2048]{1,0:T(8,128)}) fusion(bf16[768,2048]{1,0:T(8,128)(2,1)} %collective-permute-done.34, bf16[768,2048]{1,0:T(8,128)(2,1)S(1)} %bitcast.114, bf16[2048,2048]{1,0:T(8,128)(2,1)} %copy-done.115), kind=kOutput, calls=%fused_computation.221 | convolution fusion | flops 6447169536 | bytes 24117248 | tf_op jit(solution)/shard_map/dot_general | solution.py:23
  358.4 3.1 fusion.126
  363.4 4.0 convolution_add_fusion
  371.4 16.7 %shard_map.243 = (bf16[4,192,2048]{2,1,0:T(8,128)(2,1)}, bf16[4,192,2048]{2,1,0:T(8,128)(2,1)}) custom-call(bf16[1536,2048]{1,0:T(8,128)(2,1)} %all-gather.9.cloned.1.call-done.refs_0_.refs_1_, bf16[1024,2048]{1,0:T(8,128)(2,1)} %refs_1_.1, f32[1536,2048]{1,0:T(8,128)} %fusion.125.refs_2_.refs_3_, f32[1536,2048]{1,0:T(8,128)} %fusion.125.refs_2_.refs_3_), custom_call_target="tpu_custom_call" | custom-call | flops 6442450944 | bytes 29360128 | tf_op jit(solution)/shard_map/pallas_call | solution.py:382
  388.3 3.5 multiply_reduce_fusion
  395.7 2.8 copy-done.14
  405.7 3.9 fusion.128
  421.8 4.3 collective-permute-done.43
  449.3 19.4 %shard_map.245 = (f32[8,192,512]{2,1,0:T(8,128)S(1)}, bf16[8,192,256]{2,1,0:T(8,128)(2,1)S(1)}, f32[8,2,192]{2,1,0:T(2,128)S(1)}, f32[2,256]{1,0:T(2,128)S(1)}) custom-call(s32[8]{0:T(128)S(1)} %copy-done.80, f32[8,192,768]{2,1,0:T(8,128)S(1)} %bitcast.127, f32[8,192,2]{2,1,0:T(8,128)S(1)} %bitcast.132, f32[2,256]{1,0:T(2,128)S(1)} %copy-done.78, ...), custom_call_target="tpu_custom_call" | custom-call | flops 8000000000 | bytes 20000000 | tf_op jit(solution)/shard_map/pallas_call | solution.py:322
  483.9 10.9 %convolution_convert_fusion.4 = bf16[2048,768]{1,0:T(8,128)(2,1)} fusion(bf16[1536,2048]{1,0:T(8,128)(2,1)} %copy-done.38, bf16[1536,256]{1,0:T(8,128)(2,1)S(1)} %bitcast.129, bf16[1536,256]{1,0:T(8,128)(2,1)S(1)} %get-tuple-element.267, bf16[1536,256]{1,0:T(8,128)(2,1)S(1)} %get-tuple-element.266), kind=kOutput, calls=%fused_computation.12 | convolution fusion | flops 4840488960 | bytes 11796480 | tf_op jit(solution)/shard_map/dot_general | solution.py:19
  497.2 4.1 convolution_convert_fusion.1
  507.2 5.7 fusion.124
  529.9 3.2 convolution_add_fusion.2
  533.1 4.4 add_add_fusion
  543.9 3.6 dynamic-slice_bitcast_fusion
  548.2 2.8 collective-permute-done.54
  551.0 3.1 fusion.27
  554.1 44.9 %reduce-scatter.5.cloned.1.call-done = bf16[512,768]{1,0:T(8,128)(2,1)} async-done(((bf16[2048,768]{1,0:T(8,128)(2,1)}), bf16[512,768]{1,0:T(8,128)(2,1)}) %reduce-scatter.5.cloned.1.call-update) | async-done | bytes 786448 | tf_op jit(solution)/shard_map/reduce_scatter | solution.py:136
  (571 shorter events, 201.2 us)
Async XLA Ops:
  7.2 236.6 %all-gather.7.cloned.1.call-start = ((), (), s32[]{:S(2)}) async-start(), calls=%async_computation.2 | async-start | bytes 7077888 | tf_op jit(solution)/shard_map/all_gather | solution.py:539
  7.2 21.2 %collective-permute-start = (bf16[192,2048]{1,0:T(8,128)(2,1)}, bf16[192,2048]{1,0:T(8,128)(2,1)S(1)}, u32[]{:S(2)}, u32[]{:S(2)}) collective-permute-start(bf16[192,2048]{1,0:T(8,128)(2,1)} %refs_2_.3), channel_id=1, source_target_pairs={{0,4},{1,3},{2,6},{3,1},{4,0},{5,7},{6,2},{7,5},{8,12},{9,11},{10,... | collective-permute-start | bytes 2359304 | tf_op jit(solution)/shard_map/ppermute | solution.py:52
  10.3 25.8 %collective-permute-start.2 = (bf16[192,2048]{1,0:T(8,128)(2,1)}, bf16[192,2048]{1,0:T(8,128)(2,1)S(1)}, u32[]{:S(2)}, u32[]{:S(2)}) collective-permute-start(bf16[192,2048]{1,0:T(8,128)(2,1)} %refs_2_.3), channel_id=1, source_target_pairs={{0,1},{1,0},{2,3},{3,2},{4,5},{5,4},{6,7},{7,6},{8,9},{9,8},{10,11... | collective-permute-start | bytes 2359304 | tf_op jit(solution)/shard_map/ppermute | solution.py:52
  10.3 18.2 %collective-permute-start.3 = (bf16[192,2048]{1,0:T(8,128)(2,1)}, bf16[192,2048]{1,0:T(8,128)(2,1)S(1)}, u32[]{:S(2)}, u32[]{:S(2)}) collective-permute-start(bf16[192,2048]{1,0:T(8,128)(2,1)} %refs_2_.3), channel_id=1, source_target_pairs={{0,2},{1,5},{2,0},{3,7},{4,6},{5,1},{6,4},{7,3},{8,10},{9,13},{10,... | collective-permute-start | bytes 2359304 | tf_op jit(solution)/shard_map/ppermute | solution.py:52
  28.4 10.1 %collective-permute-start.5 = (bf16[192,2048]{1,0:T(8,128)(2,1)S(1)}, bf16[192,2048]{1,0:T(8,128)(2,1)}, u32[]{:S(2)}, u32[]{:S(2)}) collective-permute-start(bf16[192,2048]{1,0:T(8,128)(2,1)S(1)} %collective-permute-done.refs_1_), channel_id=1, source_target_pairs={{0,1},{1,0},{2,3},{3,2},{4,5},{5,4},{6,7},{7,6},{8,9},{9,8},{10,11... | collective-permute-start | bytes 2359304 | tf_op jit(solution)/shard_map/ppermute | solution.py:52
  28.4 10.1 %collective-permute-start.4 = (bf16[192,2048]{1,0:T(8,128)(2,1)S(1)}, bf16[192,2048]{1,0:T(8,128)(2,1)}, u32[]{:S(2)}, u32[]{:S(2)}) collective-permute-start(bf16[192,2048]{1,0:T(8,128)(2,1)S(1)} %collective-permute-done.3.refs_0_), channel_id=1, source_target_pairs={{0,1},{1,0},{2,3},{3,2},{4,5},{5,4},{6,7},{7,6},{8,9},{9,8},{10,11... | collective-permute-start | bytes 2359304 | tf_op jit(solution)/shard_map/ppermute | solution.py:52
  34.4 12.1 %collective-permute-start.1 = (bf16[192,2048]{1,0:T(8,128)(2,1)S(1)}, bf16[192,2048]{1,0:T(8,128)(2,1)}, u32[]{:S(2)}, u32[]{:S(2)}) collective-permute-start(bf16[192,2048]{1,0:T(8,128)(2,1)S(1)} %collective-permute-done.refs_1_), channel_id=1, source_target_pairs={{0,2},{1,5},{2,0},{3,7},{4,6},{5,1},{6,4},{7,3},{8,10},{9,13},{10,... | collective-permute-start | bytes 2359304 | tf_op jit(solution)/shard_map/ppermute | solution.py:52
  94.9 12.1 %collective-permute-start.12 = (bf16[192,2048]{1,0:T(8,128)(2,1)S(1)}, bf16[192,2048]{1,0:T(8,128)(2,1)S(1)}, u32[]{:S(2)}, u32[]{:S(2)}) collective-permute-start(bf16[192,2048]{1,0:T(8,128)(2,1)S(1)} %get-tuple-element.277), channel_id=1, source_target_pairs={{0,2},{1,5},{2,0},{3,7},{4,6},{5,1},{6,4},{7,3},{8,10},{9,13},{10,... | collective-permute-start | bytes 2359304 | tf_op jit(solution)/shard_map/ppermute | solution.py:52
  96.5 24.8 %collective-permute-start.11 = (bf16[192,2048]{1,0:T(8,128)(2,1)S(1)}, bf16[192,2048]{1,0:T(8,128)(2,1)S(1)}, u32[]{:S(2)}, u32[]{:S(2)}) collective-permute-start(bf16[192,2048]{1,0:T(8,128)(2,1)S(1)} %get-tuple-element.276), channel_id=1, source_target_pairs={{0,2},{1,5},{2,0},{3,7},{4,6},{5,1},{6,4},{7,3},{8,10},{9,13},{10,... | collective-permute-start | bytes 2359304 | tf_op jit(solution)/shard_map/ppermute | solution.py:52
  107.2 16.0 %collective-permute-start.13 = (bf16[192,2048]{1,0:T(8,128)(2,1)S(1)}, bf16[192,2048]{1,0:T(8,128)(2,1)S(1)}, u32[]{:S(2)}, u32[]{:S(2)}) collective-permute-start(bf16[192,2048]{1,0:T(8,128)(2,1)S(1)} %fusion.38), channel_id=1, source_target_pairs={{0,4},{1,3},{2,6},{3,1},{4,0},{5,7},{6,2},{7,5},{8,12},{9,11},{10,... | collective-permute-start | bytes 2359304 | tf_op jit(solution)/shard_map/ppermute | solution.py:52
  124.7 19.6 %collective-permute-start.14 = (bf16[192,2048]{1,0:T(8,128)(2,1)S(1)}, bf16[192,2048]{1,0:T(8,128)(2,1)S(1)}, u32[]{:S(2)}, u32[]{:S(2)}) collective-permute-start(bf16[192,2048]{1,0:T(8,128)(2,1)S(1)} %fusion.74.refs_2_), channel_id=1, source_target_pairs={{0,4},{1,3},{2,6},{3,1},{4,0},{5,7},{6,2},{7,5},{8,12},{9,11},{10,... | collective-permute-start | bytes 2359304 | tf_op jit(solution)/shard_map/ppermute | solution.py:52
  126.5 20.1 %collective-permute-start.17 = (bf16[192,2048]{1,0:T(8,128)(2,1)S(1)}, bf16[192,2048]{1,0:T(8,128)(2,1)S(1)}, u32[]{:S(2)}, u32[]{:S(2)}) collective-permute-start(bf16[192,2048]{1,0:T(8,128)(2,1)S(1)} %fusion.74.refs_2_), channel_id=1, source_target_pairs={{0,2},{1,5},{2,0},{3,7},{4,6},{5,1},{6,4},{7,3},{8,10},{9,13},{10,... | collective-permute-start | bytes 2359304 | tf_op jit(solution)/shard_map/ppermute | solution.py:52
  128.0 19.1 %collective-permute-start.16 = (bf16[192,2048]{1,0:T(8,128)(2,1)S(1)}, bf16[192,2048]{1,0:T(8,128)(2,1)S(1)}, u32[]{:S(2)}, u32[]{:S(2)}) collective-permute-start(bf16[192,2048]{1,0:T(8,128)(2,1)S(1)} %fusion.74.refs_2_), channel_id=1, source_target_pairs={{0,1},{1,0},{2,3},{3,2},{4,5},{5,4},{6,7},{7,6},{8,9},{9,8},{10,11... | collective-permute-start | bytes 2359304 | tf_op jit(solution)/shard_map/ppermute | solution.py:52
  133.9 37.8 %collective-permute-start.21 = (bf16[192,2048]{1,0:T(8,128)(2,1)S(1)}, bf16[192,2048]{1,0:T(8,128)(2,1)}, u32[]{:S(2)}, u32[]{:S(2)}) collective-permute-start(bf16[192,2048]{1,0:T(8,128)(2,1)S(1)} %fusion.74.refs_2_), channel_id=1, source_target_pairs={{0,16},{8,24},{16,0},{24,8},{1,17},{9,25},{17,1},{25,9},{2,18},{10... | collective-permute-start | bytes 2359304 | tf_op jit(solution)/shard_map/ppermute | solution.py:533
  144.2 17.9 %collective-permute-start.15 = (bf16[192,2048]{1,0:T(8,128)(2,1)S(1)}, bf16[192,2048]{1,0:T(8,128)(2,1)S(1)}, u32[]{:S(2)}, u32[]{:S(2)}) collective-permute-start(bf16[192,2048]{1,0:T(8,128)(2,1)S(1)} %collective-permute-done.14.refs_1_), channel_id=1, source_target_pairs={{0,2},{1,5},{2,0},{3,7},{4,6},{5,1},{6,4},{7,3},{8,10},{9,13},{10,... | collective-permute-start | bytes 2359304 | tf_op jit(solution)/shard_map/ppermute | solution.py:52
  146.6 6.2 %collective-permute-start.19 = (bf16[192,2048]{1,0:T(8,128)(2,1)S(1)}, bf16[192,2048]{1,0:T(8,128)(2,1)S(1)}, u32[]{:S(2)}, u32[]{:S(2)}) collective-permute-start(bf16[192,2048]{1,0:T(8,128)(2,1)S(1)} %collective-permute-done.14.refs_1_), channel_id=1, source_target_pairs={{0,1},{1,0},{2,3},{3,2},{4,5},{5,4},{6,7},{7,6},{8,9},{9,8},{10,11... | collective-permute-start | bytes 2359304 | tf_op jit(solution)/shard_map/ppermute | solution.py:52
  146.6 6.2 collective-permute-start.18
  162.2 9.5 %collective-permute-start.20 = (bf16[192,2048]{1,0:T(8,128)(2,1)S(1)}, bf16[192,2048]{1,0:T(8,128)(2,1)S(1)}, u32[]{:S(2)}, u32[]{:S(2)}) collective-permute-start(bf16[192,2048]{1,0:T(8,128)(2,1)S(1)} %collective-permute-done.15.refs_3_), channel_id=1, source_target_pairs={{0,1},{1,0},{2,3},{3,2},{4,5},{5,4},{6,7},{7,6},{8,9},{9,8},{10,11... | collective-permute-start | bytes 2359304 | tf_op jit(solution)/shard_map/ppermute | solution.py:52
  171.7 199.7 %all-gather.9.cloned.1.call-start = ((), (), s32[]{:S(2)}) async-start(), calls=%async_computation.3 | async-start | bytes 7077888 | tf_op jit(solution)/shard_map/all_gather | solution.py:572
  196.5 27.4 %collective-permute-start.24 = (bf16[192,2048]{1,0:T(8,128)(2,1)S(1)}, bf16[192,2048]{1,0:T(8,128)(2,1)S(1)}, u32[]{:S(2)}, u32[]{:S(2)}) collective-permute-start(bf16[192,2048]{1,0:T(8,128)(2,1)S(1)} %get-tuple-element.275), channel_id=1, source_target_pairs={{0,2},{1,5},{2,0},{3,7},{4,6},{5,1},{6,4},{7,3},{8,10},{9,13},{10,... | collective-permute-start | bytes 2359304 | tf_op jit(solution)/shard_map/ppermute | solution.py:52
  197.1 40.5 %collective-permute-start.23 = (bf16[192,2048]{1,0:T(8,128)(2,1)S(1)}, bf16[192,2048]{1,0:T(8,128)(2,1)S(1)}, u32[]{:S(2)}, u32[]{:S(2)}) collective-permute-start(bf16[192,2048]{1,0:T(8,128)(2,1)S(1)} %get-tuple-element.274), channel_id=1, source_target_pairs={{0,2},{1,5},{2,0},{3,7},{4,6},{5,1},{6,4},{7,3},{8,10},{9,13},{10,... | collective-permute-start | bytes 2359304 | tf_op jit(solution)/shard_map/ppermute | solution.py:52
  224.2 16.6 %collective-permute-start.25 = (bf16[192,2048]{1,0:T(8,128)(2,1)S(1)}, bf16[192,2048]{1,0:T(8,128)(2,1)S(1)}, u32[]{:S(2)}, u32[]{:S(2)}) collective-permute-start(bf16[192,2048]{1,0:T(8,128)(2,1)S(1)} %fusion.34), channel_id=1, source_target_pairs={{0,4},{1,3},{2,6},{3,1},{4,0},{5,7},{6,2},{7,5},{8,12},{9,11},{10,... | collective-permute-start | bytes 2359304 | tf_op jit(solution)/shard_map/ppermute | solution.py:52
  243.7 21.1 %collective-permute-start.26 = (bf16[192,2048]{1,0:T(8,128)(2,1)}, bf16[192,2048]{1,0:T(8,128)(2,1)}, u32[]{:S(2)}, u32[]{:S(2)}) collective-permute-start(bf16[192,2048]{1,0:T(8,128)(2,1)} %fusion.23.refs_0_.refs_10_), channel_id=1, source_target_pairs={{0,4},{1,3},{2,6},{3,1},{4,0},{5,7},{6,2},{7,5},{8,12},{9,11},{10,... | collective-permute-start | bytes 2359304 | tf_op jit(solution)/shard_map/ppermute | solution.py:52
  244.1 20.8 %collective-permute-start.28 = (bf16[192,2048]{1,0:T(8,128)(2,1)}, bf16[192,2048]{1,0:T(8,128)(2,1)S(1)}, u32[]{:S(2)}, u32[]{:S(2)}) collective-permute-start(bf16[192,2048]{1,0:T(8,128)(2,1)} %fusion.23.refs_0_.refs_10_), channel_id=1, source_target_pairs={{0,2},{1,5},{2,0},{3,7},{4,6},{5,1},{6,4},{7,3},{8,10},{9,13},{10,... | collective-permute-start | bytes 2359304 | tf_op jit(solution)/shard_map/ppermute | solution.py:52
  245.8 20.8 %collective-permute-start.31 = (bf16[192,2048]{1,0:T(8,128)(2,1)}, bf16[192,2048]{1,0:T(8,128)(2,1)S(1)}, u32[]{:S(2)}, u32[]{:S(2)}) collective-permute-start(bf16[192,2048]{1,0:T(8,128)(2,1)} %fusion.23.refs_0_.refs_10_), channel_id=1, source_target_pairs={{0,1},{1,0},{2,3},{3,2},{4,5},{5,4},{6,7},{7,6},{8,9},{9,8},{10,11... | collective-permute-start | bytes 2359304 | tf_op jit(solution)/shard_map/ppermute | solution.py:52
  264.9 6.2 %collective-permute-start.29 = (bf16[192,2048]{1,0:T(8,128)(2,1)S(1)}, bf16[192,2048]{1,0:T(8,128)(2,1)S(1)}, u32[]{:S(2)}, u32[]{:S(2)}) collective-permute-start(bf16[192,2048]{1,0:T(8,128)(2,1)S(1)} %collective-permute-done.28.refs_0_.refs_8_), channel_id=1, source_target_pairs={{0,1},{1,0},{2,3},{3,2},{4,5},{5,4},{6,7},{7,6},{8,9},{9,8},{10,11... | collective-permute-start | bytes 2359304 | tf_op jit(solution)/shard_map/ppermute | solution.py:52
  265.3 5.7 collective-permute-start.30
  265.4 37.9 %collective-permute-start.32 = (bf16[192,2048]{1,0:T(8,128)(2,1)}, bf16[192,2048]{1,0:T(8,128)(2,1)}, u32[]{:S(2)}, u32[]{:S(2)}) collective-permute-start(bf16[192,2048]{1,0:T(8,128)(2,1)} %fusion.23.refs_0_.refs_10_), channel_id=1, source_target_pairs={{0,16},{8,24},{16,0},{24,8},{1,17},{9,25},{17,1},{25,9},{2,18},{10... | collective-permute-start | bytes 2359304 | tf_op jit(solution)/shard_map/ppermute | solution.py:533
  265.8 37.5 %collective-permute-start.27 = (bf16[192,2048]{1,0:T(8,128)(2,1)}, bf16[192,2048]{1,0:T(8,128)(2,1)}, u32[]{:S(2)}, u32[]{:S(2)}) collective-permute-start(bf16[192,2048]{1,0:T(8,128)(2,1)} %collective-permute-done.26.refs_1_.refs_9_), channel_id=1, source_target_pairs={{0,2},{1,5},{2,0},{3,7},{4,6},{5,1},{6,4},{7,3},{8,10},{9,13},{10,... | collective-permute-start | bytes 2359304 | tf_op jit(solution)/shard_map/ppermute | solution.py:52
  303.4 237.3 %all-gather.11.cloned.1.call-start = ((), (), s32[]{:S(2)}) async-start(), calls=%async_computation.6 | async-start | bytes 3145728 | tf_op jit(solution)/shard_map/all_gather | solution.py:140
  303.5 7.2 %collective-permute-start.33 = (bf16[192,2048]{1,0:T(8,128)(2,1)}, bf16[192,2048]{1,0:T(8,128)(2,1)S(1)}, u32[]{:S(2)}, u32[]{:S(2)}) collective-permute-start(bf16[192,2048]{1,0:T(8,128)(2,1)} %collective-permute-done.27.refs_0_.refs_11_), channel_id=1, source_target_pairs={{0,1},{1,0},{2,3},{3,2},{4,5},{5,4},{6,7},{7,6},{8,9},{9,8},{10,11... | collective-permute-start | bytes 2359304 | tf_op jit(solution)/shard_map/ppermute | solution.py:52
  329.7 6.7 %collective-permute-start.34 = (bf16[768,2048]{1,0:T(8,128)(2,1)}, bf16[768,2048]{1,0:T(8,128)(2,1)}, u32[]{:S(2)}, u32[]{:S(2)}) collective-permute-start(bf16[768,2048]{1,0:T(8,128)(2,1)} %convolution_convert_fusion), channel_id=1, source_target_pairs={{0,1},{1,0},{2,3},{3,2},{4,5},{5,4},{6,7},{7,6},{8,9},{9,8},{10,11... | collective-permute-start | bytes 9437192 | tf_op jit(solution)/shard_map/ppermute | solution.py:52
  351.8 15.6 %collective-permute-start.35 = (bf16[192,2048]{1,0:T(8,128)(2,1)S(1)}, bf16[192,2048]{1,0:T(8,128)(2,1)S(1)}, u32[]{:S(2)}, u32[]{:S(2)}) collective-permute-start(bf16[192,2048]{1,0:T(8,128)(2,1)S(1)} %get-tuple-element.273), channel_id=1, source_target_pairs={{0,2},{1,5},{2,0},{3,7},{4,6},{5,1},{6,4},{7,3},{8,10},{9,13},{10,... | collective-permute-start | bytes 2359304 | tf_op jit(solution)/shard_map/ppermute | solution.py:52
  352.1 36.2 %collective-permute-start.37 = (bf16[192,2048]{1,0:T(8,128)(2,1)}, bf16[192,2048]{1,0:T(8,128)(2,1)}, u32[]{:S(2)}, u32[]{:S(2)}) collective-permute-start(bf16[192,2048]{1,0:T(8,128)(2,1)} %get-tuple-element.272), channel_id=1, source_target_pairs={{0,2},{1,5},{2,0},{3,7},{4,6},{5,1},{6,4},{7,3},{8,10},{9,13},{10,... | collective-permute-start | bytes 2359304 | tf_op jit(solution)/shard_map/ppermute | solution.py:52
  370.0 18.2 %collective-permute-start.36 = (bf16[192,2048]{1,0:T(8,128)(2,1)}, bf16[192,2048]{1,0:T(8,128)(2,1)}, u32[]{:S(2)}, u32[]{:S(2)}) collective-permute-start(bf16[192,2048]{1,0:T(8,128)(2,1)} %fusion.33), channel_id=1, source_target_pairs={{0,4},{1,3},{2,6},{3,1},{4,0},{5,7},{6,2},{7,5},{8,12},{9,11},{10,... | collective-permute-start | bytes 2359304 | tf_op jit(solution)/shard_map/ppermute | solution.py:52
  394.0 19.8 %collective-permute-start.38 = (bf16[192,2048]{1,0:T(8,128)(2,1)}, bf16[192,2048]{1,0:T(8,128)(2,1)}, u32[]{:S(2)}, u32[]{:S(2)}) collective-permute-start(bf16[192,2048]{1,0:T(8,128)(2,1)} %get-tuple-element.184), channel_id=1, source_target_pairs={{0,4},{1,3},{2,6},{3,1},{4,0},{5,7},{6,2},{7,5},{8,12},{9,11},{10,... | collective-permute-start | bytes 2359304 | tf_op jit(solution)/shard_map/ppermute | solution.py:52
  395.4 23.2 %collective-permute-start.39 = (bf16[192,2048]{1,0:T(8,128)(2,1)}, bf16[192,2048]{1,0:T(8,128)(2,1)}, u32[]{:S(2)}, u32[]{:S(2)}) collective-permute-start(bf16[192,2048]{1,0:T(8,128)(2,1)} %get-tuple-element.184), channel_id=1, source_target_pairs={{0,1},{1,0},{2,3},{3,2},{4,5},{5,4},{6,7},{7,6},{8,9},{9,8},{10,11... | collective-permute-start | bytes 2359304 | tf_op jit(solution)/shard_map/ppermute | solution.py:52
  395.4 20.3 %collective-permute-start.40 = (bf16[192,2048]{1,0:T(8,128)(2,1)}, bf16[192,2048]{1,0:T(8,128)(2,1)}, u32[]{:S(2)}, u32[]{:S(2)}) collective-permute-start(bf16[192,2048]{1,0:T(8,128)(2,1)} %get-tuple-element.184), channel_id=1, source_target_pairs={{0,2},{1,5},{2,0},{3,7},{4,6},{5,1},{6,4},{7,3},{8,10},{9,13},{10,... | collective-permute-start | bytes 2359304 | tf_op jit(solution)/shard_map/ppermute | solution.py:52
  413.8 12.3 %collective-permute-start.43 = (bf16[192,2048]{1,0:T(8,128)(2,1)}, bf16[192,2048]{1,0:T(8,128)(2,1)}, u32[]{:S(2)}, u32[]{:S(2)}) collective-permute-start(bf16[192,2048]{1,0:T(8,128)(2,1)} %collective-permute-done.38), channel_id=1, source_target_pairs={{0,2},{1,5},{2,0},{3,7},{4,6},{5,1},{6,4},{7,3},{8,10},{9,13},{10,... | collective-permute-start | bytes 2359304 | tf_op jit(solution)/shard_map/ppermute | solution.py:52
  415.6 126.5 %reduce-scatter.3.cloned.1.call-start = ((), (), s32[]{:S(2)}) async-start(), calls=%async_computation.4 | async-start | bytes 1310720 | tf_op jit(solution)/shard_map/reduce_scatter | solution.py:136
  432.6 111.3 %all-gather.13.cloned.1.call-start = ((), (), s32[]{:S(2)}) async-start(), calls=%async_computation.7 | async-start | bytes 6291456 | tf_op jit(solution)/shard_map/all_gather | solution.py:140
  477.6 121.4 %reduce-scatter.5.cloned.1.call-start = ((), (), s32[]{:S(2)}) async-start(), calls=%async_computation.5 | async-start | bytes 3932160 | tf_op jit(solution)/shard_map/reduce_scatter | solution.py:136
  501.2 6.0 collective-permute-start.48
  501.7 14.5 %collective-permute-start.52 = (f32[8192]{0:T(1024)S(1)}, f32[8192]{0:T(1024)S(1)}, u32[]{:S(2)}, u32[]{:S(2)}) collective-permute-start(f32[8192]{0:T(1024)S(1)} %bitcast.144), channel_id=1, source_target_pairs={{0,16},{8,24},{16,0},{24,8},{1,17},{9,25},{17,1},{25,9},{2,18},{10... | collective-permute-start | bytes 98312 | tf_op jit(solution)/shard_map/ppermute | solution.py:152
  504.1 12.1 %collective-permute-start.53 = (f32[8192]{0:T(1024)S(1)}, f32[8192]{0:T(1024)S(1)}, u32[]{:S(2)}, u32[]{:S(2)}) collective-permute-start(f32[8192]{0:T(1024)S(1)} %bitcast.145), channel_id=1, source_target_pairs={{0,24},{8,16},{16,8},{24,0},{1,25},{9,17},{17,9},{25,1},{2,26},{10... | collective-permute-start | bytes 98312 | tf_op jit(solution)/shard_map/ppermute | solution.py:152
  514.2 23.3 %collective-permute-start.50 = (bf16[192,2048]{1,0:T(8,128)(2,1)S(1)}, bf16[192,2048]{1,0:T(8,128)(2,1)S(1)}, u32[]{:S(2)}, u32[]{:S(2)}) collective-permute-start(bf16[192,2048]{1,0:T(8,128)(2,1)S(1)} %get-tuple-element.271), channel_id=1, source_target_pairs={{0,2},{1,5},{2,0},{3,7},{4,6},{5,1},{6,4},{7,3},{8,10},{9,13},{10,... | collective-permute-start | bytes 2359304 | tf_op jit(solution)/shard_map/ppermute | solution.py:52
  515.8 32.4 %collective-permute-start.49 = (bf16[192,2048]{1,0:T(8,128)(2,1)}, bf16[192,2048]{1,0:T(8,128)(2,1)S(1)}, u32[]{:S(2)}, u32[]{:S(2)}) collective-permute-start(bf16[192,2048]{1,0:T(8,128)(2,1)} %get-tuple-element.270), channel_id=1, source_target_pairs={{0,2},{1,5},{2,0},{3,7},{4,6},{5,1},{6,4},{7,3},{8,10},{9,13},{10,... | collective-permute-start | bytes 2359304 | tf_op jit(solution)/shard_map/ppermute | solution.py:52
  538.6 12.3 %collective-permute-start.54 = (bf16[192,2048]{1,0:T(8,128)(2,1)}, bf16[192,2048]{1,0:T(8,128)(2,1)}, u32[]{:S(2)}, u32[]{:S(2)}) collective-permute-start(bf16[192,2048]{1,0:T(8,128)(2,1)} %fusion.25), channel_id=1, source_target_pairs={{0,4},{1,3},{2,6},{3,1},{4,0},{5,7},{6,2},{7,5},{8,12},{9,11},{10,... | collective-permute-start | bytes 2359304 | tf_op jit(solution)/shard_map/ppermute | solution.py:52
  (175 other events, 1169.1 us)
Sparse Core Ops, SparseCore 0:
  171.9 53.9 all-gather.6
  303.5 43.4 all-gather.8
  415.8 31.1 all-gather.10
  449.7 27.1 reduce-scatter.2
  478.9 57.5 all-gather.12
  538.7 60.2 reduce-scatter.4

commit v2 on v1

v2 whole, which is shorter than its diff:
```python
import functools

import jax
import jax.numpy as jnp
from jax import lax
from jax.experimental import pallas as pl
from jax.experimental.pallas import tpu as pltpu
from jax.sharding import PartitionSpec as P

HEAD_DIM = 128
BF16 = jnp.bfloat16
F32 = jnp.float32

norm_eps = 1e-06
rope_base = 500000.0


def contract_rows(left, right):
    return lax.dot_general(left, right, (((0,), (0,)), ((), ())), preferred_element_type=F32)


def times_transposed(left, right):
    return lax.dot_general(left, right, (((1,), (1,)), ((), ())), preferred_element_type=F32)


def times(left, right):
    return jnp.dot(left, right, preferred_element_type=F32)


def rope_table(length, head_dim):
    half = head_dim // 2
    freq = rope_base ** (-(2.0 * jnp.arange(half, dtype=F32)) / head_dim)
    angle = jnp.arange(length, dtype=F32)[:, None] * freq[None, :]
    return jnp.concatenate([jnp.cos(angle), jnp.sin(angle)], axis=1)


def norm_back(grad, unit, inverse, gain):
    inner = grad * gain
    return inverse * (inner - unit * jnp.mean(inner * unit, axis=1, keepdims=True))


class PairedCores:
    def __init__(self):
        turn = lambda low, high: [(i, i ^ (low if i % 2 == 0 else high)) for i in range(8)]
        self.first, self.second, self.core = turn(2, 4), turn(4, 2), turn(1, 1)

    def send(self, value, way):
        return lax.ppermute(value, "tensor", way)

    def order(self):
        me = lax.axis_index("tensor")
        near = jnp.where(me % 2 == 0, 2, 4)
        far = 6 - near
        return jnp.stack([me ^ near, me ^ far, me, me ^ 6, me ^ 1 ^ far, me ^ 1 ^ near, me ^ 1, me ^ 7])

    def gather(self, own, meanwhile=None, early=None):
        first, second = self.send(own, self.first), self.send(own, self.second)
        other = self.send(own, self.core)
        if meanwhile is not None:
            second, meanwhile = lax.optimization_barrier((second, meanwhile))
        opposite = self.send(second, self.first)
        first_other, second_other = self.send(first, self.core), self.send(second, self.core)
        groups = [[own, other], [first, second, first_other, second_other]]
        made = None
        if early is not None:
            opposite, made = lax.optimization_barrier((opposite, early(*groups)))
        groups.append([opposite, self.send(opposite, self.core)])
        return groups, meanwhile, made

    def whole(self, groups):
        near, middle, last = groups
        if not isinstance(near, list):
            near, middle, last = jnp.split(near, 2), jnp.split(middle, 4), jnp.split(last, 2)
        first, second, first_other, second_other = middle
        return [first, second, near[0], last[0], first_other, second_other, near[1], last[1]]

    def groups(self, whole):
        first, second, own, opposite, first_other, second_other, other, opposite_other = jnp.split(whole, 8)
        groups = [[own, other], [first, second, first_other, second_other], [opposite, opposite_other]]
        return [jnp.concatenate(group, axis=0) for group in groups]

    def scatter(self, halves, product, meanwhile=None, late=None):
        mine, others = halves
        from_core = self.send(product(others).astype(BF16), self.core)
        own_part, from_core = lax.optimization_barrier((product(mine).astype(BF16), from_core))
        first, second, own, opposite = (
            part.astype(F32) + other.astype(F32)
            for part, other in zip(jnp.split(own_part, 4), jnp.split(from_core, 4))
        )
        sent = opposite.astype(BF16), first.astype(BF16)
        passing, from_first = (self.send(part, self.first) for part in sent)
        if meanwhile is not None:
            passing, meanwhile = lax.optimization_barrier((passing, meanwhile(sent)))
        from_second = self.send((second + passing.astype(F32)).astype(BF16), self.second)
        if late is not None:
            from_second, late = lax.optimization_barrier((from_second, late(passing)))
        return own + from_first.astype(F32) + from_second.astype(F32), meanwhile, late

    def add(self, value):
        for bit in (1, 2, 4):
            value = value + self.send(value, [(i, i ^ bit) for i in range(8)])
        return value


class AnyDevices:
    def __init__(self, size):
        self.size = size

    def order(self):
        return jnp.arange(self.size)

    def gather(self, own, meanwhile=None, early=None):
        return [[lax.all_gather(own, "tensor", axis=0, tiled=True)]], meanwhile, []

    def groups(self, whole):
        return [whole]

    def whole(self, groups):
        return groups[0] if isinstance(groups[0], list) else groups

    def scatter(self, halves, product, meanwhile=None, late=None):
        part = product(jnp.concatenate(halves, axis=0)).astype(BF16)
        total = lax.psum_scatter(part, "tensor", scatter_dimension=0, tiled=True).astype(F32)
        return total, meanwhile, late

    def add(self, value):
        return lax.psum(value, "tensor")


def in_pairs(step):
    return [(i, i ^ step) for i in range(4)]


def scatter_rows(part, dimension):
    return lax.psum_scatter(part, "dp", scatter_dimension=dimension, tiled=True).astype(F32)


def halve_rows(part, dimension):
    me = lax.axis_index("dp")
    away = [piece_of(part, dimension, me ^ step) for step in (1, 3)]
    kept = [piece_of(part, dimension, me ^ step) for step in (0, 2)]
    return kept, lax.ppermute(jnp.concatenate(away, axis=dimension), "dp", in_pairs(1))


def quarter_rows(halved, dimension):
    kept, got = halved
    own, other = (k.astype(F32) + g.astype(F32) for k, g in zip(kept, jnp.split(got, 2, axis=dimension)))
    return own, lax.ppermute(other.astype(BF16), "dp", in_pairs(2))


def piece_of(part, dimension, place):
    size = part.shape[dimension] // 4
    return lax.dynamic_slice_in_dim(part, place * size, size, dimension)


def add_rows(value, count):
    if count != 4:
        return lax.psum(value, "dp")
    one, two, three = (lax.ppermute(value, "dp", in_pairs(step)) for step in (1, 2, 3))
    return value, one, two, three


def turned(value):
    return pltpu.roll(value, HEAD_DIM // 2, 1)


def cosine_sine(table):
    lanes = lax.broadcasted_iota(jnp.int32, table.shape, 1)
    front, swapped = lanes < HEAD_DIM // 2, turned(table)
    return jnp.where(front, table, swapped), jnp.where(front, -swapped, table)


def scale_of(sums, at, width):
    return lax.rsqrt(sums[:, at : at + 1] * (1.0 / width) + norm_eps)


def window_of(b, block, back):
    first = jnp.maximum(b - back, 0)
    return first, pl.ds(pl.multiple_of(first * block, block), (back + 1) * block)


def allowed_in(docs, ahead, block, back):
    docs_row, docs_col = docs[:1, :], docs[:, :block].T[:, 1:2]
    window = (back + 1) * block
    rows = lax.broadcasted_iota(jnp.int32, (block, window), 0) + ahead * block
    columns = lax.broadcasted_iota(jnp.int32, (block, window), 1)
    return (docs_col == docs_row) & (columns <= rows)


def put_in_row(groups, row):
    block = row.shape[1]
    if len(groups) == 1:
        for at in range(row.shape[0]):
            row[at] = groups[0][at * block : (at + 1) * block, :]
        return
    near, beside, last = groups
    places = (beside, 0), (beside, 1), (near, 0), (last, 0), (beside, 2), (beside, 3), (near, 1), (last, 1)
    for at, (group, place) in enumerate(places):
        row[at] = group[place * block : (place + 1) * block, :]


def attend_kernel(
    shape,
    count,
    order,
    *refs,
):
    raws, refs = refs[:count], refs[count:]
    attend_body(shape, order, raws, *refs)


def attend_body(
    shape,
    order,
    raws,
    sums,
    gains,
    table,
    docs,
    attended,
    query,
    key,
    value,
    logsum,
    keys,
    values,
    raw,
):
    blocks, block, width, local, back, scale = shape
    heads = local // HEAD_DIM
    b = pl.program_id(0)

    @pl.when(b == 0)
    def _():
        put_in_row(raws, raw)
        keys[...] = jnp.zeros(keys.shape, BF16)
        values[...] = jnp.zeros(values.shape, BF16)

    total = sums[0].T
    cos, sin = cosine_sine(table[...])
    for which in range(2):
        inverse = scale_of(total, which, width)
        for h in range(heads):
            lanes = slice(h * HEAD_DIM, (h + 1) * HEAD_DIM)
            own = slice(which * local + h * HEAD_DIM, which * local + (h + 1) * HEAD_DIM)
            v = raw[order[b], :, own] * inverse * gains[which : which + 1, lanes]
            (query, key)[which][:, lanes] = (v * cos + turned(v) * sin).astype(BF16)
    value[...] = raw[order[b], :, 2 * local :].astype(BF16)
    now = pl.ds(pl.multiple_of(b * block, block), block)
    keys[now, :] = key[...]
    values[now, :] = value[...]
    first, window = window_of(b, block, back)
    allowed = allowed_in(docs[0], b - first, block, back)
    logsums = []
    for h in range(heads):
        lanes = slice(h * HEAD_DIM, (h + 1) * HEAD_DIM)
        scores = times_transposed(query[:, lanes], keys[window, lanes]) * scale
        scores = jnp.where(allowed, scores, -1e30)
        top = jnp.max(scores, axis=1, keepdims=True)
        weights = jnp.exp(scores - top)
        mass = jnp.sum(weights, axis=1, keepdims=True)
        shares = (weights * (1.0 / mass)).astype(BF16)
        attended[0, :, lanes] = times(shares, values[window, lanes]).astype(BF16)
        logsums.append(top + jnp.log(mass))
    logsum[0] = jnp.concatenate(logsums, axis=1).T


def attend_back_kernel(
    shape,
    order,
    raw,
    sums,
    gains,
    table,
    docs,
    query,
    keys,
    values,
    logsum,
    *refs,
):
    grads = refs[:-8]
    inner, grad_value, products, gain_parts, grad_query_sum, grad_key_sum, grad_value_sum, grad = refs[-8:]
    blocks, block, width, local, back, scale = shape
    heads = local // HEAD_DIM
    b = pl.program_id(0)

    @pl.when(b == 0)
    def _():
        put_in_row(grads, grad)
        grad_key_sum[...] = jnp.zeros(grad_key_sum.shape, F32)
        grad_value_sum[...] = jnp.zeros(grad_value_sum.shape, F32)
        gain_parts[...] = jnp.zeros(gain_parts.shape, F32)

    @pl.when(b < blocks)
    def _():
        first, window = window_of(b, block, back)
        allowed = allowed_in(docs[0], b - first, block, back)
        now = pl.ds(pl.multiple_of(b * block, block), block)
        tops = logsum[0].T
        for h in range(heads):
            lanes = slice(h * HEAD_DIM, (h + 1) * HEAD_DIM)
            q, k, v, g = query[:, lanes], keys[window, lanes], values[window, lanes], grad[order[b], :, lanes]
            scores = times_transposed(q, k) * scale
            chances = jnp.exp(jnp.where(allowed, scores, -1e30) - tops[:, h : h + 1])
            grad_shares = times_transposed(g, v)
            offset = jnp.sum(chances * grad_shares, axis=1, keepdims=True)
            grad_scores = (chances * (grad_shares - offset)).astype(BF16)
            grad_query_sum[now, lanes] = times(grad_scores, k) * scale
            grad_key_sum[window, lanes] += contract_rows(grad_scores, q) * scale
            grad_value_sum[window, lanes] += contract_rows(chances.astype(BF16), g)

    @pl.when(b >= back)
    def _():
        rows = pl.ds(pl.multiple_of((b - back) * block, block), block)
        total = sums[0].T
        cos, sin = cosine_sine(table[...])
        grad_value[0] = grad_value_sum[rows, :].astype(BF16)
        all_dots = []
        for which in range(2):
            inverse = scale_of(total, which, width)
            dots = jnp.zeros((block, 1), F32)
            for h in range(heads):
                lanes = slice(h * HEAD_DIM, (h + 1) * HEAD_DIM)
                own = slice(which * local + h * HEAD_DIM, which * local + (h + 1) * HEAD_DIM)
                unit = raw[0, :, own] * inverse
                g = (grad_query_sum, grad_key_sum)[which][rows, lanes]
                g = g * cos + turned(g * sin)
                gain_parts[which : which + 1, lanes] += jnp.sum(g * unit, axis=0, keepdims=True)
                c = g * gains[which : which + 1, lanes]
                inner[0, :, own] = c
                dots = dots + jnp.sum(c * unit, axis=1, keepdims=True)
            all_dots.append(dots)
        products[0] = jnp.concatenate(all_dots, axis=1).T


def attend(shape, order, raws, sums, gains, table, docs):
    blocks, block, width, local, back, scale = shape
    heads, length = local // HEAD_DIM, blocks * block
    in_row = lambda columns: pl.BlockSpec((block, columns), lambda b, order: (b, 0))
    arrived = lambda columns: pl.BlockSpec((1, block, columns), lambda b, order: (order[b], 0, 0))
    return pl.pallas_call(
        functools.partial(attend_kernel, shape, len(raws)),
        out_shape=(
            jax.ShapeDtypeStruct((blocks, block, local), BF16),
            jax.ShapeDtypeStruct((length, local), BF16),
            jax.ShapeDtypeStruct((length, local), BF16),
            jax.ShapeDtypeStruct((length, local), BF16),
            jax.ShapeDtypeStruct((blocks, heads, block), F32),
        ),
        grid_spec=pltpu.PrefetchScalarGridSpec(
            num_scalar_prefetch=1,
            grid=(blocks,),
            in_specs=[pl.BlockSpec(raw.shape, lambda b, order: (0, 0)) for raw in raws]
            + [
                pl.BlockSpec((1, 2, block), lambda b, order: (b, 0, 0)),
                pl.BlockSpec((2, local), lambda b, order: (0, 0)),
                in_row(HEAD_DIM),
                pl.BlockSpec((1, 2, (back + 1) * block), lambda b, order: (b, 0, 0)),
            ],
            out_specs=(
                arrived(local),
                in_row(local),
                in_row(local),
                in_row(local),
                pl.BlockSpec((1, heads, block), lambda b, order: (b, 0, 0)),
            ),
            scratch_shapes=[pltpu.VMEM((length, local), BF16)] * 2 + [pltpu.VMEM((blocks, block, 3 * local), F32)],
        ),
        compiler_params=pltpu.CompilerParams(vmem_limit_bytes=30 * 2**20),
        cost_estimate=pl.CostEstimate(flops=4 * 10**9, bytes_accessed=10**7, transcendentals=2 * 10**6),
    )(order, *raws, sums, gains, table, docs)


def attend_back(shape, order, raw, sums, gains, table, docs, query, key, value, logsum, grads):
    blocks, block, width, local, back, scale = shape
    heads, length = local // HEAD_DIM, blocks * block
    now = lambda b: jnp.minimum(b, blocks - 1)
    done = lambda b: jnp.maximum(b - back, 0)
    whole = pl.BlockSpec((length, local), lambda b, order: (0, 0))
    finished = lambda columns: pl.BlockSpec((1, block, columns), lambda b, order: (order[done(b)], 0, 0))
    return pl.pallas_call(
        functools.partial(attend_back_kernel, shape),
        out_shape=(
            jax.ShapeDtypeStruct((blocks, block, 2 * local), F32),
            jax.ShapeDtypeStruct((blocks, block, local), BF16),
            jax.ShapeDtypeStruct((blocks, 2, block), F32),
            jax.ShapeDtypeStruct((2, local), F32),
        ),
        grid_spec=pltpu.PrefetchScalarGridSpec(
            num_scalar_prefetch=1,
            grid=(blocks + back,),
            in_specs=[
                finished(3 * local),
                pl.BlockSpec((1, 2, block), lambda b, order: (done(b), 0, 0)),
                pl.BlockSpec((2, local), lambda b, order: (0, 0)),
                pl.BlockSpec((block, HEAD_DIM), lambda b, order: (done(b), 0)),
                pl.BlockSpec((1, 2, (back + 1) * block), lambda b, order: (now(b), 0, 0)),
                pl.BlockSpec((block, local), lambda b, order: (now(b), 0)),
                whole,
                whole,
                pl.BlockSpec((1, heads, block), lambda b, order: (now(b), 0, 0)),
            ]
            + [pl.BlockSpec(grad.shape, lambda b, order: (0, 0)) for grad in grads],
            out_specs=(
                finished(2 * local),
                finished(local),
                pl.BlockSpec((1, 2, block), lambda b, order: (done(b), 0, 0)),
                pl.BlockSpec((2, local), lambda b, order: (0, 0)),
            ),
            scratch_shapes=[pltpu.VMEM((length, local), F32)] * 3 + [pltpu.VMEM((blocks, block, local), BF16)],
        ),
        compiler_params=pltpu.CompilerParams(vmem_limit_bytes=28 * 2**20),
        cost_estimate=pl.CostEstimate(flops=8 * 10**9, bytes_accessed=2 * 10**7, transcendentals=2 * 10**6),
    )(order, raw, sums, gains, table, docs, query, key, value, logsum, *grads)


TILE = 256


def gated_grad(grad_act, gate, up):
    sigma = jax.nn.sigmoid(gate)
    grad_gate = grad_act * up * sigma * (1.0 + gate * (1.0 - sigma))
    return grad_gate.astype(BF16), (grad_act * gate * sigma).astype(BF16)


def feed_back_kernel(count, with_activated, *refs):
    grads, (weight, both) = refs[:count], refs[count : count + 2]
    *_, mine, others, rows = refs
    activated = refs[-4] if with_activated else None
    block, tile = grads[0].shape[0], weight.shape[0]
    units, half = mine.shape[-1] // 2, rows.shape[0] // 2
    j = pl.program_id(0)

    @pl.when(j == 0)
    def _():
        for at, grad in enumerate(grads):
            rows[at * block : (at + 1) * block, :] = grad[...]

    start = pl.multiple_of(j * tile, tile)
    gate, up = (both[:, pl.ds(at, tile)].astype(F32) for at in (start, start + units))
    if activated is not None:
        activated[...] = (gate * jax.nn.sigmoid(gate) * up).astype(BF16)
    grad_act = times_transposed(rows[...], weight[...])
    for at, part in zip((start, start + units), gated_grad(grad_act, gate, up)):
        for out, own in ((mine, part[:half]), (others, part[half:])):
            out[:, :, pl.ds(at, tile)] = own.reshape(out.shape[:2] + (tile,))


def feed_back(grads, down_weight, both, slot, slots, before=(), with_activated=False):
    count, width = len(grads), grads[0].shape[1]
    units, tile = down_weight.shape[0], min(TILE, down_weight.shape[0])
    tiles, rows = units // tile, sum(grad.shape[0] for grad in grads)
    once = lambda shape: pl.BlockSpec(shape, lambda j: (0, 0), pipeline_mode=pl.Buffered(1))
    in_specs = [once(grad.shape) for grad in grads]
    in_specs += [pl.BlockSpec((tile, width), lambda j: (j, 0)), once(both.shape)]
    in_specs += [pl.BlockSpec(memory_space=pl.ANY)] * len(before)
    args = [*grads, down_weight, both, *before]
    part = rows // (2 * slots)
    extra_shape, extra_spec = (), ()
    if with_activated:
        extra_shape = (jax.ShapeDtypeStruct((rows, units), BF16),)
        extra_spec = (pl.BlockSpec((rows, tile), lambda j: (0, j)),)
    return pl.pallas_call(
        functools.partial(feed_back_kernel, count, with_activated),
        grid=(tiles,),
        out_shape=extra_shape + (jax.ShapeDtypeStruct((4, part, 2 * units), BF16),) * 2,
        in_specs=in_specs,
        out_specs=extra_spec + (pl.BlockSpec((slots, part, 2 * units), lambda j: (slot // slots, 0, 0)),) * 2,
        scratch_shapes=[pltpu.VMEM((rows, width), BF16)],
        input_output_aliases={count + 2 + at: at for at in range(len(before))},
        compiler_params=pltpu.CompilerParams(vmem_limit_bytes=(8 + 7 * rows // 192) * 2**20),
        cost_estimate=pl.CostEstimate(
            flops=2 * rows * width * units,
            bytes_accessed=2 * units * width + 12 * rows * units + 2 * rows * width,
            transcendentals=rows * units,
        ),
    )(*args)


def pieces_kernel(plan, count, place, *refs):
    sources, outs, sems = refs[:count], refs[count:-1], refs[-1]
    copies = []
    for out, parts in zip(outs, plan):
        size = out.shape[1]
        columns = pl.ds(pl.multiple_of(place[0] * size, size), size)
        at = 0
        for source, start, rows in parts:
            copies.append(
                pltpu.make_async_copy(
                    sources[source].at[pl.ds(start, rows), columns],
                    out.at[pl.ds(at, rows), :],
                    sems.at[len(copies)],
                )
            )
            at += rows
    for copy in copies:
        copy.start()
    for copy in copies:
        copy.wait()


def pieces_of(sources, plan, place, count=4):
    size = sources[0].shape[1] // count
    shapes = [(sum(rows for _, _, rows in parts), size) for parts in plan]
    return pl.pallas_call(
        functools.partial(pieces_kernel, plan, len(sources)),
        out_shape=[jax.ShapeDtypeStruct(shape, BF16) for shape in shapes],
        in_specs=[pl.BlockSpec(memory_space=pltpu.SMEM)] + [pl.BlockSpec(memory_space=pltpu.HBM)] * len(sources),
        out_specs=[pl.BlockSpec(memory_space=pltpu.HBM)] * len(plan),
        scratch_shapes=[pltpu.SemaphoreType.DMA((sum(len(parts) for parts in plan),))],
        compiler_params=pltpu.CompilerParams(vmem_limit_bytes=2**20),
        cost_estimate=pl.CostEstimate(
            flops=0, bytes_accessed=sum(4 * rows * columns for rows, columns in shapes), transcendentals=0
        ),
    )(jnp.reshape(place, (1,)).astype(jnp.int32), *sources)


def joined_rows(blocks):
    return pieces_of(blocks, [[(at, 0, block.shape[0]) for at, block in enumerate(blocks)]], 0, 1)[0]


def body(
    sizes,
    hidden_in,
    doc_ids,
    query_weight,
    key_weight,
    value_weight,
    output_weight,
    gate_weight,
    up_weight,
    down_weight,
    query_gain,
    key_gain,
    attention_gain,
    feedforward_gain,
    out_grad,
):
    tensor, rows = sizes["tensor"], sizes["dp"]
    moves = PairedCores() if tensor == 8 else AnyDevices(tensor)
    width = hidden_in.shape[1]
    local = query_weight.shape[1]
    hidden_units = gate_weight.shape[1]
    documents = doc_ids[0]
    length = documents.shape[0]
    block = length // tensor
    most = length // 4
    back = -(-(most - 1) // block)
    shape = (tensor, block, width, local, back, HEAD_DIM ** (-0.5))

    places = moves.order()
    steps = jnp.arange(tensor, dtype=jnp.int32)
    meets = places[None, :] == steps[:, None]
    order = jnp.sum(jnp.where(meets, steps[None, :], 0), axis=1)

    def in_row(value):
        parts = value.reshape(1, 2, tensor, block)
        return jnp.sum(jnp.where(meets[:, None, :, None], parts, 0.0), axis=2)

    def as_arrived(value):
        parts = value.transpose(1, 0, 2)[:, :, None]
        return jnp.sum(jnp.where(meets[None, :, :, None], parts, 0.0), axis=1).reshape(2, length)

    table = rope_table(length, HEAD_DIM)
    firsts = [max(b - back, 0) * block for b in range(tensor)]
    numbers = documents.astype(F32)
    docs = jnp.stack([numbers[first : first + (back + 1) * block] for first in firsts])
    own_docs = jnp.pad(numbers.reshape(tensor, block), ((0, 0), (0, back * block)))
    docs = jnp.stack([docs, own_docs], axis=1)
    gains = jnp.stack([query_gain, key_gain])

    def row_of(groups):
        return jnp.concatenate(moves.whole(groups), axis=0)

    def joined(group):
        return jnp.concatenate(group, axis=0)

    weight_qkv = jnp.concatenate([query_weight, key_weight, value_weight], axis=1)
    weight_gate_up = jnp.concatenate([gate_weight, up_weight], axis=1)
    paired = rows == 4 and tensor == 8

    def halves_of(whole):
        return jnp.split(whole, 2)

    def raw_of(*groups):
        return [times(joined(group), weight_qkv) for group in groups]

    hidden_groups, _, raw = moves.gather(hidden_in, early=raw_of)
    raw = raw + raw_of(hidden_groups[-1])
    squares = jnp.stack(
        [
            row_of([jnp.sum(jnp.square(part[:, at : at + local]), axis=1) for part in raw])
            for at in (0, local)
        ]
    )
    raws, raw = raw, row_of(raw)
    sums = moves.add(in_row(squares))
    tables = (sums, gains, table, docs)
    attended_blocks, query, key, value, logsum = attend(shape, order, raws, *tables)
    attended = attended_blocks.reshape(length, local)
    def join_hidden(passing):
        groups, _ = lax.optimization_barrier((hidden_groups, passing))
        return joined_rows(moves.whole(groups))

    attn_proj, _, hidden_all = moves.scatter(
        halves_of(attended),
        lambda part: times(part, output_weight),
        late=join_hidden if tensor == 8 else None,
    )
    if tensor != 8:
        hidden_all = hidden_groups[0][0]
    attn_scale = lax.rsqrt(jnp.mean(attn_proj * attn_proj, axis=1, keepdims=True) + norm_eps)
    attn_unit = attn_proj * attn_scale
    middle = hidden_in.astype(F32) + attn_unit * attention_gain
    middle_low = middle.astype(BF16)

    def activate(both):
        gate, up = both[:, :hidden_units], both[:, hidden_units:]
        return (gate * jax.nn.sigmoid(gate) * up).astype(BF16)

    def both_of(*groups):
        both = [times(joined(group), weight_gate_up) for group in groups]
        return both, [activate(part) for part in both]

    def to_pair(value):
        return lax.ppermute(value, "dp", in_pairs(2))

    def gather_pair(value):
        return lax.all_gather(value, "tensor", axis=0, tiled=True)

    pair_middle = to_pair(middle_low) if paired else None

    def both_early(*groups):
        return both_of(*groups), pair_middle

    middle_groups, _, made = moves.gather(middle_low, early=both_early)
    made, pair_middle = made or (([], []), None)
    if paired:
        pair_middle_all = gather_pair(pair_middle)
    both_groups, activated = (early + late for early, late in zip(made, both_of(middle_groups[-1])))
    activated = lax.optimization_barrier(row_of(activated))
    mlp_proj, _, _ = moves.scatter(halves_of(activated), lambda part: times(part, down_weight))
    mlp_scale = lax.rsqrt(jnp.mean(mlp_proj * mlp_proj, axis=1, keepdims=True) + norm_eps)
    mlp_unit = mlp_proj * mlp_scale
    result = middle + mlp_unit * feedforward_gain

    grad_out = out_grad.astype(F32)
    grad_mlp = norm_back(grad_out, mlp_unit, mlp_scale, feedforward_gain).astype(BF16)
    feedforward_part = jnp.sum(grad_out * mlp_unit, axis=0)
    pair_both = None
    if paired:
        pair_middle_all, grad_mlp = lax.optimization_barrier((pair_middle_all, grad_mlp))
        pair_both = times(pair_middle_all, weight_gate_up).astype(BF16)

    def back_early(near, beside):
        part = feed_back(near, down_weight, both_groups[0], 2, 1)
        part = feed_back(beside, down_weight, both_groups[1], 0, 2, part)
        return part, pair_grad_mlp[1]

    pair_grad_mlp = [None, None]
    if paired:
        first_half, second_half = jnp.split(grad_mlp, 2, axis=1)
        first_half, second_half = lax.optimization_barrier((to_pair(first_half), second_half))
        pair_grad_mlp = [first_half, to_pair(second_half)]
    meanwhile = (pair_both, pair_grad_mlp[0])
    grad_mlp_groups, (pair_both, first_half), made = moves.gather(grad_mlp, meanwhile, back_early)
    if tensor == 8:
        made, second_half = made
        grad_gate_up = feed_back(grad_mlp_groups[-1], down_weight, both_groups[2], 3, 1, made)
        grad_gate_up = [half.reshape(length // 2, 2 * hidden_units) for half in grad_gate_up]
    else:
        grad_act = times_transposed(grad_mlp_groups[0][0], down_weight)
        both = both_groups[0].astype(F32)
        grad_gate_up = gated_grad(grad_act, both[:, :hidden_units], both[:, hidden_units:])
        grad_gate_up = halves_of(jnp.concatenate(grad_gate_up, axis=1))
    if paired:
        pair_grad_mlp_all = gather_pair(jnp.concatenate([first_half, second_half], axis=1))

    me = lax.axis_index("dp")
    half_rows = length // 2

    def own_weight_pieces(place):
        blocks = moves.whole(middle_groups) + moves.whole(grad_mlp_groups)
        part = [(at, 0, block) for at in range(16)]
        mine, others, grads = pieces_of(blocks, [part[:4], part[4:8], part[8:]], place)
        return [
            contract_rows(grads, activated),
            contract_rows(mine, grad_gate_up[0]) + contract_rows(others, grad_gate_up[1]),
        ]

    def pair_weight_pieces(place):
        plan = [[(0, 0, half_rows)], [(0, half_rows, half_rows)], [(1, 0, length)]]
        first, second, grads = pieces_of([pair_middle_all, pair_grad_mlp_all], plan, place)
        return [
            contract_rows(grads, pair_activated),
            contract_rows(first, pair_gate_up[0]) + contract_rows(second, pair_gate_up[1]),
        ]

    def gate_up_own(place):
        part = [(at, 0, block) for at in range(8)]
        mine, others = pieces_of(moves.whole(middle_groups), [part[:4], part[4:]], place)
        return contract_rows(mine, grad_gate_up[0]) + contract_rows(others, grad_gate_up[1])

    def gate_up_pair(place):
        plan = [[(0, 0, half_rows)], [(0, half_rows, half_rows)]]
        first, second = pieces_of([pair_middle_all], plan, place)
        return contract_rows(first, pair_gate_up[0]) + contract_rows(second, pair_gate_up[1])

    def down_pieces(place):
        part = [(at, 0, block) for at in range(8)]
        blocks = moves.whole(grad_mlp_groups) + [pair_grad_mlp_all]
        own, pair = pieces_of(blocks, [part, [(8, 0, length)]], place)
        return contract_rows(own, activated) + contract_rows(pair, pair_activated)

    def own_away(sent):
        nonlocal grad_mlp_groups, middle_groups
        grad_mlp_groups, middle_groups, _ = lax.optimization_barrier((grad_mlp_groups, middle_groups, sent))
        return own_weight_pieces(me ^ 1)

    def pair_back(passing):
        grads, _ = lax.optimization_barrier((pair_grad_mlp_all, passing))
        pair_activated, *pair_gate_up = feed_back([grads], down_weight, pair_both, 0, 4, with_activated=True)
        return pair_activated, [half.reshape(half_rows, 2 * hidden_units) for half in pair_gate_up]

    back_part, away, pair_gate_up = moves.scatter(
        grad_gate_up,
        lambda part: times_transposed(part, weight_gate_up),
        own_away if paired else None,
        pair_back if paired else None,
    )
    grad_middle = grad_out + back_part

    grad_proj = norm_back(grad_middle, attn_unit, attn_scale, attention_gain).astype(BF16)
    attention_part = jnp.sum(grad_middle * attn_unit, axis=0)
    if paired:
        (pair_activated, pair_gate_up), grad_proj = lax.optimization_barrier((pair_gate_up, grad_proj))
        away = [(own + pair).astype(BF16) for own, pair in zip(away, pair_weight_pieces(me ^ 1))]
        away = [away[0], *jnp.split(away[1], 2, axis=1)]
        away = [half for part in away for half in jnp.split(part, 2)]
        got = [lax.ppermute(part, "dp", in_pairs(1)) for part in away]

    def attended_early(*groups):
        return [times_transposed(joined(group), output_weight).astype(BF16) for group in groups]

    def proj_early(*groups):
        if not paired:
            return attended_early(*groups), None, None
        return attended_early(*groups), got[0], gate_up_own(me)

    grad_proj_groups, away, made = moves.gather(grad_proj, away, proj_early)
    made, *rest = made or ([],)
    if paired:
        got[0], kept_gate_up = rest
    else:
        down_grad = scatter_rows(contract_rows(activated, row_of(grad_mlp_groups)).astype(BF16), 1)
        back = contract_rows(row_of(middle_groups), jnp.concatenate(grad_gate_up, axis=0))
        gate_grad, up_grad = jnp.split(scatter_rows(back.astype(BF16), 0), 2, axis=1)
    grad_attended = made + attended_early(grad_proj_groups[-1])
    raw_blocks = raw.reshape(tensor, block, 3 * local)
    inner, grad_value, products, gain_parts = attend_back(
        shape, order, raw_blocks, *tables, query, key, value, logsum, grad_attended
    )
    if paired:
        (products, grad_proj_groups), *got[1:3] = lax.optimization_barrier(
            ((products, grad_proj_groups), *got[1:3])
        )
    output_part = sum(
        contract_rows(joined(right), left) for left, right in zip(moves.groups(attended), grad_proj_groups)
    )
    place = lax.axis_index("tensor") * local
    spread = lax.dynamic_update_slice(jnp.zeros((2, width), F32), gain_parts, (0, place))
    spread = jnp.concatenate([spread, attention_part[None], feedforward_part[None]], axis=0)
    packed = moves.add(jnp.concatenate([products.reshape(-1), spread.reshape(-1)]).reshape(-1, 256))
    if paired:
        packed, got[3] = lax.optimization_barrier((packed, got[3]))
    packed = packed.reshape(-1)
    products = as_arrived(packed[: 2 * length].reshape(tensor, 2, block)).T * (1.0 / width)
    gain_sums = add_rows(packed[2 * length :], rows)
    inner = inner.reshape(length, 2 * local)
    grad_qkv = [None, None, grad_value.reshape(length, local)]
    flat = as_arrived(sums).T
    for which in range(2):
        own = slice(which * local, (which + 1) * local)
        inverse = lax.rsqrt(flat[:, which : which + 1] * (1.0 / width) + norm_eps)
        unit = raw[:, own] * inverse
        grad_qkv[which] = (inverse * (inner[:, own] - unit * products[:, which : which + 1])).astype(BF16)
    grad_qkv = jnp.concatenate(grad_qkv, axis=1)
    qkv_part = contract_rows(hidden_all, grad_qkv)
    projections_part = jnp.concatenate([qkv_part, output_part], axis=1).astype(BF16)
    if paired:
        projections_part, got[4] = lax.optimization_barrier((projections_part, got[4]))
    grad_qkv, projections_part = lax.optimization_barrier((grad_qkv, projections_part))
    projections_grad = scatter_rows(projections_part, 0)

    def finish_gate_up(sent):
        nonlocal pair_middle_all, pair_gate_up
        values, _ = lax.optimization_barrier(((pair_middle_all, pair_gate_up, got[5]), sent))
        pair_middle_all, pair_gate_up, got[5] = values
        kept = kept_gate_up + gate_up_pair(me)
        gate_got, up_got = (jnp.concatenate(parts, axis=0).astype(F32) for parts in (got[2:4], got[4:]))
        return kept[:, :hidden_units] + gate_got, kept[:, hidden_units:] + up_got

    def finish_down(passing):
        nonlocal grad_mlp_groups, pair_grad_mlp_all
        values, _ = lax.optimization_barrier(((grad_mlp_groups, pair_grad_mlp_all), passing))
        grad_mlp_groups, pair_grad_mlp_all = values
        return (down_pieces(me) + jnp.concatenate(got[:2], axis=0).astype(F32)).T

    input_part, made, down_made = moves.scatter(
        halves_of(grad_qkv),
        lambda part: times_transposed(part, weight_qkv),
        finish_gate_up if paired else None,
        finish_down if paired else None,
    )
    input_grad = grad_middle + input_part
    if paired:
        (gate_grad, up_grad), down_grad = made, down_made
        results = input_grad, down_grad, gate_grad, up_grad
        gain_sums, results = lax.optimization_barrier((gain_sums, results))
        input_grad, down_grad, gate_grad, up_grad = results
        own, one, two, three = gain_sums
        gain_sums = (own + one) + (two + three)
    output_grad = projections_grad[:, 3 * local :].T
    summed = gain_sums.reshape(4, width)
    return (
        result,
        input_grad,
        projections_grad[:, :local],
        projections_grad[:, local : 2 * local],
        projections_grad[:, 2 * local : 3 * local],
        output_grad,
        gate_grad,
        up_grad,
        down_grad,
        summed[0],
        summed[1],
        summed[2],
        summed[3],
    )


def solution(mesh):
    in_specs = (
        P(("dp", "tensor"), None),
        P("dp", None),
        P(None, "tensor"),
        P(None, "tensor"),
        P(None, "tensor"),
        P("tensor", None),
        P(None, "tensor"),
        P(None, "tensor"),
        P("tensor", None),
        P("tensor"),
        P("tensor"),
        P(),
        P(),
        P(("dp", "tensor"), None),
    )
    out_specs = (
        P(("dp", "tensor"), None),
        P(("dp", "tensor"), None),
        P("dp", "tensor"),
        P("dp", "tensor"),
        P("dp", "tensor"),
        P("tensor", "dp"),
        P("dp", "tensor"),
        P("dp", "tensor"),
        P("tensor", "dp"),
        P(),
        P(),
        P(),
        P(),
    )
    sizes = {axis: mesh.shape[axis] for axis in ("dp", "tensor")}
    return jax.shard_map(
        functools.partial(body, sizes), mesh=mesh, in_specs=in_specs, out_specs=out_specs, check_vma=False
    )
```

time: 624 us -> 577 us (0.925)
  local copies, waits for them, and re-layouts: 85.9 us -> 59.8 us
  waiting for transfers between devices: 198 us -> 178 us
  other arithmetic: 49.5 us -> 57.9 us
    ppermute x0 -> x6, waiting for transfers between devices: none -> 31.2 us  [body(): got = [lax.ppermute(part, 'dp', in_pairs(1)) for part in away]]
    reduce_scatter x2 -> x1, waiting for transfers between devices: 44.9 us -> 17.1 us  [scatter_rows(): lax.psum_scatter(part, 'dp', scatter_dimension=dimension, tiled=True)]
    ppermute x2 -> x3, waiting for transfers between devices: 30.9 us -> 10.1 us  [to_pair(): return lax.ppermute(value, 'dp', in_pairs(2))]
    unnamed x350 -> x376, local copies, waits for them, and re-layouts: 64.3 us -> 51.9 us
    ppermute x50, starting transfers between devices: 44.5 us -> 37.3 us  [send(): return lax.ppermute(value, 'tensor', way)]
    convert_element_type x0 -> x6, other arithmetic: none -> 7 us  [the longest x4 6.97 us: scatter(): sent = (opposite.astype(BF16), first.astype(BF16))]
  transfers between devices with their start and end apart: 61 -> 65, of which waited for: 27 -> 25; matrix products, arithmetic and copies ran while one was open for 33% -> 33% of each run, Pallas kernels for 10% -> 10%
where the time goes in v2:
time: 577 us; the launch traced here: 569 us
  waiting for transfers between devices  178 us (31%)
  matrix products  136 us (24%)
  Pallas kernels  70.2 us (12%)
  local copies, waits for them, and re-layouts  59.8 us (10%)
  other arithmetic  57.9 us (10%)
  starting transfers between devices  50.9 us (9%)
  between operations  16.5 us (3%)
    ppermute x50, waiting for transfers between devices, send(): return lax.ppermute(value, 'tensor', way)  120 us
    dot_general x11, matrix products, times(): return jnp.dot(left, right, preferred_element_type=F32)  57.4 us
    unnamed x376, local copies, waits for them, and re-layouts  51.9 us
    dot_general x16, matrix products, contract_rows(): lax.dot_general(left, right, (((0,), (0,)), ((), ())), preferred_element_...  43.8 us
    ppermute x50, starting transfers between devices, send(): return lax.ppermute(value, 'tensor', way)  37.3 us
    dot_general x7, matrix products, times_transposed(): lax.dot_general(left, right, (((1,), (1,)), ((), ())), preferred_element_...  34.6 us
    pallas_call x4, Pallas kernels, feed_back(): pl.pallas_call(functools.partial(feed_back_kernel, count, with_activated)...  32.2 us
    ppermute x6, waiting for transfers between devices, body(): got = [lax.ppermute(part, 'dp', in_pairs(1)) for part in away]  31.2 us
  transfers between devices with their start and end apart: 65, of which 25 were waited for; matrix products, arithmetic and copies ran while one was open for 33% of the time, Pallas kernels for 10%

profile of v2, /device:TPU:0, one launch (start us, length us, event | category | flops | bytes accessed | tf_op | source)
XLA Modules:
  0.0 569.1 jit_solution(2781797532410027262)
XLA Ops:
  7.2 3.0 collective-permute-start
  11.8 3.7 fusion.99
  21.0 7.5 %collective-permute-done.refs_1_ = bf16[192,2048]{1,0:T(8,128)(2,1)} collective-permute-done((bf16[192,2048]{1,0:T(8,128)(2,1)}, bf16[192,2048]{1,0:T(8,128)(2,1)}, u32[]{:S(2)}, u32[]{:S(2)}) %collective-permute-start) | collective-permute-done | bytes 786464 | tf_op jit(solution)/shard_map/ppermute | solution.py:48
  32.8 4.6 fusion.55.refs_0_
  37.4 4.5 fusion.1.refs_1_
  46.2 3.8 fusion.59.refs_2_
  64.7 14.2 %shard_map.237 = (bf16[8,192,256]{2,1,0:T(8,128)(2,1)S(1)}, bf16[1536,256]{1,0:T(8,128)(2,1)S(1)}, bf16[1536,256]{1,0:T(8,128)(2,1)S(1)}, bf16[1536,256]{1,0:T(8,128)(2,1)S(1)}, f32[8,2,192]{2,1,0:T(2,128)S(1)}) custom-call(s32[8]{0:T(128)S(1)} %select_reduce_fusion.3.order, f32[384,768]{1,0:T(8,128)S(1)} %copy-done.48, f32[768,768]{1,0:T(8,128)S(1)} %fusion.1.refs_1_, ...), custom_call_target="tpu_custom_call" | custom-call | flops 4000000000 | bytes 10000000 | tf_op jit(solution)/shard_map/pallas_call | solution.py:342
  81.7 4.6 collective-permute-done.10
  88.1 10.9 %collective-permute-done.12 = bf16[192,2048]{1,0:T(8,128)(2,1)S(1)} collective-permute-done((bf16[192,2048]{1,0:T(8,128)(2,1)S(1)}, bf16[192,2048]{1,0:T(8,128)(2,1)S(1)}, u32[]{:S(2)}, u32[]{:S(2)}) %collective-permute-start.12) | collective-permute-done | bytes 786464 | tf_op jit(solution)/shard_map/ppermute | solution.py:48
  106.6 12.4 %collective-permute-done.13 = bf16[192,2048]{1,0:T(8,128)(2,1)S(1)} collective-permute-done((bf16[192,2048]{1,0:T(8,128)(2,1)S(1)}, bf16[192,2048]{1,0:T(8,128)(2,1)S(1)}, u32[]{:S(2)}, u32[]{:S(2)}) %collective-permute-start.13) | collective-permute-done | bytes 786464 | tf_op jit(solution)/shard_map/ppermute | solution.py:48
  127.4 13.0 %collective-permute-done.14.refs_1_ = bf16[192,2048]{1,0:T(8,128)(2,1)S(1)} collective-permute-done((bf16[192,2048]{1,0:T(8,128)(2,1)S(1)}, bf16[192,2048]{1,0:T(8,128)(2,1)S(1)}, u32[]{:S(2)}, u32[]{:S(2)}) %collective-permute-start.14) | collective-permute-done | bytes 786464 | tf_op jit(solution)/shard_map/ppermute | solution.py:48
  142.3 3.5 fusion.63.refs_3_
  148.9 6.7 %fusion.9.refs_5_ = f32[768,2048]{1,0:T(8,128)S(1)} fusion(bf16[2048,2048]{1,0:T(8,128)(2,1)S(1)} %constant_dynamic-update-slice_fusion.3, bf16[192,2048]{1,0:T(8,128)(2,1)S(1)} %collective-permute-done.19.refs_5_, bf16[192,2048]{1,0:T(8,128)(2,1)S(1)} %collective-permute-done.18.refs_4_, bf16[192,2048]{1,0:T(8,128)(2,1)S(1)} %collective-permute-done.14.refs_1_, ...), kind=kOutput, calls=%fused_computation.23 | convolution fusion | flops 6455033856 | bytes 17825792 | tf_op jit(solution)/shard_map/dot_general | solution.py:27
  158.4 4.2 collective-permute-done.20
  164.9 6.2 %fusion.67.refs_3_ = f32[384,2048]{1,0:T(8,128)S(1)} fusion(bf16[2048,2048]{1,0:T(8,128)(2,1)} %copy-done.126, bf16[192,2048]{1,0:T(8,128)(2,1)S(1)} %collective-permute-done.21.refs_7_, bf16[192,2048]{1,0:T(8,128)(2,1)S(1)} %collective-permute-done.15.refs_3_), kind=kOutput, calls=%fused_computation.94 | convolution fusion | flops 3224371200 | bytes 13107200 | tf_op jit(solution)/shard_map/dot_general | solution.py:27
  174.7 3.6 convolution_convert_fusion.5
  178.5 3.6 convolution_convert_fusion.6
  186.7 25.1 %collective-permute-done.24 = bf16[192,2048]{1,0:T(8,128)(2,1)S(1)} collective-permute-done((bf16[192,2048]{1,0:T(8,128)(2,1)S(1)}, bf16[192,2048]{1,0:T(8,128)(2,1)S(1)}, u32[]{:S(2)}, u32[]{:S(2)}) %collective-permute-start.24) | collective-permute-done | bytes 786464 | tf_op jit(solution)/shard_map/ppermute | solution.py:48
  212.3 17.9 %collective-permute-done.23 = bf16[192,2048]{1,0:T(8,128)(2,1)S(1)} collective-permute-done((bf16[192,2048]{1,0:T(8,128)(2,1)S(1)}, bf16[192,2048]{1,0:T(8,128)(2,1)S(1)}, u32[]{:S(2)}, u32[]{:S(2)}) %collective-permute-start.23) | collective-permute-done | bytes 786464 | tf_op jit(solution)/shard_map/ppermute | solution.py:48
  234.0 19.0 %convolution_convert_fusion.refs_2_ = bf16[1536,2048]{1,0:T(8,128)(2,1)} fusion(bf16[1536,2048]{1,0:T(8,128)(2,1)} %all-gather.3.cloned.1.call-done.refs_0_, bf16[2048,2048]{1,0:T(8,128)(2,1)} %copy-done.126), kind=kOutput, calls=%fused_computation | convolution fusion | flops 12888047616 | bytes 20971520 | tf_op jit(solution)/shard_map/dot_general | solution.py:27
  258.6 3.0 shard_map.239
  261.7 8.3 %shard_map.240 = (bf16[4,192,2048]{2,1,0:T(8,128)(2,1)S(1)}, bf16[4,192,2048]{2,1,0:T(8,128)(2,1)S(1)}) custom-call(bf16[192,2048]{1,0:T(8,128)(2,1)S(1)} %collective-permute-done.29.refs_0_.refs_8_, bf16[192,2048]{1,0:T(8,128)(2,1)S(1)} %collective-permute-done.26.refs_1_.refs_9_, ...), custom_call_target="tpu_custom_call", output_to_operand_aliasing={{0}: (6, {}), {1}: (7, {})} | custom-call | flops 3221225472 | bytes 16777216 | tf_op jit(solution)/shard_map/pallas_call | solution.py:464
  271.7 4.8 collective-permute-done.33
  293.3 10.3 %convolution_convert_fusion.1 = bf16[768,2048]{1,0:T(8,128)(2,1)} fusion(bf16[768,2048]{1,0:T(8,128)(2,1)S(1)} %bitcast.103, bf16[2048,2048]{1,0:T(8,128)(2,1)} %copy-done.126), kind=kOutput, calls=%fused_computation.4 | convolution fusion | flops 6444023808 | bytes 14680064 | tf_op jit(solution)/shard_map/dot_general | solution.py:23
  309.6 10.5 %convolution_convert_fusion.2 = bf16[768,2048]{1,0:T(8,128)(2,1)} fusion(bf16[768,2048]{1,0:T(8,128)(2,1)S(1)} %bitcast.106, bf16[2048,2048]{1,0:T(8,128)(2,1)} %copy-done.126), kind=kOutput, calls=%fused_computation.5 | convolution fusion | flops 6444023808 | bytes 14680064 | tf_op jit(solution)/shard_map/dot_general | solution.py:23
  320.1 3.5 add_convert_fusion.6
  328.8 3.2 fusion.146
  334.4 4.0 convolution_add_fusion.1
  341.6 3.8 fusion.151
  345.3 18.1 %shard_map.243 = (bf16[1536,1024]{1,0:T(8,128)(2,1)}, bf16[4,192,2048]{2,1,0:T(8,128)(2,1)}, bf16[4,192,2048]{2,1,0:T(8,128)(2,1)}) custom-call(bf16[1536,2048]{1,0:T(8,128)(2,1)} %all-gather.5.cloned.1.call-done.refs_0_.refs_1_.refs_8_, bf16[1024,2048]{1,0:T(8,128)(2,1)} %refs_1_.1, bf16[1536,2048]{1,0:T(8,128)(2,1)} %convolution_convert_fusion.refs_2_), custom_call_target="tpu_custom_call" | custom-call | flops 6442450944 | bytes 29360128 | tf_op jit(solution)/shard_map/pallas_call | solution.py:464
  363.6 3.6 multiply_reduce_fusion.1
  367.3 4.6 multiply_convert_fusion
  384.6 7.6 %collective-permute-done.39 = bf16[192,2048]{1,0:T(8,128)(2,1)S(1)} collective-permute-done((bf16[192,2048]{1,0:T(8,128)(2,1)S(1)}, bf16[192,2048]{1,0:T(8,128)(2,1)S(1)}, u32[]{:S(2)}, u32[]{:S(2)}) %collective-permute-start.39) | collective-permute-done | bytes 786464 | tf_op jit(solution)/shard_map/ppermute | solution.py:48
  393.0 4.0 convolution_add_fusion
  398.8 12.5 %collective-permute-done.45 = bf16[256,1024]{1,0:T(8,128)(2,1)S(1)} collective-permute-done((bf16[256,1024]{1,0:T(8,128)(2,1)S(1)}, bf16[256,1024]{1,0:T(8,128)(2,1)S(1)}, u32[]{:S(2)}, u32[]{:S(2)}) %collective-permute-start.45) | collective-permute-done | bytes 524320 | tf_op jit(solution)/shard_map/ppermute | solution.py:741
  417.9 19.0 %shard_map.246 = (f32[8,192,512]{2,1,0:T(8,128)S(1)}, bf16[8,192,256]{2,1,0:T(8,128)(2,1)S(1)}, f32[8,2,192]{2,1,0:T(2,128)S(1)}, f32[2,256]{1,0:T(2,128)S(1)}) custom-call(s32[8]{0:T(128)S(1)} %copy-done.90, f32[8,192,768]{2,1,0:T(8,128)S(1)} %bitcast.119, f32[8,2,192]{2,1,0:T(2,128)S(1)} %copy-done.84, f32[2,256]{1,0:T(2,128)S(1)} %copy-done.88, ...), custom_call_target="tpu_custom_call" | custom-call | flops 8000000000 | bytes 20000000 | tf_op jit(solution)/shard_map/pallas_call | solution.py:382
  450.9 3.6 fusion.50
  455.0 5.8 %convolution_convert_fusion.9 = bf16[2048,768]{0,1:T(8,128)(2,1)S(1)} fusion(bf16[1536,2048]{1,0:T(8,128)(2,1)S(1)} %bitcast.116, bf16[1536,256]{1,0:T(8,128)(2,1)S(1)} %bitcast.121, bf16[1536,256]{1,0:T(8,128)(2,1)S(1)} %get-tuple-element.364, bf16[1536,256]{1,0:T(8,128)(2,1)S(1)} %get-tuple-element.363), kind=kOutput, calls=%fused_computation.12 | convolution fusion | flops 4840488960 | bytes 11796480 | tf_op jit(solution)/shard_map/dot_general | solution.py:19
  465.0 6.1 %convolution_convert_fusion.3 = bf16[768,2048]{1,0:T(8,128)(2,1)} fusion(bf16[2048,768]{1,0:T(8,128)(2,1)} %constant_dynamic-update-slice_fusion, bf16[1536,768]{1,0:T(8,128)(2,1)S(1)} %copy-done.125), kind=kOutput, calls=%fused_computation.6 | convolution fusion | flops 2417491968 | bytes 7471104 | tf_op jit(solution)/shard_map/dot_general | solution.py:23
  476.2 5.4 convolution_convert_fusion.4
  485.3 18.7 %collective-permute-done.60 = bf16[256,1024]{1,0:T(8,128)(2,1)S(1)} collective-permute-done((bf16[256,1024]{1,0:T(8,128)(2,1)}, bf16[256,1024]{1,0:T(8,128)(2,1)S(1)}, u32[]{:S(2)}, u32[]{:S(2)}) %collective-permute-start.60) | collective-permute-done | bytes 524320 | tf_op jit(solution)/shard_map/ppermute | solution.py:741
  508.0 4.0 fusion.152
  512.0 3.8 add_add_fusion
  515.8 4.5 slice_add_fusion
  526.0 3.0 add_bitcast_fusion
  528.9 5.1 collective-permute-done.61
  534.1 3.1 add_add_fusion.1
  539.6 17.1 %reduce-scatter.2.cloned.1.call-done = bf16[512,1024]{0,1:T(8,128)(2,1)} async-done(((bf16[2048,1024]{0,1:T(8,128)(2,1)}), bf16[512,1024]{0,1:T(8,128)(2,1)}) %reduce-scatter.2.cloned.1.call-update) | async-done | bytes 1048592 | tf_op jit(solution)/shard_map/reduce_scatter | solution.py:135
  (607 shorter events, 180.1 us)
Async XLA Ops:
  7.2 225.1 %all-gather.3.cloned.1.call-start = ((), (), s32[]{:S(2)}) async-start(), calls=%async_computation.1 | async-start | bytes 7077888 | tf_op jit(solution)/shard_map/all_gather | solution.py:630
  7.2 21.2 %collective-permute-start = (bf16[192,2048]{1,0:T(8,128)(2,1)}, bf16[192,2048]{1,0:T(8,128)(2,1)}, u32[]{:S(2)}, u32[]{:S(2)}) collective-permute-start(bf16[192,2048]{1,0:T(8,128)(2,1)} %refs_2_.2), channel_id=1, source_target_pairs={{0,4},{1,3},{2,6},{3,1},{4,0},{5,7},{6,2},{7,5},{8,12},{9,11},{10,... | collective-permute-start | bytes 2359304 | tf_op jit(solution)/shard_map/ppermute | solution.py:48
  10.3 18.2 %collective-permute-start.3 = (bf16[192,2048]{1,0:T(8,128)(2,1)}, bf16[192,2048]{1,0:T(8,128)(2,1)S(1)}, u32[]{:S(2)}, u32[]{:S(2)}) collective-permute-start(bf16[192,2048]{1,0:T(8,128)(2,1)} %refs_2_.2), channel_id=1, source_target_pairs={{0,2},{1,5},{2,0},{3,7},{4,6},{5,1},{6,4},{7,3},{8,10},{9,13},{10,... | collective-permute-start | bytes 2359304 | tf_op jit(solution)/shard_map/ppermute | solution.py:48
  11.8 21.0 %collective-permute-start.2 = (bf16[192,2048]{1,0:T(8,128)(2,1)}, bf16[192,2048]{1,0:T(8,128)(2,1)S(1)}, u32[]{:S(2)}, u32[]{:S(2)}) collective-permute-start(bf16[192,2048]{1,0:T(8,128)(2,1)} %refs_2_.2), channel_id=1, source_target_pairs={{0,1},{1,0},{2,3},{3,2},{4,5},{5,4},{6,7},{7,6},{8,9},{9,8},{10,11... | collective-permute-start | bytes 2359304 | tf_op jit(solution)/shard_map/ppermute | solution.py:48
  28.5 8.9 %collective-permute-start.5 = (bf16[192,2048]{1,0:T(8,128)(2,1)}, bf16[192,2048]{1,0:T(8,128)(2,1)S(1)}, u32[]{:S(2)}, u32[]{:S(2)}) collective-permute-start(bf16[192,2048]{1,0:T(8,128)(2,1)} %collective-permute-done.refs_1_), channel_id=1, source_target_pairs={{0,1},{1,0},{2,3},{3,2},{4,5},{5,4},{6,7},{7,6},{8,9},{9,8},{10,11... | collective-permute-start | bytes 2359304 | tf_op jit(solution)/shard_map/ppermute | solution.py:48
  28.5 8.9 %collective-permute-start.4 = (bf16[192,2048]{1,0:T(8,128)(2,1)S(1)}, bf16[192,2048]{1,0:T(8,128)(2,1)S(1)}, u32[]{:S(2)}, u32[]{:S(2)}) collective-permute-start(bf16[192,2048]{1,0:T(8,128)(2,1)S(1)} %collective-permute-done.3.refs_0_), channel_id=1, source_target_pairs={{0,1},{1,0},{2,3},{3,2},{4,5},{5,4},{6,7},{7,6},{8,9},{9,8},{10,11... | collective-permute-start | bytes 2359304 | tf_op jit(solution)/shard_map/ppermute | solution.py:48
  31.3 12.3 %collective-permute-start.1 = (bf16[192,2048]{1,0:T(8,128)(2,1)}, bf16[192,2048]{1,0:T(8,128)(2,1)}, u32[]{:S(2)}, u32[]{:S(2)}) collective-permute-start(bf16[192,2048]{1,0:T(8,128)(2,1)} %collective-permute-done.refs_1_), channel_id=1, source_target_pairs={{0,2},{1,5},{2,0},{3,7},{4,6},{5,1},{6,4},{7,3},{8,10},{9,13},{10,... | collective-permute-start | bytes 2359304 | tf_op jit(solution)/shard_map/ppermute | solution.py:48
  87.0 12.1 %collective-permute-start.12 = (bf16[192,2048]{1,0:T(8,128)(2,1)S(1)}, bf16[192,2048]{1,0:T(8,128)(2,1)S(1)}, u32[]{:S(2)}, u32[]{:S(2)}) collective-permute-start(bf16[192,2048]{1,0:T(8,128)(2,1)S(1)} %get-tuple-element.372), channel_id=1, source_target_pairs={{0,2},{1,5},{2,0},{3,7},{4,6},{5,1},{6,4},{7,3},{8,10},{9,13},{10,... | collective-permute-start | bytes 2359304 | tf_op jit(solution)/shard_map/ppermute | solution.py:48
  99.4 19.6 %collective-permute-start.13 = (bf16[192,2048]{1,0:T(8,128)(2,1)S(1)}, bf16[192,2048]{1,0:T(8,128)(2,1)S(1)}, u32[]{:S(2)}, u32[]{:S(2)}) collective-permute-start(bf16[192,2048]{1,0:T(8,128)(2,1)S(1)} %add_convert_fusion.11), channel_id=1, source_target_pairs={{0,4},{1,3},{2,6},{3,1},{4,0},{5,7},{6,2},{7,5},{8,12},{9,11},{10,... | collective-permute-start | bytes 2359304 | tf_op jit(solution)/shard_map/ppermute | solution.py:48
  101.5 17.5 %collective-permute-start.11 = (bf16[192,2048]{1,0:T(8,128)(2,1)S(1)}, bf16[192,2048]{1,0:T(8,128)(2,1)S(1)}, u32[]{:S(2)}, u32[]{:S(2)}) collective-permute-start(bf16[192,2048]{1,0:T(8,128)(2,1)S(1)} %get-tuple-element.371), channel_id=1, source_target_pairs={{0,2},{1,5},{2,0},{3,7},{4,6},{5,1},{6,4},{7,3},{8,10},{9,13},{10,... | collective-permute-start | bytes 2359304 | tf_op jit(solution)/shard_map/ppermute | solution.py:48
  120.4 20.0 %collective-permute-start.14 = (bf16[192,2048]{1,0:T(8,128)(2,1)S(1)}, bf16[192,2048]{1,0:T(8,128)(2,1)S(1)}, u32[]{:S(2)}, u32[]{:S(2)}) collective-permute-start(bf16[192,2048]{1,0:T(8,128)(2,1)S(1)} %fusion.97.refs_2_), channel_id=1, source_target_pairs={{0,4},{1,3},{2,6},{3,1},{4,0},{5,7},{6,2},{7,5},{8,12},{9,11},{10,... | collective-permute-start | bytes 2359304 | tf_op jit(solution)/shard_map/ppermute | solution.py:48
  122.0 18.9 %collective-permute-start.17 = (bf16[192,2048]{1,0:T(8,128)(2,1)S(1)}, bf16[192,2048]{1,0:T(8,128)(2,1)S(1)}, u32[]{:S(2)}, u32[]{:S(2)}) collective-permute-start(bf16[192,2048]{1,0:T(8,128)(2,1)S(1)} %fusion.97.refs_2_), channel_id=1, source_target_pairs={{0,2},{1,5},{2,0},{3,7},{4,6},{5,1},{6,4},{7,3},{8,10},{9,13},{10,... | collective-permute-start | bytes 2359304 | tf_op jit(solution)/shard_map/ppermute | solution.py:48
  123.4 18.9 %collective-permute-start.16 = (bf16[192,2048]{1,0:T(8,128)(2,1)S(1)}, bf16[192,2048]{1,0:T(8,128)(2,1)S(1)}, u32[]{:S(2)}, u32[]{:S(2)}) collective-permute-start(bf16[192,2048]{1,0:T(8,128)(2,1)S(1)} %fusion.97.refs_2_), channel_id=1, source_target_pairs={{0,1},{1,0},{2,3},{3,2},{4,5},{5,4},{6,7},{7,6},{8,9},{9,8},{10,11... | collective-permute-start | bytes 2359304 | tf_op jit(solution)/shard_map/ppermute | solution.py:48
  124.7 37.9 %collective-permute-start.20 = (bf16[192,2048]{1,0:T(8,128)(2,1)S(1)}, bf16[192,2048]{1,0:T(8,128)(2,1)}, u32[]{:S(2)}, u32[]{:S(2)}) collective-permute-start(bf16[192,2048]{1,0:T(8,128)(2,1)S(1)} %fusion.97.refs_2_), channel_id=1, source_target_pairs={{0,16},{8,24},{16,0},{24,8},{1,17},{9,25},{17,1},{25,9},{2,18},{10... | collective-permute-start | bytes 2359304 | tf_op jit(solution)/shard_map/ppermute | solution.py:627
  140.3 8.6 %collective-permute-start.19 = (bf16[192,2048]{1,0:T(8,128)(2,1)S(1)}, bf16[192,2048]{1,0:T(8,128)(2,1)S(1)}, u32[]{:S(2)}, u32[]{:S(2)}) collective-permute-start(bf16[192,2048]{1,0:T(8,128)(2,1)S(1)} %collective-permute-done.14.refs_1_), channel_id=1, source_target_pairs={{0,1},{1,0},{2,3},{3,2},{4,5},{5,4},{6,7},{7,6},{8,9},{9,8},{10,11... | collective-permute-start | bytes 2359304 | tf_op jit(solution)/shard_map/ppermute | solution.py:48
  140.3 22.2 %collective-permute-start.15 = (bf16[192,2048]{1,0:T(8,128)(2,1)S(1)}, bf16[192,2048]{1,0:T(8,128)(2,1)S(1)}, u32[]{:S(2)}, u32[]{:S(2)}) collective-permute-start(bf16[192,2048]{1,0:T(8,128)(2,1)S(1)} %collective-permute-done.14.refs_1_), channel_id=1, source_target_pairs={{0,2},{1,5},{2,0},{3,7},{4,6},{5,1},{6,4},{7,3},{8,10},{9,13},{10,... | collective-permute-start | bytes 2359304 | tf_op jit(solution)/shard_map/ppermute | solution.py:48
  162.6 182.7 %all-gather.5.cloned.1.call-start = ((), (), s32[]{:S(2)}) async-start(), calls=%async_computation.2 | async-start | bytes 7077888 | tf_op jit(solution)/shard_map/all_gather | solution.py:630
  184.6 27.1 %collective-permute-start.24 = (bf16[192,2048]{1,0:T(8,128)(2,1)S(1)}, bf16[192,2048]{1,0:T(8,128)(2,1)S(1)}, u32[]{:S(2)}, u32[]{:S(2)}) collective-permute-start(bf16[192,2048]{1,0:T(8,128)(2,1)S(1)} %get-tuple-element.370), channel_id=1, source_target_pairs={{0,2},{1,5},{2,0},{3,7},{4,6},{5,1},{6,4},{7,3},{8,10},{9,13},{10,... | collective-permute-start | bytes 2359304 | tf_op jit(solution)/shard_map/ppermute | solution.py:48
  185.4 44.7 %collective-permute-start.23 = (bf16[192,2048]{1,0:T(8,128)(2,1)S(1)}, bf16[192,2048]{1,0:T(8,128)(2,1)S(1)}, u32[]{:S(2)}, u32[]{:S(2)}) collective-permute-start(bf16[192,2048]{1,0:T(8,128)(2,1)S(1)} %get-tuple-element.369), channel_id=1, source_target_pairs={{0,2},{1,5},{2,0},{3,7},{4,6},{5,1},{6,4},{7,3},{8,10},{9,13},{10,... | collective-permute-start | bytes 2359304 | tf_op jit(solution)/shard_map/ppermute | solution.py:48
  212.2 18.0 %collective-permute-start.25 = (bf16[192,2048]{1,0:T(8,128)(2,1)S(1)}, bf16[192,2048]{1,0:T(8,128)(2,1)S(1)}, u32[]{:S(2)}, u32[]{:S(2)}) collective-permute-start(bf16[192,2048]{1,0:T(8,128)(2,1)S(1)} %add_convert_fusion.8), channel_id=1, source_target_pairs={{0,4},{1,3},{2,6},{3,1},{4,0},{5,7},{6,2},{7,5},{8,12},{9,11},{10,... | collective-permute-start | bytes 2359304 | tf_op jit(solution)/shard_map/ppermute | solution.py:48
  232.3 25.1 %collective-permute-start.32 = (bf16[192,2048]{1,0:T(8,128)(2,1)S(1)}, bf16[192,2048]{1,0:T(8,128)(2,1)S(1)}, u32[]{:S(2)}, u32[]{:S(2)}) collective-permute-start(bf16[192,2048]{1,0:T(8,128)(2,1)S(1)} %fusion.41.refs_0_.refs_10_.refs_2_), channel_id=1, source_target_pairs={{0,1},{1,0},{2,3},{3,2},{4,5},{5,4},{6,7},{7,6},{8,9},{9,8},{10,11... | collective-permute-start | bytes 2359304 | tf_op jit(solution)/shard_map/ppermute | solution.py:48
  232.6 21.5 %collective-permute-start.26 = (bf16[192,2048]{1,0:T(8,128)(2,1)S(1)}, bf16[192,2048]{1,0:T(8,128)(2,1)S(1)}, u32[]{:S(2)}, u32[]{:S(2)}) collective-permute-start(bf16[192,2048]{1,0:T(8,128)(2,1)S(1)} %fusion.41.refs_0_.refs_10_.refs_2_), channel_id=1, source_target_pairs={{0,4},{1,3},{2,6},{3,1},{4,0},{5,7},{6,2},{7,5},{8,12},{9,11},{10,... | collective-permute-start | bytes 2359304 | tf_op jit(solution)/shard_map/ppermute | solution.py:48
  233.1 21.0 %collective-permute-start.29 = (bf16[192,2048]{1,0:T(8,128)(2,1)S(1)}, bf16[192,2048]{1,0:T(8,128)(2,1)S(1)}, u32[]{:S(2)}, u32[]{:S(2)}) collective-permute-start(bf16[192,2048]{1,0:T(8,128)(2,1)S(1)} %fusion.41.refs_0_.refs_10_.refs_2_), channel_id=1, source_target_pairs={{0,2},{1,5},{2,0},{3,7},{4,6},{5,1},{6,4},{7,3},{8,10},{9,13},{10,... | collective-permute-start | bytes 2359304 | tf_op jit(solution)/shard_map/ppermute | solution.py:48
  234.0 20.1 %collective-permute-start.27 = (bf16[192,1024]{1,0:T(8,128)(2,1)S(1)}, bf16[192,1024]{1,0:T(8,128)(2,1)S(1)}, u32[]{:S(2)}, u32[]{:S(2)}) collective-permute-start(bf16[192,1024]{1,0:T(8,128)(2,1)S(1)} %get-tuple-element.395), channel_id=1, source_target_pairs={{0,16},{8,24},{16,0},{24,8},{1,17},{9,25},{17,1},{25,9},{2,18},{10... | collective-permute-start | bytes 1179656 | tf_op jit(solution)/shard_map/ppermute | solution.py:627
  254.6 21.9 %collective-permute-start.28 = (bf16[192,2048]{1,0:T(8,128)(2,1)S(1)}, bf16[192,2048]{1,0:T(8,128)(2,1)S(1)}, u32[]{:S(2)}, u32[]{:S(2)}) collective-permute-start(bf16[192,2048]{1,0:T(8,128)(2,1)S(1)} %collective-permute-done.26.refs_1_.refs_9_), channel_id=1, source_target_pairs={{0,2},{1,5},{2,0},{3,7},{4,6},{5,1},{6,4},{7,3},{8,10},{9,13},{10,... | collective-permute-start | bytes 2359304 | tf_op jit(solution)/shard_map/ppermute | solution.py:48
  255.7 20.8 %collective-permute-start.33 = (bf16[192,1024]{1,0:T(8,128)(2,1)S(1)}, bf16[192,1024]{1,0:T(8,128)(2,1)S(1)}, u32[]{:S(2)}, u32[]{:S(2)}) collective-permute-start(bf16[192,1024]{1,0:T(8,128)(2,1)S(1)} %get-tuple-element.193), channel_id=1, source_target_pairs={{0,16},{8,24},{16,0},{24,8},{1,17},{9,25},{17,1},{25,9},{2,18},{10... | collective-permute-start | bytes 1179656 | tf_op jit(solution)/shard_map/ppermute | solution.py:627
  278.5 278.2 %reduce-scatter.2.cloned.1.call-start = ((), (), s32[]{:S(2)}) async-start(), calls=%async_computation.3 | async-start | bytes 5242880 | tf_op jit(solution)/shard_map/reduce_scatter | solution.py:135
  303.6 16.5 %collective-permute-start.35 = (bf16[768,2048]{1,0:T(8,128)(2,1)}, bf16[768,2048]{1,0:T(8,128)(2,1)}, u32[]{:S(2)}, u32[]{:S(2)}) collective-permute-start(bf16[768,2048]{1,0:T(8,128)(2,1)} %convolution_convert_fusion.1), channel_id=1, source_target_pairs={{0,1},{1,0},{2,3},{3,2},{4,5},{5,4},{6,7},{7,6},{8,9},{9,8},{10,11... | collective-permute-start | bytes 9437192 | tf_op jit(solution)/shard_map/ppermute | solution.py:48
  323.6 14.8 %collective-permute-start.36 = (bf16[192,2048]{1,0:T(8,128)(2,1)S(1)}, bf16[192,2048]{1,0:T(8,128)(2,1)S(1)}, u32[]{:S(2)}, u32[]{:S(2)}) collective-permute-start(bf16[192,2048]{1,0:T(8,128)(2,1)S(1)} %get-tuple-element.368), channel_id=1, source_target_pairs={{0,2},{1,5},{2,0},{3,7},{4,6},{5,1},{6,4},{7,3},{8,10},{9,13},{10,... | collective-permute-start | bytes 2359304 | tf_op jit(solution)/shard_map/ppermute | solution.py:48
  324.5 39.0 %collective-permute-start.38 = (bf16[192,2048]{1,0:T(8,128)(2,1)}, bf16[192,2048]{1,0:T(8,128)(2,1)}, u32[]{:S(2)}, u32[]{:S(2)}) collective-permute-start(bf16[192,2048]{1,0:T(8,128)(2,1)} %get-tuple-element.367), channel_id=1, source_target_pairs={{0,2},{1,5},{2,0},{3,7},{4,6},{5,1},{6,4},{7,3},{8,10},{9,13},{10,... | collective-permute-start | bytes 2359304 | tf_op jit(solution)/shard_map/ppermute | solution.py:48
  341.1 22.4 %collective-permute-start.37 = (bf16[192,2048]{1,0:T(8,128)(2,1)}, bf16[192,2048]{1,0:T(8,128)(2,1)}, u32[]{:S(2)}, u32[]{:S(2)}) collective-permute-start(bf16[192,2048]{1,0:T(8,128)(2,1)} %add_convert_fusion.5), channel_id=1, source_target_pairs={{0,4},{1,3},{2,6},{3,1},{4,0},{5,7},{6,2},{7,5},{8,12},{9,11},{10,... | collective-permute-start | bytes 2359304 | tf_op jit(solution)/shard_map/ppermute | solution.py:48
  371.8 20.4 %collective-permute-start.39 = (bf16[192,2048]{1,0:T(8,128)(2,1)S(1)}, bf16[192,2048]{1,0:T(8,128)(2,1)S(1)}, u32[]{:S(2)}, u32[]{:S(2)}) collective-permute-start(bf16[192,2048]{1,0:T(8,128)(2,1)S(1)} %get-tuple-element.254), channel_id=1, source_target_pairs={{0,4},{1,3},{2,6},{3,1},{4,0},{5,7},{6,2},{7,5},{8,12},{9,11},{10,... | collective-permute-start | bytes 2359304 | tf_op jit(solution)/shard_map/ppermute | solution.py:48
  373.4 19.5 %collective-permute-start.42 = (bf16[192,2048]{1,0:T(8,128)(2,1)S(1)}, bf16[192,2048]{1,0:T(8,128)(2,1)S(1)}, u32[]{:S(2)}, u32[]{:S(2)}) collective-permute-start(bf16[192,2048]{1,0:T(8,128)(2,1)S(1)} %get-tuple-element.254), channel_id=1, source_target_pairs={{0,2},{1,5},{2,0},{3,7},{4,6},{5,1},{6,4},{7,3},{8,10},{9,13},{10,... | collective-permute-start | bytes 2359304 | tf_op jit(solution)/shard_map/ppermute | solution.py:48
  374.3 22.6 %collective-permute-start.41 = (bf16[192,2048]{1,0:T(8,128)(2,1)S(1)}, bf16[192,2048]{1,0:T(8,128)(2,1)S(1)}, u32[]{:S(2)}, u32[]{:S(2)}) collective-permute-start(bf16[192,2048]{1,0:T(8,128)(2,1)S(1)} %get-tuple-element.254), channel_id=1, source_target_pairs={{0,1},{1,0},{2,3},{3,2},{4,5},{5,4},{6,7},{7,6},{8,9},{9,8},{10,11... | collective-permute-start | bytes 2359304 | tf_op jit(solution)/shard_map/ppermute | solution.py:48
  392.2 19.0 %collective-permute-start.40 = (bf16[192,2048]{1,0:T(8,128)(2,1)S(1)}, bf16[192,2048]{1,0:T(8,128)(2,1)S(1)}, u32[]{:S(2)}, u32[]{:S(2)}) collective-permute-start(bf16[192,2048]{1,0:T(8,128)(2,1)S(1)} %collective-permute-done.39), channel_id=1, source_target_pairs={{0,2},{1,5},{2,0},{3,7},{4,6},{5,1},{6,4},{7,3},{8,10},{9,13},{10,... | collective-permute-start | bytes 2359304 | tf_op jit(solution)/shard_map/ppermute | solution.py:48
  396.9 14.3 %collective-permute-start.45 = (bf16[256,1024]{1,0:T(8,128)(2,1)S(1)}, bf16[256,1024]{1,0:T(8,128)(2,1)S(1)}, u32[]{:S(2)}, u32[]{:S(2)}) collective-permute-start(bf16[256,1024]{1,0:T(8,128)(2,1)S(1)} %get-tuple-element.385), channel_id=1, source_target_pairs={{0,8},{8,0},{16,24},{24,16},{1,9},{9,1},{17,25},{25,17},{2,10},{10... | collective-permute-start | bytes 1572872 | tf_op jit(solution)/shard_map/ppermute | solution.py:741
  412.9 25.7 %collective-permute-start.48 = (bf16[256,1024]{1,0:T(8,128)(2,1)S(1)}, bf16[256,1024]{1,0:T(8,128)(2,1)S(1)}, u32[]{:S(2)}, u32[]{:S(2)}) collective-permute-start(bf16[256,1024]{1,0:T(8,128)(2,1)S(1)} %get-tuple-element.378), channel_id=1, source_target_pairs={{0,8},{8,0},{16,24},{24,16},{1,9},{9,1},{17,25},{25,17},{2,10},{10... | collective-permute-start | bytes 1572872 | tf_op jit(solution)/shard_map/ppermute | solution.py:741
  413.2 26.3 %collective-permute-start.47 = (bf16[256,1024]{1,0:T(8,128)(2,1)S(1)}, bf16[256,1024]{1,0:T(8,128)(2,1)}, u32[]{:S(2)}, u32[]{:S(2)}) collective-permute-start(bf16[256,1024]{1,0:T(8,128)(2,1)S(1)} %get-tuple-element.384), channel_id=1, source_target_pairs={{0,8},{8,0},{16,24},{24,16},{1,9},{9,1},{17,25},{25,17},{2,10},{10... | collective-permute-start | bytes 1572872 | tf_op jit(solution)/shard_map/ppermute | solution.py:741
  414.9 35.5 %collective-permute-start.52 = (bf16[256,1024]{1,0:T(8,128)(2,1)}, bf16[256,1024]{1,0:T(8,128)(2,1)S(1)}, u32[]{:S(2)}, u32[]{:S(2)}) collective-permute-start(bf16[256,1024]{1,0:T(8,128)(2,1)} %get-tuple-element.377), channel_id=1, source_target_pairs={{0,8},{8,0},{16,24},{24,16},{1,9},{9,1},{17,25},{25,17},{2,10},{10... | collective-permute-start | bytes 1572872 | tf_op jit(solution)/shard_map/ppermute | solution.py:741
  415.2 49.5 %collective-permute-start.56 = (bf16[256,1024]{1,0:T(8,128)(2,1)}, bf16[256,1024]{1,0:T(8,128)(2,1)}, u32[]{:S(2)}, u32[]{:S(2)}) collective-permute-start(bf16[256,1024]{1,0:T(8,128)(2,1)} %get-tuple-element.376), channel_id=1, source_target_pairs={{0,8},{8,0},{16,24},{24,16},{1,9},{9,1},{17,25},{25,17},{2,10},{10... | collective-permute-start | bytes 1572872 | tf_op jit(solution)/shard_map/ppermute | solution.py:741
  471.1 10.5 %collective-permute-start.57 = (bf16[768,2048]{1,0:T(8,128)(2,1)}, bf16[768,2048]{1,0:T(8,128)(2,1)S(1)}, u32[]{:S(2)}, u32[]{:S(2)}) collective-permute-start(bf16[768,2048]{1,0:T(8,128)(2,1)} %convolution_convert_fusion.3), channel_id=1, source_target_pairs={{0,1},{1,0},{2,3},{3,2},{4,5},{5,4},{6,7},{7,6},{8,9},{9,8},{10,11... | collective-permute-start | bytes 9437192 | tf_op jit(solution)/shard_map/ppermute | solution.py:48
  471.2 32.8 %collective-permute-start.60 = (bf16[256,1024]{1,0:T(8,128)(2,1)}, bf16[256,1024]{1,0:T(8,128)(2,1)S(1)}, u32[]{:S(2)}, u32[]{:S(2)}) collective-permute-start(bf16[256,1024]{1,0:T(8,128)(2,1)} %get-tuple-element.375), channel_id=1, source_target_pairs={{0,8},{8,0},{16,24},{24,16},{1,9},{9,1},{17,25},{25,17},{2,10},{10... | collective-permute-start | bytes 1572872 | tf_op jit(solution)/shard_map/ppermute | solution.py:741
  471.6 65.6 %collective-permute-start.53 = (f32[8192]{0:T(1024)S(1)}, f32[8192]{0:T(1024)S(1)}, u32[]{:S(2)}, u32[]{:S(2)}) collective-permute-start(f32[8192]{0:T(1024)S(1)} %bitcast.130), channel_id=1, source_target_pairs={{0,8},{8,0},{16,24},{24,16},{1,9},{9,1},{17,25},{25,17},{2,10},{10... | collective-permute-start | bytes 98312 | tf_op jit(solution)/shard_map/ppermute | solution.py:159
  473.4 63.8 %collective-permute-start.54 = (f32[8192]{0:T(1024)S(1)}, f32[8192]{0:T(1024)S(1)}, u32[]{:S(2)}, u32[]{:S(2)}) collective-permute-start(f32[8192]{0:T(1024)S(1)} %bitcast.131), channel_id=1, source_target_pairs={{0,16},{8,24},{16,0},{24,8},{1,17},{9,25},{17,1},{25,9},{2,18},{10... | collective-permute-start | bytes 98312 | tf_op jit(solution)/shard_map/ppermute | solution.py:159
  475.0 62.2 %collective-permute-start.55 = (f32[8192]{0:T(1024)S(1)}, f32[8192]{0:T(1024)S(1)}, u32[]{:S(2)}, u32[]{:S(2)}) collective-permute-start(f32[8192]{0:T(1024)S(1)} %bitcast.132), channel_id=1, source_target_pairs={{0,24},{8,16},{16,8},{24,0},{1,25},{9,17},{17,9},{25,1},{2,26},{10... | collective-permute-start | bytes 98312 | tf_op jit(solution)/shard_map/ppermute | solution.py:159
  483.9 36.4 %collective-permute-start.59 = (bf16[192,2048]{1,0:T(8,128)(2,1)}, bf16[192,2048]{1,0:T(8,128)(2,1)}, u32[]{:S(2)}, u32[]{:S(2)}) collective-permute-start(bf16[192,2048]{1,0:T(8,128)(2,1)} %get-tuple-element.366), channel_id=1, source_target_pairs={{0,2},{1,5},{2,0},{3,7},{4,6},{5,1},{6,4},{7,3},{8,10},{9,13},{10,... | collective-permute-start | bytes 2359304 | tf_op jit(solution)/shard_map/ppermute | solution.py:48
  504.0 30.0 %collective-permute-start.58 = (bf16[192,2048]{1,0:T(8,128)(2,1)}, bf16[192,2048]{1,0:T(8,128)(2,1)}, u32[]{:S(2)}, u32[]{:S(2)}) collective-permute-start(bf16[192,2048]{1,0:T(8,128)(2,1)} %get-tuple-element.365), channel_id=1, source_target_pairs={{0,2},{1,5},{2,0},{3,7},{4,6},{5,1},{6,4},{7,3},{8,10},{9,13},{10,... | collective-permute-start | bytes 2359304 | tf_op jit(solution)/shard_map/ppermute | solution.py:48
  522.0 12.1 %collective-permute-start.61 = (bf16[192,2048]{1,0:T(8,128)(2,1)S(1)}, bf16[192,2048]{1,0:T(8,128)(2,1)S(1)}, u32[]{:S(2)}, u32[]{:S(2)}) collective-permute-start(bf16[192,2048]{1,0:T(8,128)(2,1)S(1)} %add_convert_fusion.2), channel_id=1, source_target_pairs={{0,4},{1,3},{2,6},{3,1},{4,0},{5,7},{6,2},{7,5},{8,12},{9,11},{10,... | collective-permute-start | bytes 2359304 | tf_op jit(solution)/shard_map/ppermute | solution.py:48
  (195 other events, 1521.3 us)
Sparse Core Ops, SparseCore 0:
  162.7 53.9 all-gather.2
  278.6 44.3 all-gather.4
  471.3 85.3 reduce-scatter.1

commit v3 on v2

--- a/solution.py
+++ b/solution.py
@@ -132,7 +132,7 @@
 
 
 def scatter_rows(part, dimension):
-    return lax.psum_scatter(part, "dp", scatter_dimension=dimension, tiled=True).astype(F32)
+    return lax.psum_scatter(part, "dp", scatter_dimension=dimension, tiled=True)
 
 
 def halve_rows(part, dimension):
@@ -447,7 +447,7 @@
             out[:, :, pl.ds(at, tile)] = own.reshape(out.shape[:2] + (tile,))
 
 
-def feed_back(grads, down_weight, both, slot, slots, before=(), with_activated=False):
+def feed_back(grads, down_weight, both, slot, slots, before=(), with_activated=False, limit=None):
     count, width = len(grads), grads[0].shape[1]
     units, tile = down_weight.shape[0], min(TILE, down_weight.shape[0])
     tiles, rows = units // tile, sum(grad.shape[0] for grad in grads)
@@ -469,7 +469,7 @@
         out_specs=extra_spec + (pl.BlockSpec((slots, part, 2 * units), lambda j: (slot // slots, 0, 0)),) * 2,
         scratch_shapes=[pltpu.VMEM((rows, width), BF16)],
         input_output_aliases={count + 2 + at: at for at in range(len(before))},
-        compiler_params=pltpu.CompilerParams(vmem_limit_bytes=(8 + 7 * rows // 192) * 2**20),
+        compiler_params=pltpu.CompilerParams(vmem_limit_bytes=(limit or 8 + 7 * rows // 192) * 2**20),
         cost_estimate=pl.CostEstimate(
             flops=2 * rows * width * units,
             bytes_accessed=2 * units * width + 12 * rows * units + 2 * rows * width,
@@ -667,7 +667,7 @@
     grad_mlp_groups, (pair_both, first_half), made = moves.gather(grad_mlp, meanwhile, back_early)
     if tensor == 8:
         made, second_half = made
-        grad_gate_up = feed_back(grad_mlp_groups[-1], down_weight, both_groups[2], 3, 1, made)
+        grad_gate_up = feed_back(grad_mlp_groups[-1], down_weight, both_groups[2], 3, 1, made, limit=60)
         grad_gate_up = [half.reshape(length // 2, 2 * hidden_units) for half in grad_gate_up]
     else:
         grad_act = times_transposed(grad_mlp_groups[0][0], down_weight)
@@ -745,25 +745,25 @@
 
     def proj_early(*groups):
         if not paired:
-            return attended_early(*groups), None, None
-        return attended_early(*groups), got[0], gate_up_own(me)
+            return attended_early(*groups), None
+        return attended_early(*groups), gate_up_own(me)
 
     grad_proj_groups, away, made = moves.gather(grad_proj, away, proj_early)
     made, *rest = made or ([],)
     if paired:
-        got[0], kept_gate_up = rest
+        (kept_gate_up,) = rest
     else:
-        down_grad = scatter_rows(contract_rows(activated, row_of(grad_mlp_groups)).astype(BF16), 1)
+        down_grad = scatter_rows(contract_rows(activated, row_of(grad_mlp_groups)).astype(BF16), 1).astype(F32)
         back = contract_rows(row_of(middle_groups), jnp.concatenate(grad_gate_up, axis=0))
-        gate_grad, up_grad = jnp.split(scatter_rows(back.astype(BF16), 0), 2, axis=1)
+        gate_grad, up_grad = jnp.split(scatter_rows(back.astype(BF16), 0).astype(F32), 2, axis=1)
     grad_attended = made + attended_early(grad_proj_groups[-1])
     raw_blocks = raw.reshape(tensor, block, 3 * local)
     inner, grad_value, products, gain_parts = attend_back(
         shape, order, raw_blocks, *tables, query, key, value, logsum, grad_attended
     )
     if paired:
-        (products, grad_proj_groups), *got[1:3] = lax.optimization_barrier(
-            ((products, grad_proj_groups), *got[1:3])
+        (products, grad_proj_groups), *got[:2] = lax.optimization_barrier(
+            ((products, grad_proj_groups), *got[:2])
         )
     output_part = sum(
         contract_rows(joined(right), left) for left, right in zip(moves.groups(attended), grad_proj_groups)
@@ -773,7 +773,7 @@
     spread = jnp.concatenate([spread, attention_part[None], feedforward_part[None]], axis=0)
     packed = moves.add(jnp.concatenate([products.reshape(-1), spread.reshape(-1)]).reshape(-1, 256))
     if paired:
-        packed, got[3] = lax.optimization_barrier((packed, got[3]))
+        packed, got[2] = lax.optimization_barrier((packed, got[2]))
     packed = packed.reshape(-1)
     products = as_arrived(packed[: 2 * length].reshape(tensor, 2, block)).T * (1.0 / width)
     gain_sums = add_rows(packed[2 * length :], rows)
@@ -786,20 +786,20 @@
         unit = raw[:, own] * inverse
         grad_qkv[which] = (inverse * (inner[:, own] - unit * products[:, which : which + 1])).astype(BF16)
     grad_qkv = jnp.concatenate(grad_qkv, axis=1)
-    qkv_part = contract_rows(hidden_all, grad_qkv)
-    projections_part = jnp.concatenate([qkv_part, output_part], axis=1).astype(BF16)
-    if paired:
-        projections_part, got[4] = lax.optimization_barrier((projections_part, got[4]))
+    qkv_part = contract_rows(hidden_all, grad_qkv).astype(BF16)
+    projections_part = jnp.concatenate([qkv_part, output_part.astype(BF16)], axis=1)
+    if paired:
+        projections_part, *got[3:5] = lax.optimization_barrier((projections_part, *got[3:5]))
     grad_qkv, projections_part = lax.optimization_barrier((grad_qkv, projections_part))
     projections_grad = scatter_rows(projections_part, 0)
 
-    def finish_gate_up(sent):
+    def finish_gate(sent):
         nonlocal pair_middle_all, pair_gate_up
-        values, _ = lax.optimization_barrier(((pair_middle_all, pair_gate_up, got[5]), sent))
-        pair_middle_all, pair_gate_up, got[5] = values
+        values, _ = lax.optimization_barrier(((pair_middle_all, pair_gate_up), sent))
+        pair_middle_all, pair_gate_up = values
         kept = kept_gate_up + gate_up_pair(me)
-        gate_got, up_got = (jnp.concatenate(parts, axis=0).astype(F32) for parts in (got[2:4], got[4:]))
-        return kept[:, :hidden_units] + gate_got, kept[:, hidden_units:] + up_got
+        gate_got = jnp.concatenate(got[2:4], axis=0).astype(F32)
+        return kept[:, :hidden_units] + gate_got, kept[:, hidden_units:]
 
     def finish_down(passing):
         nonlocal grad_mlp_groups, pair_grad_mlp_all
@@ -810,25 +810,29 @@
     input_part, made, down_made = moves.scatter(
         halves_of(grad_qkv),
         lambda part: times_transposed(part, weight_qkv),
-        finish_gate_up if paired else None,
+        finish_gate if paired else None,
         finish_down if paired else None,
     )
     input_grad = grad_middle + input_part
     if paired:
-        (gate_grad, up_grad), down_grad = made, down_made
+        (gate_grad, up_kept), down_grad = made, down_made
+        up_grad = up_kept + jnp.concatenate(got[4:], axis=0).astype(F32)
         results = input_grad, down_grad, gate_grad, up_grad
         gain_sums, results = lax.optimization_barrier((gain_sums, results))
         input_grad, down_grad, gate_grad, up_grad = results
         own, one, two, three = gain_sums
         gain_sums = (own + one) + (two + three)
-    output_grad = projections_grad[:, 3 * local :].T
+    query_grad, key_grad, value_grad, output_grad = (
+        projections_grad[:, at * local : (at + 1) * local].astype(F32) for at in range(4)
+    )
+    output_grad = output_grad.T
     summed = gain_sums.reshape(4, width)
     return (
         result,
         input_grad,
-        projections_grad[:, :local],
-        projections_grad[:, local : 2 * local],
-        projections_grad[:, 2 * local : 3 * local],
+        query_grad,
+        key_grad,
+        value_grad,
         output_grad,
         gate_grad,
         up_grad,

time: 577 us -> 573 us (level)
  local copies, waits for them, and re-layouts: 59.8 us -> 51.6 us
  waiting for transfers between devices: 178 us -> 172 us
    ppermute x6, waiting for transfers between devices: 31.2 us -> 7.64 us  [body(): got = [lax.ppermute(part, 'dp', in_pairs(1)) for part in away]]
    reduce_scatter x1, waiting for transfers between devices: 17.1 us -> 33 us  [scatter_rows(): return lax.psum_scatter(part, 'dp', scatter_dimension=dimension, tiled=True)]
    unnamed x376 -> x364, local copies, waits for them, and re-layouts: 51.9 us -> 44.5 us
  transfers between devices with their start and end apart: 65 -> 65, of which waited for: 25 -> 25; matrix products, arithmetic and copies ran while one was open for 33% -> 34% of each run, Pallas kernels for 10% -> 11%
where the time goes in v3:
time: 573 us; the launch traced here: 565 us
  waiting for transfers between devices  172 us (30%)
  matrix products  140 us (24%)
  Pallas kernels  75 us (13%)
  other arithmetic  59.9 us (10%)
  local copies, waits for them, and re-layouts  51.6 us (9%)
  starting transfers between devices  50.2 us (9%)
  between operations  16.5 us (3%)
    ppermute x50, waiting for transfers between devices, send(): return lax.ppermute(value, 'tensor', way)  121 us
    dot_general x11, matrix products, times(): return jnp.dot(left, right, preferred_element_type=F32)  57.4 us
    unnamed x364, local copies, waits for them, and re-layouts  44.5 us
    dot_general x16, matrix products, contract_rows(): lax.dot_general(left, right, (((0,), (0,)), ((), ())), preferred_element_...  43.7 us
    dot_general x7, matrix products, times_transposed(): lax.dot_general(left, right, (((1,), (1,)), ((), ())), preferred_element_...  39.1 us
    pallas_call x4, Pallas kernels, feed_back(): pl.pallas_call(functools.partial(feed_back_kernel, count, with_activated)...  36.9 us
    ppermute x50, starting transfers between devices, send(): return lax.ppermute(value, 'tensor', way)  36.7 us
    reduce_scatter x1, waiting for transfers between devices, scatter_rows(): return lax.psum_scatter(part, 'dp', scatter_dimension=dimension, tiled=True)  33 us
  transfers between devices with their start and end apart: 65, of which 25 were waited for; matrix products, arithmetic and copies ran while one was open for 34% of the time, Pallas kernels for 11%

profile of v3, /device:TPU:0, one launch (start us, length us, event | category | flops | bytes accessed | tf_op | source)
XLA Modules:
  0.0 564.9 jit_solution(1345374061970918805)
XLA Ops:
  7.2 3.0 collective-permute-start
  11.8 3.7 fusion.99
  21.0 7.5 %collective-permute-done.refs_1_ = bf16[192,2048]{1,0:T(8,128)(2,1)} collective-permute-done((bf16[192,2048]{1,0:T(8,128)(2,1)}, bf16[192,2048]{1,0:T(8,128)(2,1)}, u32[]{:S(2)}, u32[]{:S(2)}) %collective-permute-start) | collective-permute-done | bytes 786464 | tf_op jit(solution)/shard_map/ppermute | solution.py:48
  32.8 4.6 fusion.55.refs_0_
  37.5 4.5 fusion.1.refs_1_
  46.3 3.7 fusion.59.refs_2_
  64.8 14.2 %shard_map.237 = (bf16[8,192,256]{2,1,0:T(8,128)(2,1)S(1)}, bf16[1536,256]{1,0:T(8,128)(2,1)S(1)}, bf16[1536,256]{1,0:T(8,128)(2,1)S(1)}, bf16[1536,256]{1,0:T(8,128)(2,1)S(1)}, f32[8,2,192]{2,1,0:T(2,128)S(1)}) custom-call(s32[8]{0:T(128)S(1)} %select_reduce_fusion.3.order, f32[384,768]{1,0:T(8,128)S(1)} %copy-done.43, f32[768,768]{1,0:T(8,128)S(1)} %fusion.1.refs_1_, ...), custom_call_target="tpu_custom_call" | custom-call | flops 4000000000 | bytes 10000000 | tf_op jit(solution)/shard_map/pallas_call | solution.py:342
  81.7 4.6 collective-permute-done.10
  88.1 11.0 %collective-permute-done.12 = bf16[192,2048]{1,0:T(8,128)(2,1)S(1)} collective-permute-done((bf16[192,2048]{1,0:T(8,128)(2,1)S(1)}, bf16[192,2048]{1,0:T(8,128)(2,1)S(1)}, u32[]{:S(2)}, u32[]{:S(2)}) %collective-permute-start.12) | collective-permute-done | bytes 786464 | tf_op jit(solution)/shard_map/ppermute | solution.py:48
  106.7 12.4 %collective-permute-done.13 = bf16[192,2048]{1,0:T(8,128)(2,1)S(1)} collective-permute-done((bf16[192,2048]{1,0:T(8,128)(2,1)S(1)}, bf16[192,2048]{1,0:T(8,128)(2,1)S(1)}, u32[]{:S(2)}, u32[]{:S(2)}) %collective-permute-start.13) | collective-permute-done | bytes 786464 | tf_op jit(solution)/shard_map/ppermute | solution.py:48
  127.4 13.0 %collective-permute-done.14.refs_1_ = bf16[192,2048]{1,0:T(8,128)(2,1)S(1)} collective-permute-done((bf16[192,2048]{1,0:T(8,128)(2,1)S(1)}, bf16[192,2048]{1,0:T(8,128)(2,1)S(1)}, u32[]{:S(2)}, u32[]{:S(2)}) %collective-permute-start.14) | collective-permute-done | bytes 786464 | tf_op jit(solution)/shard_map/ppermute | solution.py:48
  142.4 3.5 fusion.63.refs_3_
  149.0 6.7 %fusion.9.refs_5_ = f32[768,2048]{1,0:T(8,128)S(1)} fusion(bf16[2048,2048]{1,0:T(8,128)(2,1)S(1)} %constant_dynamic-update-slice_fusion.3, bf16[192,2048]{1,0:T(8,128)(2,1)S(1)} %collective-permute-done.19.refs_5_, bf16[192,2048]{1,0:T(8,128)(2,1)S(1)} %collective-permute-done.18.refs_4_, bf16[192,2048]{1,0:T(8,128)(2,1)S(1)} %collective-permute-done.14.refs_1_, ...), kind=kOutput, calls=%fused_computation.23 | convolution fusion | flops 6455033856 | bytes 17825792 | tf_op jit(solution)/shard_map/dot_general | solution.py:27
  158.4 4.2 collective-permute-done.20
  164.9 6.2 %fusion.67.refs_3_ = f32[384,2048]{1,0:T(8,128)S(1)} fusion(bf16[2048,2048]{1,0:T(8,128)(2,1)} %copy-done.122, bf16[192,2048]{1,0:T(8,128)(2,1)S(1)} %collective-permute-done.21.refs_7_, bf16[192,2048]{1,0:T(8,128)(2,1)S(1)} %collective-permute-done.15.refs_3_), kind=kOutput, calls=%fused_computation.94 | convolution fusion | flops 3224371200 | bytes 13107200 | tf_op jit(solution)/shard_map/dot_general | solution.py:27
  174.7 3.6 convolution_convert_fusion.5
  178.5 3.6 convolution_convert_fusion.6
  186.7 25.1 %collective-permute-done.24 = bf16[192,2048]{1,0:T(8,128)(2,1)S(1)} collective-permute-done((bf16[192,2048]{1,0:T(8,128)(2,1)S(1)}, bf16[192,2048]{1,0:T(8,128)(2,1)S(1)}, u32[]{:S(2)}, u32[]{:S(2)}) %collective-permute-start.24) | collective-permute-done | bytes 786464 | tf_op jit(solution)/shard_map/ppermute | solution.py:48
  212.3 17.9 %collective-permute-done.23 = bf16[192,2048]{1,0:T(8,128)(2,1)S(1)} collective-permute-done((bf16[192,2048]{1,0:T(8,128)(2,1)S(1)}, bf16[192,2048]{1,0:T(8,128)(2,1)S(1)}, u32[]{:S(2)}, u32[]{:S(2)}) %collective-permute-start.23) | collective-permute-done | bytes 786464 | tf_op jit(solution)/shard_map/ppermute | solution.py:48
  234.0 19.0 %convolution_convert_fusion.refs_2_ = bf16[1536,2048]{1,0:T(8,128)(2,1)} fusion(bf16[1536,2048]{1,0:T(8,128)(2,1)} %all-gather.3.cloned.1.call-done.refs_0_, bf16[2048,2048]{1,0:T(8,128)(2,1)} %copy-done.122), kind=kOutput, calls=%fused_computation | convolution fusion | flops 12888047616 | bytes 20971520 | tf_op jit(solution)/shard_map/dot_general | solution.py:27
  257.5 3.0 shard_map.239
  260.6 8.3 %shard_map.240 = (bf16[4,192,2048]{2,1,0:T(8,128)(2,1)S(1)}, bf16[4,192,2048]{2,1,0:T(8,128)(2,1)S(1)}) custom-call(bf16[192,2048]{1,0:T(8,128)(2,1)S(1)} %collective-permute-done.29.refs_0_.refs_8_, bf16[192,2048]{1,0:T(8,128)(2,1)S(1)} %collective-permute-done.26.refs_1_.refs_9_, ...), custom_call_target="tpu_custom_call", output_to_operand_aliasing={{0}: (6, {}), {1}: (7, {})} | custom-call | flops 3221225472 | bytes 16777216 | tf_op jit(solution)/shard_map/pallas_call | solution.py:464
  272.4 4.2 collective-permute-done.33
  281.0 7.5 %shard_map.241 = (bf16[4,192,2048]{2,1,0:T(8,128)(2,1)}, bf16[4,192,2048]{2,1,0:T(8,128)(2,1)}) custom-call(bf16[192,2048]{1,0:T(8,128)(2,1)} %copy-done.32, bf16[192,2048]{1,0:T(8,128)(2,1)} %copy-done.35, bf16[1024,2048]{1,0:T(8,128)(2,1)} %refs_1_.1, f32[384,2048]{1,0:T(8,128)} %copy-done.108, ...), custom_call_target="tpu_custom_call", output_to_operand_aliasing={{0}: (4, {}), {1}: (5, {})} | custom-call | flops 1610612736 | bytes 10485760 | tf_op jit(solution)/shard_map/pallas_call | solution.py:464
  288.5 11.9 %convolution_convert_fusion.1 = bf16[768,2048]{1,0:T(8,128)(2,1)} fusion(bf16[768,2048]{1,0:T(8,128)(2,1)} %bitcast.103, bf16[2048,2048]{1,0:T(8,128)(2,1)} %copy-done.122), kind=kOutput, calls=%fused_computation.4 | convolution fusion | flops 6444023808 | bytes 14680064 | tf_op jit(solution)/shard_map/dot_general | solution.py:23
  307.1 10.6 %convolution_convert_fusion.2 = bf16[768,2048]{1,0:T(8,128)(2,1)} fusion(bf16[768,2048]{1,0:T(8,128)(2,1)S(1)} %bitcast.106, bf16[2048,2048]{1,0:T(8,128)(2,1)} %copy-done.122), kind=kOutput, calls=%fused_computation.5 | convolution fusion | flops 6444023808 | bytes 14680064 | tf_op jit(solution)/shard_map/dot_general | solution.py:23
  317.8 3.5 add_convert_fusion.6
  325.3 3.2 fusion.146
  331.0 4.0 convolution_add_fusion.1
  337.6 3.9 fusion.151
  341.5 18.1 %shard_map.243 = (bf16[1536,1024]{1,0:T(8,128)(2,1)}, bf16[4,192,2048]{2,1,0:T(8,128)(2,1)}, bf16[4,192,2048]{2,1,0:T(8,128)(2,1)}) custom-call(bf16[1536,2048]{1,0:T(8,128)(2,1)} %all-gather.5.cloned.1.call-done.refs_0_.refs_1_.refs_8_, bf16[1024,2048]{1,0:T(8,128)(2,1)} %refs_1_.1, bf16[1536,2048]{1,0:T(8,128)(2,1)} %convolution_convert_fusion.refs_2_), custom_call_target="tpu_custom_call" | custom-call | flops 6442450944 | bytes 29360128 | tf_op jit(solution)/shard_map/pallas_call | solution.py:464
  359.7 3.6 multiply_reduce_fusion.1
  363.4 4.6 multiply_convert_fusion
  380.7 7.3 %collective-permute-done.39 = bf16[192,2048]{1,0:T(8,128)(2,1)S(1)} collective-permute-done((bf16[192,2048]{1,0:T(8,128)(2,1)S(1)}, bf16[192,2048]{1,0:T(8,128)(2,1)S(1)}, u32[]{:S(2)}, u32[]{:S(2)}) %collective-permute-start.39) | collective-permute-done | bytes 786464 | tf_op jit(solution)/shard_map/ppermute | solution.py:48
  389.3 3.9 convolution_add_fusion
  395.2 2.8 fusion.86.refs_1_
  406.2 19.0 %shard_map.246 = (f32[8,192,512]{2,1,0:T(8,128)S(1)}, bf16[8,192,256]{2,1,0:T(8,128)(2,1)S(1)}, f32[8,2,192]{2,1,0:T(2,128)S(1)}, f32[2,256]{1,0:T(2,128)S(1)}) custom-call(s32[8]{0:T(128)S(1)} %copy-done.86, f32[8,192,768]{2,1,0:T(8,128)S(1)} %bitcast.119, f32[8,2,192]{2,1,0:T(2,128)S(1)} %copy-done.80, f32[2,256]{1,0:T(2,128)S(1)} %copy-done.84, ...), custom_call_target="tpu_custom_call" | custom-call | flops 8000000000 | bytes 20000000 | tf_op jit(solution)/shard_map/pallas_call | solution.py:382
  439.0 3.6 fusion.50
  443.0 5.8 %convolution_convert_fusion.9 = bf16[2048,768]{0,1:T(8,128)(2,1)S(1)} fusion(bf16[1536,2048]{1,0:T(8,128)(2,1)S(1)} %bitcast.116, bf16[1536,256]{1,0:T(8,128)(2,1)S(1)} %bitcast.121, bf16[1536,256]{1,0:T(8,128)(2,1)S(1)} %get-tuple-element.362, bf16[1536,256]{1,0:T(8,128)(2,1)S(1)} %get-tuple-element.361), kind=kOutput, calls=%fused_computation.12 | convolution fusion | flops 4840488960 | bytes 11796480 | tf_op jit(solution)/shard_map/dot_general | solution.py:19
  452.8 7.6 %collective-permute-done.56 = bf16[256,1024]{1,0:T(8,128)(2,1)S(1)} collective-permute-done((bf16[256,1024]{1,0:T(8,128)(2,1)}, bf16[256,1024]{1,0:T(8,128)(2,1)S(1)}, u32[]{:S(2)}, u32[]{:S(2)}) %collective-permute-start.56) | collective-permute-done | bytes 524320 | tf_op jit(solution)/shard_map/ppermute | solution.py:741
  461.2 6.1 %convolution_convert_fusion.3 = bf16[768,2048]{1,0:T(8,128)(2,1)} fusion(bf16[2048,768]{1,0:T(8,128)(2,1)} %constant_dynamic-update-slice_fusion, bf16[1536,768]{1,0:T(8,128)(2,1)S(1)} %copy-done.121), kind=kOutput, calls=%fused_computation.6 | convolution fusion | flops 2417491968 | bytes 7471104 | tf_op jit(solution)/shard_map/dot_general | solution.py:23
  472.2 5.2 convolution_convert_fusion.4
  484.9 4.0 fusion.152
  488.9 3.8 add_add_fusion
  492.8 3.4 fusion.133
  508.2 6.3 %collective-permute-done.60 = bf16[192,2048]{1,0:T(8,128)(2,1)S(1)} collective-permute-done((bf16[192,2048]{1,0:T(8,128)(2,1)S(1)}, bf16[192,2048]{1,0:T(8,128)(2,1)S(1)}, u32[]{:S(2)}, u32[]{:S(2)}) %collective-permute-start.60) | collective-permute-done | bytes 786464 | tf_op jit(solution)/shard_map/ppermute | solution.py:48
  514.6 2.9 add_add_fusion.1
  519.9 33.0 %reduce-scatter.2.cloned.1.call-done = bf16[512,1024]{0,1:T(8,128)(2,1)} async-done(((bf16[2048,1024]{0,1:T(8,128)(2,1)}), bf16[512,1024]{0,1:T(8,128)(2,1)}) %reduce-scatter.2.cloned.1.call-update) | async-done | bytes 1048592 | tf_op jit(solution)/shard_map/reduce_scatter | solution.py:135
  (594 shorter events, 175.7 us)
Async XLA Ops:
  7.2 225.2 %all-gather.3.cloned.1.call-start = ((), (), s32[]{:S(2)}) async-start(), calls=%async_computation.1 | async-start | bytes 7077888 | tf_op jit(solution)/shard_map/all_gather | solution.py:630
  7.2 21.2 %collective-permute-start = (bf16[192,2048]{1,0:T(8,128)(2,1)}, bf16[192,2048]{1,0:T(8,128)(2,1)}, u32[]{:S(2)}, u32[]{:S(2)}) collective-permute-start(bf16[192,2048]{1,0:T(8,128)(2,1)} %refs_2_.2), channel_id=1, source_target_pairs={{0,4},{1,3},{2,6},{3,1},{4,0},{5,7},{6,2},{7,5},{8,12},{9,11},{10,... | collective-permute-start | bytes 2359304 | tf_op jit(solution)/shard_map/ppermute | solution.py:48
  10.3 18.2 %collective-permute-start.3 = (bf16[192,2048]{1,0:T(8,128)(2,1)}, bf16[192,2048]{1,0:T(8,128)(2,1)S(1)}, u32[]{:S(2)}, u32[]{:S(2)}) collective-permute-start(bf16[192,2048]{1,0:T(8,128)(2,1)} %refs_2_.2), channel_id=1, source_target_pairs={{0,2},{1,5},{2,0},{3,7},{4,6},{5,1},{6,4},{7,3},{8,10},{9,13},{10,... | collective-permute-start | bytes 2359304 | tf_op jit(solution)/shard_map/ppermute | solution.py:48
  11.8 21.1 %collective-permute-start.2 = (bf16[192,2048]{1,0:T(8,128)(2,1)}, bf16[192,2048]{1,0:T(8,128)(2,1)S(1)}, u32[]{:S(2)}, u32[]{:S(2)}) collective-permute-start(bf16[192,2048]{1,0:T(8,128)(2,1)} %refs_2_.2), channel_id=1, source_target_pairs={{0,1},{1,0},{2,3},{3,2},{4,5},{5,4},{6,7},{7,6},{8,9},{9,8},{10,11... | collective-permute-start | bytes 2359304 | tf_op jit(solution)/shard_map/ppermute | solution.py:48
  28.5 8.9 %collective-permute-start.5 = (bf16[192,2048]{1,0:T(8,128)(2,1)}, bf16[192,2048]{1,0:T(8,128)(2,1)S(1)}, u32[]{:S(2)}, u32[]{:S(2)}) collective-permute-start(bf16[192,2048]{1,0:T(8,128)(2,1)} %collective-permute-done.refs_1_), channel_id=1, source_target_pairs={{0,1},{1,0},{2,3},{3,2},{4,5},{5,4},{6,7},{7,6},{8,9},{9,8},{10,11... | collective-permute-start | bytes 2359304 | tf_op jit(solution)/shard_map/ppermute | solution.py:48
  28.5 9.0 %collective-permute-start.4 = (bf16[192,2048]{1,0:T(8,128)(2,1)S(1)}, bf16[192,2048]{1,0:T(8,128)(2,1)S(1)}, u32[]{:S(2)}, u32[]{:S(2)}) collective-permute-start(bf16[192,2048]{1,0:T(8,128)(2,1)S(1)} %collective-permute-done.3.refs_0_), channel_id=1, source_target_pairs={{0,1},{1,0},{2,3},{3,2},{4,5},{5,4},{6,7},{7,6},{8,9},{9,8},{10,11... | collective-permute-start | bytes 2359304 | tf_op jit(solution)/shard_map/ppermute | solution.py:48
  31.4 12.3 %collective-permute-start.1 = (bf16[192,2048]{1,0:T(8,128)(2,1)}, bf16[192,2048]{1,0:T(8,128)(2,1)}, u32[]{:S(2)}, u32[]{:S(2)}) collective-permute-start(bf16[192,2048]{1,0:T(8,128)(2,1)} %collective-permute-done.refs_1_), channel_id=1, source_target_pairs={{0,2},{1,5},{2,0},{3,7},{4,6},{5,1},{6,4},{7,3},{8,10},{9,13},{10,... | collective-permute-start | bytes 2359304 | tf_op jit(solution)/shard_map/ppermute | solution.py:48
  87.0 12.1 %collective-permute-start.12 = (bf16[192,2048]{1,0:T(8,128)(2,1)S(1)}, bf16[192,2048]{1,0:T(8,128)(2,1)S(1)}, u32[]{:S(2)}, u32[]{:S(2)}) collective-permute-start(bf16[192,2048]{1,0:T(8,128)(2,1)S(1)} %get-tuple-element.370), channel_id=1, source_target_pairs={{0,2},{1,5},{2,0},{3,7},{4,6},{5,1},{6,4},{7,3},{8,10},{9,13},{10,... | collective-permute-start | bytes 2359304 | tf_op jit(solution)/shard_map/ppermute | solution.py:48
  99.5 19.5 %collective-permute-start.13 = (bf16[192,2048]{1,0:T(8,128)(2,1)S(1)}, bf16[192,2048]{1,0:T(8,128)(2,1)S(1)}, u32[]{:S(2)}, u32[]{:S(2)}) collective-permute-start(bf16[192,2048]{1,0:T(8,128)(2,1)S(1)} %add_convert_fusion.11), channel_id=1, source_target_pairs={{0,4},{1,3},{2,6},{3,1},{4,0},{5,7},{6,2},{7,5},{8,12},{9,11},{10,... | collective-permute-start | bytes 2359304 | tf_op jit(solution)/shard_map/ppermute | solution.py:48
  101.5 17.5 %collective-permute-start.11 = (bf16[192,2048]{1,0:T(8,128)(2,1)S(1)}, bf16[192,2048]{1,0:T(8,128)(2,1)S(1)}, u32[]{:S(2)}, u32[]{:S(2)}) collective-permute-start(bf16[192,2048]{1,0:T(8,128)(2,1)S(1)} %get-tuple-element.369), channel_id=1, source_target_pairs={{0,2},{1,5},{2,0},{3,7},{4,6},{5,1},{6,4},{7,3},{8,10},{9,13},{10,... | collective-permute-start | bytes 2359304 | tf_op jit(solution)/shard_map/ppermute | solution.py:48
  120.4 19.9 %collective-permute-start.14 = (bf16[192,2048]{1,0:T(8,128)(2,1)S(1)}, bf16[192,2048]{1,0:T(8,128)(2,1)S(1)}, u32[]{:S(2)}, u32[]{:S(2)}) collective-permute-start(bf16[192,2048]{1,0:T(8,128)(2,1)S(1)} %fusion.97.refs_2_), channel_id=1, source_target_pairs={{0,4},{1,3},{2,6},{3,1},{4,0},{5,7},{6,2},{7,5},{8,12},{9,11},{10,... | collective-permute-start | bytes 2359304 | tf_op jit(solution)/shard_map/ppermute | solution.py:48
  122.1 18.9 %collective-permute-start.17 = (bf16[192,2048]{1,0:T(8,128)(2,1)S(1)}, bf16[192,2048]{1,0:T(8,128)(2,1)S(1)}, u32[]{:S(2)}, u32[]{:S(2)}) collective-permute-start(bf16[192,2048]{1,0:T(8,128)(2,1)S(1)} %fusion.97.refs_2_), channel_id=1, source_target_pairs={{0,2},{1,5},{2,0},{3,7},{4,6},{5,1},{6,4},{7,3},{8,10},{9,13},{10,... | collective-permute-start | bytes 2359304 | tf_op jit(solution)/shard_map/ppermute | solution.py:48
  123.4 18.9 %collective-permute-start.16 = (bf16[192,2048]{1,0:T(8,128)(2,1)S(1)}, bf16[192,2048]{1,0:T(8,128)(2,1)S(1)}, u32[]{:S(2)}, u32[]{:S(2)}) collective-permute-start(bf16[192,2048]{1,0:T(8,128)(2,1)S(1)} %fusion.97.refs_2_), channel_id=1, source_target_pairs={{0,1},{1,0},{2,3},{3,2},{4,5},{5,4},{6,7},{7,6},{8,9},{9,8},{10,11... | collective-permute-start | bytes 2359304 | tf_op jit(solution)/shard_map/ppermute | solution.py:48
  124.8 37.9 %collective-permute-start.20 = (bf16[192,2048]{1,0:T(8,128)(2,1)S(1)}, bf16[192,2048]{1,0:T(8,128)(2,1)}, u32[]{:S(2)}, u32[]{:S(2)}) collective-permute-start(bf16[192,2048]{1,0:T(8,128)(2,1)S(1)} %fusion.97.refs_2_), channel_id=1, source_target_pairs={{0,16},{8,24},{16,0},{24,8},{1,17},{9,25},{17,1},{25,9},{2,18},{10... | collective-permute-start | bytes 2359304 | tf_op jit(solution)/shard_map/ppermute | solution.py:627
  140.4 8.5 %collective-permute-start.19 = (bf16[192,2048]{1,0:T(8,128)(2,1)S(1)}, bf16[192,2048]{1,0:T(8,128)(2,1)S(1)}, u32[]{:S(2)}, u32[]{:S(2)}) collective-permute-start(bf16[192,2048]{1,0:T(8,128)(2,1)S(1)} %collective-permute-done.14.refs_1_), channel_id=1, source_target_pairs={{0,1},{1,0},{2,3},{3,2},{4,5},{5,4},{6,7},{7,6},{8,9},{9,8},{10,11... | collective-permute-start | bytes 2359304 | tf_op jit(solution)/shard_map/ppermute | solution.py:48
  140.4 22.3 %collective-permute-start.15 = (bf16[192,2048]{1,0:T(8,128)(2,1)S(1)}, bf16[192,2048]{1,0:T(8,128)(2,1)S(1)}, u32[]{:S(2)}, u32[]{:S(2)}) collective-permute-start(bf16[192,2048]{1,0:T(8,128)(2,1)S(1)} %collective-permute-done.14.refs_1_), channel_id=1, source_target_pairs={{0,2},{1,5},{2,0},{3,7},{4,6},{5,1},{6,4},{7,3},{8,10},{9,13},{10,... | collective-permute-start | bytes 2359304 | tf_op jit(solution)/shard_map/ppermute | solution.py:48
  162.7 178.8 %all-gather.5.cloned.1.call-start = ((), (), s32[]{:S(2)}) async-start(), calls=%async_computation.2 | async-start | bytes 7077888 | tf_op jit(solution)/shard_map/all_gather | solution.py:630
  184.7 27.1 %collective-permute-start.24 = (bf16[192,2048]{1,0:T(8,128)(2,1)S(1)}, bf16[192,2048]{1,0:T(8,128)(2,1)S(1)}, u32[]{:S(2)}, u32[]{:S(2)}) collective-permute-start(bf16[192,2048]{1,0:T(8,128)(2,1)S(1)} %get-tuple-element.368), channel_id=1, source_target_pairs={{0,2},{1,5},{2,0},{3,7},{4,6},{5,1},{6,4},{7,3},{8,10},{9,13},{10,... | collective-permute-start | bytes 2359304 | tf_op jit(solution)/shard_map/ppermute | solution.py:48
  185.5 44.7 %collective-permute-start.23 = (bf16[192,2048]{1,0:T(8,128)(2,1)S(1)}, bf16[192,2048]{1,0:T(8,128)(2,1)S(1)}, u32[]{:S(2)}, u32[]{:S(2)}) collective-permute-start(bf16[192,2048]{1,0:T(8,128)(2,1)S(1)} %get-tuple-element.367), channel_id=1, source_target_pairs={{0,2},{1,5},{2,0},{3,7},{4,6},{5,1},{6,4},{7,3},{8,10},{9,13},{10,... | collective-permute-start | bytes 2359304 | tf_op jit(solution)/shard_map/ppermute | solution.py:48
  212.2 18.0 %collective-permute-start.25 = (bf16[192,2048]{1,0:T(8,128)(2,1)S(1)}, bf16[192,2048]{1,0:T(8,128)(2,1)S(1)}, u32[]{:S(2)}, u32[]{:S(2)}) collective-permute-start(bf16[192,2048]{1,0:T(8,128)(2,1)S(1)} %add_convert_fusion.8), channel_id=1, source_target_pairs={{0,4},{1,3},{2,6},{3,1},{4,0},{5,7},{6,2},{7,5},{8,12},{9,11},{10,... | collective-permute-start | bytes 2359304 | tf_op jit(solution)/shard_map/ppermute | solution.py:48
  232.4 25.1 %collective-permute-start.32 = (bf16[192,2048]{1,0:T(8,128)(2,1)S(1)}, bf16[192,2048]{1,0:T(8,128)(2,1)S(1)}, u32[]{:S(2)}, u32[]{:S(2)}) collective-permute-start(bf16[192,2048]{1,0:T(8,128)(2,1)S(1)} %fusion.41.refs_0_.refs_10_.refs_2_), channel_id=1, source_target_pairs={{0,1},{1,0},{2,3},{3,2},{4,5},{5,4},{6,7},{7,6},{8,9},{9,8},{10,11... | collective-permute-start | bytes 2359304 | tf_op jit(solution)/shard_map/ppermute | solution.py:48
  232.6 21.5 %collective-permute-start.26 = (bf16[192,2048]{1,0:T(8,128)(2,1)S(1)}, bf16[192,2048]{1,0:T(8,128)(2,1)S(1)}, u32[]{:S(2)}, u32[]{:S(2)}) collective-permute-start(bf16[192,2048]{1,0:T(8,128)(2,1)S(1)} %fusion.41.refs_0_.refs_10_.refs_2_), channel_id=1, source_target_pairs={{0,4},{1,3},{2,6},{3,1},{4,0},{5,7},{6,2},{7,5},{8,12},{9,11},{10,... | collective-permute-start | bytes 2359304 | tf_op jit(solution)/shard_map/ppermute | solution.py:48
  233.1 21.0 %collective-permute-start.29 = (bf16[192,2048]{1,0:T(8,128)(2,1)S(1)}, bf16[192,2048]{1,0:T(8,128)(2,1)S(1)}, u32[]{:S(2)}, u32[]{:S(2)}) collective-permute-start(bf16[192,2048]{1,0:T(8,128)(2,1)S(1)} %fusion.41.refs_0_.refs_10_.refs_2_), channel_id=1, source_target_pairs={{0,2},{1,5},{2,0},{3,7},{4,6},{5,1},{6,4},{7,3},{8,10},{9,13},{10,... | collective-permute-start | bytes 2359304 | tf_op jit(solution)/shard_map/ppermute | solution.py:48
  234.0 20.1 %collective-permute-start.27 = (bf16[192,1024]{1,0:T(8,128)(2,1)S(1)}, bf16[192,1024]{1,0:T(8,128)(2,1)S(1)}, u32[]{:S(2)}, u32[]{:S(2)}) collective-permute-start(bf16[192,1024]{1,0:T(8,128)(2,1)S(1)} %get-tuple-element.394), channel_id=1, source_target_pairs={{0,16},{8,24},{16,0},{24,8},{1,17},{9,25},{17,1},{25,9},{2,18},{10... | collective-permute-start | bytes 1179656 | tf_op jit(solution)/shard_map/ppermute | solution.py:627
  254.6 21.9 %collective-permute-start.28 = (bf16[192,2048]{1,0:T(8,128)(2,1)S(1)}, bf16[192,2048]{1,0:T(8,128)(2,1)S(1)}, u32[]{:S(2)}, u32[]{:S(2)}) collective-permute-start(bf16[192,2048]{1,0:T(8,128)(2,1)S(1)} %collective-permute-done.26.refs_1_.refs_9_), channel_id=1, source_target_pairs={{0,2},{1,5},{2,0},{3,7},{4,6},{5,1},{6,4},{7,3},{8,10},{9,13},{10,... | collective-permute-start | bytes 2359304 | tf_op jit(solution)/shard_map/ppermute | solution.py:48
  255.7 20.8 %collective-permute-start.33 = (bf16[192,1024]{1,0:T(8,128)(2,1)S(1)}, bf16[192,1024]{1,0:T(8,128)(2,1)S(1)}, u32[]{:S(2)}, u32[]{:S(2)}) collective-permute-start(bf16[192,1024]{1,0:T(8,128)(2,1)S(1)} %get-tuple-element.192), channel_id=1, source_target_pairs={{0,16},{8,24},{16,0},{24,8},{1,17},{9,25},{17,1},{25,9},{2,18},{10... | collective-permute-start | bytes 1179656 | tf_op jit(solution)/shard_map/ppermute | solution.py:627
  277.6 275.3 %reduce-scatter.2.cloned.1.call-start = ((), (), s32[]{:S(2)}) async-start(), calls=%async_computation.3 | async-start | bytes 5242880 | tf_op jit(solution)/shard_map/reduce_scatter | solution.py:135
  300.4 17.4 %collective-permute-start.35 = (bf16[768,2048]{1,0:T(8,128)(2,1)}, bf16[768,2048]{1,0:T(8,128)(2,1)}, u32[]{:S(2)}, u32[]{:S(2)}) collective-permute-start(bf16[768,2048]{1,0:T(8,128)(2,1)} %convolution_convert_fusion.1), channel_id=1, source_target_pairs={{0,1},{1,0},{2,3},{3,2},{4,5},{5,4},{6,7},{7,6},{8,9},{9,8},{10,11... | collective-permute-start | bytes 9437192 | tf_op jit(solution)/shard_map/ppermute | solution.py:48
  321.3 13.6 %collective-permute-start.36 = (bf16[192,2048]{1,0:T(8,128)(2,1)S(1)}, bf16[192,2048]{1,0:T(8,128)(2,1)S(1)}, u32[]{:S(2)}, u32[]{:S(2)}) collective-permute-start(bf16[192,2048]{1,0:T(8,128)(2,1)S(1)} %get-tuple-element.366), channel_id=1, source_target_pairs={{0,2},{1,5},{2,0},{3,7},{4,6},{5,1},{6,4},{7,3},{8,10},{9,13},{10,... | collective-permute-start | bytes 2359304 | tf_op jit(solution)/shard_map/ppermute | solution.py:48
  321.5 38.1 %collective-permute-start.38 = (bf16[192,2048]{1,0:T(8,128)(2,1)}, bf16[192,2048]{1,0:T(8,128)(2,1)}, u32[]{:S(2)}, u32[]{:S(2)}) collective-permute-start(bf16[192,2048]{1,0:T(8,128)(2,1)} %get-tuple-element.365), channel_id=1, source_target_pairs={{0,2},{1,5},{2,0},{3,7},{4,6},{5,1},{6,4},{7,3},{8,10},{9,13},{10,... | collective-permute-start | bytes 2359304 | tf_op jit(solution)/shard_map/ppermute | solution.py:48
  337.6 22.0 %collective-permute-start.37 = (bf16[192,2048]{1,0:T(8,128)(2,1)}, bf16[192,2048]{1,0:T(8,128)(2,1)}, u32[]{:S(2)}, u32[]{:S(2)}) collective-permute-start(bf16[192,2048]{1,0:T(8,128)(2,1)} %add_convert_fusion.5), channel_id=1, source_target_pairs={{0,4},{1,3},{2,6},{3,1},{4,0},{5,7},{6,2},{7,5},{8,12},{9,11},{10,... | collective-permute-start | bytes 2359304 | tf_op jit(solution)/shard_map/ppermute | solution.py:48
  368.0 20.1 %collective-permute-start.39 = (bf16[192,2048]{1,0:T(8,128)(2,1)S(1)}, bf16[192,2048]{1,0:T(8,128)(2,1)S(1)}, u32[]{:S(2)}, u32[]{:S(2)}) collective-permute-start(bf16[192,2048]{1,0:T(8,128)(2,1)S(1)} %get-tuple-element.253), channel_id=1, source_target_pairs={{0,4},{1,3},{2,6},{3,1},{4,0},{5,7},{6,2},{7,5},{8,12},{9,11},{10,... | collective-permute-start | bytes 2359304 | tf_op jit(solution)/shard_map/ppermute | solution.py:48
  370.0 19.1 %collective-permute-start.42 = (bf16[192,2048]{1,0:T(8,128)(2,1)S(1)}, bf16[192,2048]{1,0:T(8,128)(2,1)}, u32[]{:S(2)}, u32[]{:S(2)}) collective-permute-start(bf16[192,2048]{1,0:T(8,128)(2,1)S(1)} %get-tuple-element.253), channel_id=1, source_target_pairs={{0,2},{1,5},{2,0},{3,7},{4,6},{5,1},{6,4},{7,3},{8,10},{9,13},{10,... | collective-permute-start | bytes 2359304 | tf_op jit(solution)/shard_map/ppermute | solution.py:48
  370.2 23.0 %collective-permute-start.41 = (bf16[192,2048]{1,0:T(8,128)(2,1)S(1)}, bf16[192,2048]{1,0:T(8,128)(2,1)}, u32[]{:S(2)}, u32[]{:S(2)}) collective-permute-start(bf16[192,2048]{1,0:T(8,128)(2,1)S(1)} %get-tuple-element.253), channel_id=1, source_target_pairs={{0,1},{1,0},{2,3},{3,2},{4,5},{5,4},{6,7},{7,6},{8,9},{9,8},{10,11... | collective-permute-start | bytes 2359304 | tf_op jit(solution)/shard_map/ppermute | solution.py:48
  388.0 12.0 %collective-permute-start.40 = (bf16[192,2048]{1,0:T(8,128)(2,1)S(1)}, bf16[192,2048]{1,0:T(8,128)(2,1)S(1)}, u32[]{:S(2)}, u32[]{:S(2)}) collective-permute-start(bf16[192,2048]{1,0:T(8,128)(2,1)S(1)} %collective-permute-done.39), channel_id=1, source_target_pairs={{0,2},{1,5},{2,0},{3,7},{4,6},{5,1},{6,4},{7,3},{8,10},{9,13},{10,... | collective-permute-start | bytes 2359304 | tf_op jit(solution)/shard_map/ppermute | solution.py:48
  401.2 25.7 %collective-permute-start.46 = (bf16[256,1024]{1,0:T(8,128)(2,1)S(1)}, bf16[256,1024]{1,0:T(8,128)(2,1)S(1)}, u32[]{:S(2)}, u32[]{:S(2)}) collective-permute-start(bf16[256,1024]{1,0:T(8,128)(2,1)S(1)} %get-tuple-element.384), channel_id=1, source_target_pairs={{0,8},{8,0},{16,24},{24,16},{1,9},{9,1},{17,25},{25,17},{2,10},{10... | collective-permute-start | bytes 1572872 | tf_op jit(solution)/shard_map/ppermute | solution.py:741
  401.2 26.5 %collective-permute-start.47 = (bf16[256,1024]{1,0:T(8,128)(2,1)S(1)}, bf16[256,1024]{1,0:T(8,128)(2,1)S(1)}, u32[]{:S(2)}, u32[]{:S(2)}) collective-permute-start(bf16[256,1024]{1,0:T(8,128)(2,1)S(1)} %get-tuple-element.383), channel_id=1, source_target_pairs={{0,8},{8,0},{16,24},{24,16},{1,9},{9,1},{17,25},{25,17},{2,10},{10... | collective-permute-start | bytes 1572872 | tf_op jit(solution)/shard_map/ppermute | solution.py:741
  403.2 35.3 %collective-permute-start.51 = (bf16[256,1024]{1,0:T(8,128)(2,1)}, bf16[256,1024]{1,0:T(8,128)(2,1)}, u32[]{:S(2)}, u32[]{:S(2)}) collective-permute-start(bf16[256,1024]{1,0:T(8,128)(2,1)} %get-tuple-element.376), channel_id=1, source_target_pairs={{0,8},{8,0},{16,24},{24,16},{1,9},{9,1},{17,25},{25,17},{2,10},{10... | collective-permute-start | bytes 1572872 | tf_op jit(solution)/shard_map/ppermute | solution.py:741
  403.2 49.6 %collective-permute-start.55 = (bf16[256,1024]{1,0:T(8,128)(2,1)}, bf16[256,1024]{1,0:T(8,128)(2,1)}, u32[]{:S(2)}, u32[]{:S(2)}) collective-permute-start(bf16[256,1024]{1,0:T(8,128)(2,1)} %get-tuple-element.375), channel_id=1, source_target_pairs={{0,8},{8,0},{16,24},{24,16},{1,9},{9,1},{17,25},{25,17},{2,10},{10... | collective-permute-start | bytes 1572872 | tf_op jit(solution)/shard_map/ppermute | solution.py:741
  405.2 55.2 %collective-permute-start.56 = (bf16[256,1024]{1,0:T(8,128)(2,1)}, bf16[256,1024]{1,0:T(8,128)(2,1)S(1)}, u32[]{:S(2)}, u32[]{:S(2)}) collective-permute-start(bf16[256,1024]{1,0:T(8,128)(2,1)} %get-tuple-element.374), channel_id=1, source_target_pairs={{0,8},{8,0},{16,24},{24,16},{1,9},{9,1},{17,25},{25,17},{2,10},{10... | collective-permute-start | bytes 1572872 | tf_op jit(solution)/shard_map/ppermute | solution.py:741
  467.3 10.2 %collective-permute-start.57 = (bf16[768,2048]{1,0:T(8,128)(2,1)}, bf16[768,2048]{1,0:T(8,128)(2,1)S(1)}, u32[]{:S(2)}, u32[]{:S(2)}) collective-permute-start(bf16[768,2048]{1,0:T(8,128)(2,1)} %convolution_convert_fusion.3), channel_id=1, source_target_pairs={{0,1},{1,0},{2,3},{3,2},{4,5},{5,4},{6,7},{7,6},{8,9},{9,8},{10,11... | collective-permute-start | bytes 9437192 | tf_op jit(solution)/shard_map/ppermute | solution.py:48
  467.4 34.8 %collective-permute-start.61 = (bf16[256,1024]{1,0:T(8,128)(2,1)}, bf16[256,1024]{1,0:T(8,128)(2,1)}, u32[]{:S(2)}, u32[]{:S(2)}) collective-permute-start(bf16[256,1024]{1,0:T(8,128)(2,1)} %get-tuple-element.373), channel_id=1, source_target_pairs={{0,8},{8,0},{16,24},{24,16},{1,9},{9,1},{17,25},{25,17},{2,10},{10... | collective-permute-start | bytes 1572872 | tf_op jit(solution)/shard_map/ppermute | solution.py:741
  467.8 49.6 %collective-permute-start.52 = (f32[8192]{0:T(1024)S(1)}, f32[8192]{0:T(1024)S(1)}, u32[]{:S(2)}, u32[]{:S(2)}) collective-permute-start(f32[8192]{0:T(1024)S(1)} %bitcast.130), channel_id=1, source_target_pairs={{0,8},{8,0},{16,24},{24,16},{1,9},{9,1},{17,25},{25,17},{2,10},{10... | collective-permute-start | bytes 98312 | tf_op jit(solution)/shard_map/ppermute | solution.py:159
  469.6 47.8 %collective-permute-start.53 = (f32[8192]{0:T(1024)S(1)}, f32[8192]{0:T(1024)S(1)}, u32[]{:S(2)}, u32[]{:S(2)}) collective-permute-start(f32[8192]{0:T(1024)S(1)} %bitcast.131), channel_id=1, source_target_pairs={{0,16},{8,24},{16,0},{24,8},{1,17},{9,25},{17,1},{25,9},{2,18},{10... | collective-permute-start | bytes 98312 | tf_op jit(solution)/shard_map/ppermute | solution.py:159
  470.7 46.8 %collective-permute-start.54 = (f32[8192]{0:T(1024)S(1)}, f32[8192]{0:T(1024)S(1)}, u32[]{:S(2)}, u32[]{:S(2)}) collective-permute-start(f32[8192]{0:T(1024)S(1)} %bitcast.132), channel_id=1, source_target_pairs={{0,24},{8,16},{16,8},{24,0},{1,25},{9,17},{17,9},{25,1},{2,26},{10... | collective-permute-start | bytes 98312 | tf_op jit(solution)/shard_map/ppermute | solution.py:159
  479.7 16.4 %collective-permute-start.59 = (bf16[192,2048]{1,0:T(8,128)(2,1)}, bf16[192,2048]{1,0:T(8,128)(2,1)}, u32[]{:S(2)}, u32[]{:S(2)}) collective-permute-start(bf16[192,2048]{1,0:T(8,128)(2,1)} %get-tuple-element.364), channel_id=1, source_target_pairs={{0,2},{1,5},{2,0},{3,7},{4,6},{5,1},{6,4},{7,3},{8,10},{9,13},{10,... | collective-permute-start | bytes 2359304 | tf_op jit(solution)/shard_map/ppermute | solution.py:48
  496.1 18.4 %collective-permute-start.58 = (bf16[192,2048]{1,0:T(8,128)(2,1)S(1)}, bf16[192,2048]{1,0:T(8,128)(2,1)S(1)}, u32[]{:S(2)}, u32[]{:S(2)}) collective-permute-start(bf16[192,2048]{1,0:T(8,128)(2,1)S(1)} %copy-done.129), channel_id=1, source_target_pairs={{0,2},{1,5},{2,0},{3,7},{4,6},{5,1},{6,4},{7,3},{8,10},{9,13},{10,... | collective-permute-start | bytes 2359304 | tf_op jit(solution)/shard_map/ppermute | solution.py:48
  502.3 12.3 %collective-permute-start.60 = (bf16[192,2048]{1,0:T(8,128)(2,1)S(1)}, bf16[192,2048]{1,0:T(8,128)(2,1)S(1)}, u32[]{:S(2)}, u32[]{:S(2)}) collective-permute-start(bf16[192,2048]{1,0:T(8,128)(2,1)S(1)} %add_convert_fusion.2), channel_id=1, source_target_pairs={{0,4},{1,3},{2,6},{3,1},{4,0},{5,7},{6,2},{7,5},{8,12},{9,11},{10,... | collective-permute-start | bytes 2359304 | tf_op jit(solution)/shard_map/ppermute | solution.py:48
  (189 other events, 1369.3 us)
Sparse Core Ops, SparseCore 0:
  162.8 53.9 all-gather.2
  277.7 44.3 all-gather.4
  467.5 85.3 reduce-scatter.1

commit v4 on v3

--- a/solution.py
+++ b/solution.py
@@ -367,7 +367,7 @@
             ),
             scratch_shapes=[pltpu.VMEM((length, local), BF16)] * 2 + [pltpu.VMEM((blocks, block, 3 * local), F32)],
         ),
-        compiler_params=pltpu.CompilerParams(vmem_limit_bytes=30 * 2**20),
+        compiler_params=pltpu.CompilerParams(vmem_limit_bytes=60 * 2**20),
         cost_estimate=pl.CostEstimate(flops=4 * 10**9, bytes_accessed=10**7, transcendentals=2 * 10**6),
     )(order, *raws, sums, gains, table, docs)
 

time: 573 us -> 575 us (level)
    unnamed x364 -> x332, local copies, waits for them, and re-layouts: 44.5 us -> 42.3 us
  transfers between devices with their start and end apart: 65 -> 65, of which waited for: 25 -> 24; matrix products, arithmetic and copies ran while one was open for 34% -> 34% of each run, Pallas kernels for 11% -> 11%
where the time goes in v4:
time: 575 us; the launch traced here: 568 us
  waiting for transfers between devices  169 us (29%)
  matrix products  139 us (24%)
  Pallas kernels  78.3 us (14%)
  other arithmetic  64.4 us (11%)
  local copies, waits for them, and re-layouts  50.6 us (9%)
  starting transfers between devices  49.9 us (9%)
  between operations  16.3 us (3%)
    ppermute x50, waiting for transfers between devices, send(): return lax.ppermute(value, 'tensor', way)  119 us
    dot_general x11, matrix products, times(): return jnp.dot(left, right, preferred_element_type=F32)  57.9 us
    dot_general x16, matrix products, contract_rows(): lax.dot_general(left, right, (((0,), (0,)), ((), ())), preferred_element_...  43.8 us
    unnamed x332, local copies, waits for them, and re-layouts  42.3 us
    dot_general x7, matrix products, times_transposed(): lax.dot_general(left, right, (((1,), (1,)), ((), ())), preferred_element_...  37.4 us
    pallas_call x4, Pallas kernels, feed_back(): pl.pallas_call(functools.partial(feed_back_kernel, count, with_activated)...  36.9 us
    ppermute x50, starting transfers between devices, send(): return lax.ppermute(value, 'tensor', way)  36.4 us
    reduce_scatter x1, waiting for transfers between devices, scatter_rows(): return lax.psum_scatter(part, 'dp', scatter_dimension=dimension, tiled=True)  33.1 us
  transfers between devices with their start and end apart: 65, of which 24 were waited for; matrix products, arithmetic and copies ran while one was open for 34% of the time, Pallas kernels for 11%

profile of v4, /device:TPU:0, one launch (start us, length us, event | category | flops | bytes accessed | tf_op | source)
XLA Modules:
  0.0 567.6 jit_solution(8402216314524897659)
XLA Ops:
  7.2 3.0 collective-permute-start
  11.8 3.8 fusion.99
  21.1 7.4 %collective-permute-done.refs_1_ = bf16[192,2048]{1,0:T(8,128)(2,1)S(1)} collective-permute-done((bf16[192,2048]{1,0:T(8,128)(2,1)}, bf16[192,2048]{1,0:T(8,128)(2,1)S(1)}, u32[]{:S(2)}, u32[]{:S(2)}) %collective-permute-start) | collective-permute-done | bytes 786464 | tf_op jit(solution)/shard_map/ppermute | solution.py:48
  32.9 4.3 fusion.55.refs_0_
  37.3 4.0 fusion.1.refs_1_
  46.9 3.8 fusion.59.refs_2_
  62.4 17.7 %shard_map.237 = (bf16[8,192,256]{2,1,0:T(8,128)(2,1)}, bf16[1536,256]{1,0:T(8,128)(2,1)}, bf16[1536,256]{1,0:T(8,128)(2,1)}, bf16[1536,256]{1,0:T(8,128)(2,1)}, f32[8,2,192]{2,1,0:T(2,128)}) custom-call(s32[8]{0:T(128)} %select_reduce_fusion.3.order, f32[384,768]{1,0:T(8,128)} %fusion.55.refs_0_, f32[768,768]{1,0:T(8,128)} %fusion.1.refs_1_, ...), custom_call_target="tpu_custom_call" | custom-call | flops 4000000000 | bytes 10000000 | tf_op jit(solution)/shard_map/pallas_call | solution.py:342
  84.7 4.6 collective-permute-done.10
  91.1 11.0 %collective-permute-done.12 = bf16[192,2048]{1,0:T(8,128)(2,1)S(1)} collective-permute-done((bf16[192,2048]{1,0:T(8,128)(2,1)S(1)}, bf16[192,2048]{1,0:T(8,128)(2,1)S(1)}, u32[]{:S(2)}, u32[]{:S(2)}) %collective-permute-start.12) | collective-permute-done | bytes 786464 | tf_op jit(solution)/shard_map/ppermute | solution.py:48
  109.5 12.5 %collective-permute-done.13 = bf16[192,2048]{1,0:T(8,128)(2,1)S(1)} collective-permute-done((bf16[192,2048]{1,0:T(8,128)(2,1)S(1)}, bf16[192,2048]{1,0:T(8,128)(2,1)S(1)}, u32[]{:S(2)}, u32[]{:S(2)}) %collective-permute-start.13) | collective-permute-done | bytes 786464 | tf_op jit(solution)/shard_map/ppermute | solution.py:48
  130.4 12.9 %collective-permute-done.14.refs_1_ = bf16[192,2048]{1,0:T(8,128)(2,1)S(1)} collective-permute-done((bf16[192,2048]{1,0:T(8,128)(2,1)S(1)}, bf16[192,2048]{1,0:T(8,128)(2,1)S(1)}, u32[]{:S(2)}, u32[]{:S(2)}) %collective-permute-start.14) | collective-permute-done | bytes 786464 | tf_op jit(solution)/shard_map/ppermute | solution.py:48
  145.3 3.5 fusion.63.refs_3_
  152.0 6.7 %fusion.9.refs_5_ = f32[768,2048]{1,0:T(8,128)S(1)} fusion(bf16[2048,2048]{1,0:T(8,128)(2,1)S(1)} %constant_dynamic-update-slice_fusion.3, bf16[192,2048]{1,0:T(8,128)(2,1)S(1)} %collective-permute-done.19.refs_5_, bf16[192,2048]{1,0:T(8,128)(2,1)S(1)} %collective-permute-done.18.refs_4_, bf16[192,2048]{1,0:T(8,128)(2,1)S(1)} %collective-permute-done.14.refs_1_, ...), kind=kOutput, calls=%fused_computation.23 | convolution fusion | flops 6455033856 | bytes 17825792 | tf_op jit(solution)/shard_map/dot_general | solution.py:27
  161.5 4.1 collective-permute-done.20
  167.9 6.2 %fusion.67.refs_3_ = f32[384,2048]{1,0:T(8,128)S(1)} fusion(bf16[2048,2048]{1,0:T(8,128)(2,1)} %copy-done.106, bf16[192,2048]{1,0:T(8,128)(2,1)S(1)} %collective-permute-done.21.refs_7_, bf16[192,2048]{1,0:T(8,128)(2,1)S(1)} %collective-permute-done.15.refs_3_), kind=kOutput, calls=%fused_computation.94 | convolution fusion | flops 3224371200 | bytes 13107200 | tf_op jit(solution)/shard_map/dot_general | solution.py:27
  177.7 3.6 convolution_convert_fusion.5
  181.5 3.6 convolution_convert_fusion.6
  189.7 25.0 %collective-permute-done.24 = bf16[192,2048]{1,0:T(8,128)(2,1)S(1)} collective-permute-done((bf16[192,2048]{1,0:T(8,128)(2,1)S(1)}, bf16[192,2048]{1,0:T(8,128)(2,1)S(1)}, u32[]{:S(2)}, u32[]{:S(2)}) %collective-permute-start.24) | collective-permute-done | bytes 786464 | tf_op jit(solution)/shard_map/ppermute | solution.py:48
  215.2 17.9 %collective-permute-done.23 = bf16[192,2048]{1,0:T(8,128)(2,1)S(1)} collective-permute-done((bf16[192,2048]{1,0:T(8,128)(2,1)S(1)}, bf16[192,2048]{1,0:T(8,128)(2,1)S(1)}, u32[]{:S(2)}, u32[]{:S(2)}) %collective-permute-start.23) | collective-permute-done | bytes 786464 | tf_op jit(solution)/shard_map/ppermute | solution.py:48
  237.0 19.0 %convolution_convert_fusion.refs_2_ = bf16[1536,2048]{1,0:T(8,128)(2,1)} fusion(bf16[1536,2048]{1,0:T(8,128)(2,1)} %all-gather.3.cloned.1.call-done.refs_0_, bf16[2048,2048]{1,0:T(8,128)(2,1)} %copy-done.106), kind=kOutput, calls=%fused_computation | convolution fusion | flops 12888047616 | bytes 20971520 | tf_op jit(solution)/shard_map/dot_general | solution.py:27
  260.5 3.0 shard_map.239
  263.6 8.3 %shard_map.240 = (bf16[4,192,2048]{2,1,0:T(8,128)(2,1)S(1)}, bf16[4,192,2048]{2,1,0:T(8,128)(2,1)S(1)}) custom-call(bf16[192,2048]{1,0:T(8,128)(2,1)S(1)} %collective-permute-done.29.refs_0_.refs_8_, bf16[192,2048]{1,0:T(8,128)(2,1)S(1)} %collective-permute-done.26.refs_1_.refs_9_, ...), custom_call_target="tpu_custom_call", output_to_operand_aliasing={{0}: (6, {}), {1}: (7, {})} | custom-call | flops 3221225472 | bytes 16777216 | tf_op jit(solution)/shard_map/pallas_call | solution.py:464
  275.4 4.2 collective-permute-done.33
  283.9 7.5 %shard_map.241 = (bf16[4,192,2048]{2,1,0:T(8,128)(2,1)}, bf16[4,192,2048]{2,1,0:T(8,128)(2,1)}) custom-call(bf16[192,2048]{1,0:T(8,128)(2,1)} %copy-done.32, bf16[192,2048]{1,0:T(8,128)(2,1)} %copy-done.35, bf16[1024,2048]{1,0:T(8,128)(2,1)} %refs_1_.1, f32[384,2048]{1,0:T(8,128)} %copy-done.86, ...), custom_call_target="tpu_custom_call", output_to_operand_aliasing={{0}: (4, {}), {1}: (5, {})} | custom-call | flops 1610612736 | bytes 10485760 | tf_op jit(solution)/shard_map/pallas_call | solution.py:464
  291.4 12.0 %convolution_convert_fusion.1 = bf16[768,2048]{1,0:T(8,128)(2,1)} fusion(bf16[768,2048]{1,0:T(8,128)(2,1)} %bitcast.103, bf16[2048,2048]{1,0:T(8,128)(2,1)} %copy-done.106), kind=kOutput, calls=%fused_computation.4 | convolution fusion | flops 6444023808 | bytes 14680064 | tf_op jit(solution)/shard_map/dot_general | solution.py:23
  310.1 9.4 %convolution_convert_fusion.2 = bf16[768,2048]{1,0:T(8,128)(2,1)S(1)} fusion(bf16[768,2048]{1,0:T(8,128)(2,1)S(1)} %bitcast.106, bf16[2048,2048]{1,0:T(8,128)(2,1)} %copy-done.106), kind=kOutput, calls=%fused_computation.5 | convolution fusion | flops 6444023808 | bytes 14680064 | tf_op jit(solution)/shard_map/dot_general | solution.py:23
  319.5 4.0 add_convert_fusion.6
  327.6 3.2 fusion.146
  333.3 4.0 convolution_add_fusion.1
  339.9 3.9 fusion.151
  343.8 18.1 %shard_map.243 = (bf16[1536,1024]{1,0:T(8,128)(2,1)}, bf16[4,192,2048]{2,1,0:T(8,128)(2,1)}, bf16[4,192,2048]{2,1,0:T(8,128)(2,1)}) custom-call(bf16[1536,2048]{1,0:T(8,128)(2,1)} %all-gather.5.cloned.1.call-done.refs_0_.refs_1_.refs_8_, bf16[1024,2048]{1,0:T(8,128)(2,1)} %refs_1_.1, bf16[1536,2048]{1,0:T(8,128)(2,1)} %convolution_convert_fusion.refs_2_), custom_call_target="tpu_custom_call" | custom-call | flops 6442450944 | bytes 29360128 | tf_op jit(solution)/shard_map/pallas_call | solution.py:464
  362.0 3.6 multiply_reduce_fusion.1
  365.7 4.6 multiply_convert_fusion
  383.0 7.4 %collective-permute-done.39 = bf16[192,2048]{1,0:T(8,128)(2,1)S(1)} collective-permute-done((bf16[192,2048]{1,0:T(8,128)(2,1)S(1)}, bf16[192,2048]{1,0:T(8,128)(2,1)S(1)}, u32[]{:S(2)}, u32[]{:S(2)}) %collective-permute-start.39) | collective-permute-done | bytes 786464 | tf_op jit(solution)/shard_map/ppermute | solution.py:48
  391.6 3.9 convolution_add_fusion
  408.8 19.0 %shard_map.246 = (f32[8,192,512]{2,1,0:T(8,128)S(1)}, bf16[8,192,256]{2,1,0:T(8,128)(2,1)S(1)}, f32[8,2,192]{2,1,0:T(2,128)S(1)}, f32[2,256]{1,0:T(2,128)S(1)}) custom-call(s32[8]{0:T(128)S(1)} %copy-done.68, f32[8,192,768]{2,1,0:T(8,128)S(1)} %bitcast.119, f32[8,2,192]{2,1,0:T(2,128)S(1)} %copy-done.65, f32[2,256]{1,0:T(2,128)S(1)} %copy-done.67, ...), custom_call_target="tpu_custom_call" | custom-call | flops 8000000000 | bytes 20000000 | tf_op jit(solution)/shard_map/pallas_call | solution.py:382
  441.6 3.6 fusion.50
  445.6 5.8 %convolution_convert_fusion.9 = bf16[2048,768]{0,1:T(8,128)(2,1)S(1)} fusion(bf16[1536,2048]{1,0:T(8,128)(2,1)S(1)} %bitcast.116, bf16[1536,256]{1,0:T(8,128)(2,1)S(1)} %bitcast.121, bf16[1536,256]{1,0:T(8,128)(2,1)S(1)} %get-tuple-element.362, bf16[1536,256]{1,0:T(8,128)(2,1)S(1)} %get-tuple-element.361), kind=kOutput, calls=%fused_computation.12 | convolution fusion | flops 4840488960 | bytes 11796480 | tf_op jit(solution)/shard_map/dot_general | solution.py:19
  455.4 7.7 %collective-permute-done.56 = bf16[256,1024]{1,0:T(8,128)(2,1)S(1)} collective-permute-done((bf16[256,1024]{1,0:T(8,128)(2,1)}, bf16[256,1024]{1,0:T(8,128)(2,1)S(1)}, u32[]{:S(2)}, u32[]{:S(2)}) %collective-permute-start.56) | collective-permute-done | bytes 524320 | tf_op jit(solution)/shard_map/ppermute | solution.py:741
  463.9 6.1 %convolution_convert_fusion.3 = bf16[768,2048]{1,0:T(8,128)(2,1)} fusion(bf16[2048,768]{1,0:T(8,128)(2,1)} %constant_dynamic-update-slice_fusion, bf16[1536,768]{1,0:T(8,128)(2,1)S(1)} %copy-done.105), kind=kOutput, calls=%fused_computation.6 | convolution fusion | flops 2417491968 | bytes 7471104 | tf_op jit(solution)/shard_map/dot_general | solution.py:23
  474.9 5.3 convolution_convert_fusion.4
  487.7 4.0 fusion.152
  491.7 3.8 add_add_fusion
  495.5 3.4 fusion.133
  506.2 2.7 convert_add_fusion.1
  510.8 6.3 %collective-permute-done.60 = bf16[192,2048]{1,0:T(8,128)(2,1)S(1)} collective-permute-done((bf16[192,2048]{1,0:T(8,128)(2,1)S(1)}, bf16[192,2048]{1,0:T(8,128)(2,1)S(1)}, u32[]{:S(2)}, u32[]{:S(2)}) %collective-permute-start.60) | collective-permute-done | bytes 786464 | tf_op jit(solution)/shard_map/ppermute | solution.py:48
  517.1 2.9 add_add_fusion.1
  522.5 33.1 %reduce-scatter.2.cloned.1.call-done = bf16[512,1024]{0,1:T(8,128)(2,1)} async-done(((bf16[2048,1024]{0,1:T(8,128)(2,1)}), bf16[512,1024]{0,1:T(8,128)(2,1)}) %reduce-scatter.2.cloned.1.call-update) | async-done | bytes 1048592 | tf_op jit(solution)/shard_map/reduce_scatter | solution.py:135
  (562 shorter events, 176.2 us)
Async XLA Ops:
  7.2 228.1 %all-gather.3.cloned.1.call-start = ((), (), s32[]{:S(2)}) async-start(), calls=%async_computation.1 | async-start | bytes 7077888 | tf_op jit(solution)/shard_map/all_gather | solution.py:630
  7.2 21.2 %collective-permute-start = (bf16[192,2048]{1,0:T(8,128)(2,1)}, bf16[192,2048]{1,0:T(8,128)(2,1)S(1)}, u32[]{:S(2)}, u32[]{:S(2)}) collective-permute-start(bf16[192,2048]{1,0:T(8,128)(2,1)} %refs_2_.2), channel_id=1, source_target_pairs={{0,4},{1,3},{2,6},{3,1},{4,0},{5,7},{6,2},{7,5},{8,12},{9,11},{10,... | collective-permute-start | bytes 2359304 | tf_op jit(solution)/shard_map/ppermute | solution.py:48
  10.3 18.2 %collective-permute-start.3 = (bf16[192,2048]{1,0:T(8,128)(2,1)}, bf16[192,2048]{1,0:T(8,128)(2,1)S(1)}, u32[]{:S(2)}, u32[]{:S(2)}) collective-permute-start(bf16[192,2048]{1,0:T(8,128)(2,1)} %refs_2_.2), channel_id=1, source_target_pairs={{0,2},{1,5},{2,0},{3,7},{4,6},{5,1},{6,4},{7,3},{8,10},{9,13},{10,... | collective-permute-start | bytes 2359304 | tf_op jit(solution)/shard_map/ppermute | solution.py:48
  11.8 21.2 %collective-permute-start.2 = (bf16[192,2048]{1,0:T(8,128)(2,1)}, bf16[192,2048]{1,0:T(8,128)(2,1)S(1)}, u32[]{:S(2)}, u32[]{:S(2)}) collective-permute-start(bf16[192,2048]{1,0:T(8,128)(2,1)} %refs_2_.2), channel_id=1, source_target_pairs={{0,1},{1,0},{2,3},{3,2},{4,5},{5,4},{6,7},{7,6},{8,9},{9,8},{10,11... | collective-permute-start | bytes 2359304 | tf_op jit(solution)/shard_map/ppermute | solution.py:48
  28.5 8.8 %collective-permute-start.5 = (bf16[192,2048]{1,0:T(8,128)(2,1)S(1)}, bf16[192,2048]{1,0:T(8,128)(2,1)S(1)}, u32[]{:S(2)}, u32[]{:S(2)}) collective-permute-start(bf16[192,2048]{1,0:T(8,128)(2,1)S(1)} %collective-permute-done.refs_1_), channel_id=1, source_target_pairs={{0,1},{1,0},{2,3},{3,2},{4,5},{5,4},{6,7},{7,6},{8,9},{9,8},{10,11... | collective-permute-start | bytes 2359304 | tf_op jit(solution)/shard_map/ppermute | solution.py:48
  28.5 8.8 %collective-permute-start.4 = (bf16[192,2048]{1,0:T(8,128)(2,1)S(1)}, bf16[192,2048]{1,0:T(8,128)(2,1)S(1)}, u32[]{:S(2)}, u32[]{:S(2)}) collective-permute-start(bf16[192,2048]{1,0:T(8,128)(2,1)S(1)} %collective-permute-done.3.refs_0_), channel_id=1, source_target_pairs={{0,1},{1,0},{2,3},{3,2},{4,5},{5,4},{6,7},{7,6},{8,9},{9,8},{10,11... | collective-permute-start | bytes 2359304 | tf_op jit(solution)/shard_map/ppermute | solution.py:48
  31.5 12.1 %collective-permute-start.1 = (bf16[192,2048]{1,0:T(8,128)(2,1)S(1)}, bf16[192,2048]{1,0:T(8,128)(2,1)}, u32[]{:S(2)}, u32[]{:S(2)}) collective-permute-start(bf16[192,2048]{1,0:T(8,128)(2,1)S(1)} %collective-permute-done.refs_1_), channel_id=1, source_target_pairs={{0,2},{1,5},{2,0},{3,7},{4,6},{5,1},{6,4},{7,3},{8,10},{9,13},{10,... | collective-permute-start | bytes 2359304 | tf_op jit(solution)/shard_map/ppermute | solution.py:48
  90.0 12.1 %collective-permute-start.12 = (bf16[192,2048]{1,0:T(8,128)(2,1)S(1)}, bf16[192,2048]{1,0:T(8,128)(2,1)S(1)}, u32[]{:S(2)}, u32[]{:S(2)}) collective-permute-start(bf16[192,2048]{1,0:T(8,128)(2,1)S(1)} %get-tuple-element.370), channel_id=1, source_target_pairs={{0,2},{1,5},{2,0},{3,7},{4,6},{5,1},{6,4},{7,3},{8,10},{9,13},{10,... | collective-permute-start | bytes 2359304 | tf_op jit(solution)/shard_map/ppermute | solution.py:48
  102.4 19.5 %collective-permute-start.13 = (bf16[192,2048]{1,0:T(8,128)(2,1)S(1)}, bf16[192,2048]{1,0:T(8,128)(2,1)S(1)}, u32[]{:S(2)}, u32[]{:S(2)}) collective-permute-start(bf16[192,2048]{1,0:T(8,128)(2,1)S(1)} %add_convert_fusion.11), channel_id=1, source_target_pairs={{0,4},{1,3},{2,6},{3,1},{4,0},{5,7},{6,2},{7,5},{8,12},{9,11},{10,... | collective-permute-start | bytes 2359304 | tf_op jit(solution)/shard_map/ppermute | solution.py:48
  104.5 17.5 %collective-permute-start.11 = (bf16[192,2048]{1,0:T(8,128)(2,1)S(1)}, bf16[192,2048]{1,0:T(8,128)(2,1)S(1)}, u32[]{:S(2)}, u32[]{:S(2)}) collective-permute-start(bf16[192,2048]{1,0:T(8,128)(2,1)S(1)} %get-tuple-element.369), channel_id=1, source_target_pairs={{0,2},{1,5},{2,0},{3,7},{4,6},{5,1},{6,4},{7,3},{8,10},{9,13},{10,... | collective-permute-start | bytes 2359304 | tf_op jit(solution)/shard_map/ppermute | solution.py:48
  123.4 19.9 %collective-permute-start.14 = (bf16[192,2048]{1,0:T(8,128)(2,1)S(1)}, bf16[192,2048]{1,0:T(8,128)(2,1)S(1)}, u32[]{:S(2)}, u32[]{:S(2)}) collective-permute-start(bf16[192,2048]{1,0:T(8,128)(2,1)S(1)} %fusion.97.refs_2_), channel_id=1, source_target_pairs={{0,4},{1,3},{2,6},{3,1},{4,0},{5,7},{6,2},{7,5},{8,12},{9,11},{10,... | collective-permute-start | bytes 2359304 | tf_op jit(solution)/shard_map/ppermute | solution.py:48
  125.1 18.9 %collective-permute-start.17 = (bf16[192,2048]{1,0:T(8,128)(2,1)S(1)}, bf16[192,2048]{1,0:T(8,128)(2,1)S(1)}, u32[]{:S(2)}, u32[]{:S(2)}) collective-permute-start(bf16[192,2048]{1,0:T(8,128)(2,1)S(1)} %fusion.97.refs_2_), channel_id=1, source_target_pairs={{0,2},{1,5},{2,0},{3,7},{4,6},{5,1},{6,4},{7,3},{8,10},{9,13},{10,... | collective-permute-start | bytes 2359304 | tf_op jit(solution)/shard_map/ppermute | solution.py:48
  126.4 18.9 %collective-permute-start.16 = (bf16[192,2048]{1,0:T(8,128)(2,1)S(1)}, bf16[192,2048]{1,0:T(8,128)(2,1)S(1)}, u32[]{:S(2)}, u32[]{:S(2)}) collective-permute-start(bf16[192,2048]{1,0:T(8,128)(2,1)S(1)} %fusion.97.refs_2_), channel_id=1, source_target_pairs={{0,1},{1,0},{2,3},{3,2},{4,5},{5,4},{6,7},{7,6},{8,9},{9,8},{10,11... | collective-permute-start | bytes 2359304 | tf_op jit(solution)/shard_map/ppermute | solution.py:48
  127.7 37.9 %collective-permute-start.20 = (bf16[192,2048]{1,0:T(8,128)(2,1)S(1)}, bf16[192,2048]{1,0:T(8,128)(2,1)}, u32[]{:S(2)}, u32[]{:S(2)}) collective-permute-start(bf16[192,2048]{1,0:T(8,128)(2,1)S(1)} %fusion.97.refs_2_), channel_id=1, source_target_pairs={{0,16},{8,24},{16,0},{24,8},{1,17},{9,25},{17,1},{25,9},{2,18},{10... | collective-permute-start | bytes 2359304 | tf_op jit(solution)/shard_map/ppermute | solution.py:627
  143.3 8.6 %collective-permute-start.19 = (bf16[192,2048]{1,0:T(8,128)(2,1)S(1)}, bf16[192,2048]{1,0:T(8,128)(2,1)S(1)}, u32[]{:S(2)}, u32[]{:S(2)}) collective-permute-start(bf16[192,2048]{1,0:T(8,128)(2,1)S(1)} %collective-permute-done.14.refs_1_), channel_id=1, source_target_pairs={{0,1},{1,0},{2,3},{3,2},{4,5},{5,4},{6,7},{7,6},{8,9},{9,8},{10,11... | collective-permute-start | bytes 2359304 | tf_op jit(solution)/shard_map/ppermute | solution.py:48
  143.3 22.3 %collective-permute-start.15 = (bf16[192,2048]{1,0:T(8,128)(2,1)S(1)}, bf16[192,2048]{1,0:T(8,128)(2,1)S(1)}, u32[]{:S(2)}, u32[]{:S(2)}) collective-permute-start(bf16[192,2048]{1,0:T(8,128)(2,1)S(1)} %collective-permute-done.14.refs_1_), channel_id=1, source_target_pairs={{0,2},{1,5},{2,0},{3,7},{4,6},{5,1},{6,4},{7,3},{8,10},{9,13},{10,... | collective-permute-start | bytes 2359304 | tf_op jit(solution)/shard_map/ppermute | solution.py:48
  165.6 178.2 %all-gather.5.cloned.1.call-start = ((), (), s32[]{:S(2)}) async-start(), calls=%async_computation.2 | async-start | bytes 7077888 | tf_op jit(solution)/shard_map/all_gather | solution.py:630
  187.6 27.1 %collective-permute-start.24 = (bf16[192,2048]{1,0:T(8,128)(2,1)S(1)}, bf16[192,2048]{1,0:T(8,128)(2,1)S(1)}, u32[]{:S(2)}, u32[]{:S(2)}) collective-permute-start(bf16[192,2048]{1,0:T(8,128)(2,1)S(1)} %get-tuple-element.368), channel_id=1, source_target_pairs={{0,2},{1,5},{2,0},{3,7},{4,6},{5,1},{6,4},{7,3},{8,10},{9,13},{10,... | collective-permute-start | bytes 2359304 | tf_op jit(solution)/shard_map/ppermute | solution.py:48
  188.4 44.7 %collective-permute-start.23 = (bf16[192,2048]{1,0:T(8,128)(2,1)S(1)}, bf16[192,2048]{1,0:T(8,128)(2,1)S(1)}, u32[]{:S(2)}, u32[]{:S(2)}) collective-permute-start(bf16[192,2048]{1,0:T(8,128)(2,1)S(1)} %get-tuple-element.367), channel_id=1, source_target_pairs={{0,2},{1,5},{2,0},{3,7},{4,6},{5,1},{6,4},{7,3},{8,10},{9,13},{10,... | collective-permute-start | bytes 2359304 | tf_op jit(solution)/shard_map/ppermute | solution.py:48
  215.1 18.0 %collective-permute-start.25 = (bf16[192,2048]{1,0:T(8,128)(2,1)S(1)}, bf16[192,2048]{1,0:T(8,128)(2,1)S(1)}, u32[]{:S(2)}, u32[]{:S(2)}) collective-permute-start(bf16[192,2048]{1,0:T(8,128)(2,1)S(1)} %add_convert_fusion.8), channel_id=1, source_target_pairs={{0,4},{1,3},{2,6},{3,1},{4,0},{5,7},{6,2},{7,5},{8,12},{9,11},{10,... | collective-permute-start | bytes 2359304 | tf_op jit(solution)/shard_map/ppermute | solution.py:48
  235.3 25.1 %collective-permute-start.32 = (bf16[192,2048]{1,0:T(8,128)(2,1)S(1)}, bf16[192,2048]{1,0:T(8,128)(2,1)S(1)}, u32[]{:S(2)}, u32[]{:S(2)}) collective-permute-start(bf16[192,2048]{1,0:T(8,128)(2,1)S(1)} %fusion.41.refs_0_.refs_10_.refs_2_), channel_id=1, source_target_pairs={{0,1},{1,0},{2,3},{3,2},{4,5},{5,4},{6,7},{7,6},{8,9},{9,8},{10,11... | collective-permute-start | bytes 2359304 | tf_op jit(solution)/shard_map/ppermute | solution.py:48
  235.6 21.5 %collective-permute-start.26 = (bf16[192,2048]{1,0:T(8,128)(2,1)S(1)}, bf16[192,2048]{1,0:T(8,128)(2,1)S(1)}, u32[]{:S(2)}, u32[]{:S(2)}) collective-permute-start(bf16[192,2048]{1,0:T(8,128)(2,1)S(1)} %fusion.41.refs_0_.refs_10_.refs_2_), channel_id=1, source_target_pairs={{0,4},{1,3},{2,6},{3,1},{4,0},{5,7},{6,2},{7,5},{8,12},{9,11},{10,... | collective-permute-start | bytes 2359304 | tf_op jit(solution)/shard_map/ppermute | solution.py:48
  236.1 21.0 %collective-permute-start.29 = (bf16[192,2048]{1,0:T(8,128)(2,1)S(1)}, bf16[192,2048]{1,0:T(8,128)(2,1)S(1)}, u32[]{:S(2)}, u32[]{:S(2)}) collective-permute-start(bf16[192,2048]{1,0:T(8,128)(2,1)S(1)} %fusion.41.refs_0_.refs_10_.refs_2_), channel_id=1, source_target_pairs={{0,2},{1,5},{2,0},{3,7},{4,6},{5,1},{6,4},{7,3},{8,10},{9,13},{10,... | collective-permute-start | bytes 2359304 | tf_op jit(solution)/shard_map/ppermute | solution.py:48
  237.0 20.1 %collective-permute-start.27 = (bf16[192,1024]{1,0:T(8,128)(2,1)S(1)}, bf16[192,1024]{1,0:T(8,128)(2,1)S(1)}, u32[]{:S(2)}, u32[]{:S(2)}) collective-permute-start(bf16[192,1024]{1,0:T(8,128)(2,1)S(1)} %get-tuple-element.394), channel_id=1, source_target_pairs={{0,16},{8,24},{16,0},{24,8},{1,17},{9,25},{17,1},{25,9},{2,18},{10... | collective-permute-start | bytes 1179656 | tf_op jit(solution)/shard_map/ppermute | solution.py:627
  257.6 21.9 %collective-permute-start.28 = (bf16[192,2048]{1,0:T(8,128)(2,1)S(1)}, bf16[192,2048]{1,0:T(8,128)(2,1)S(1)}, u32[]{:S(2)}, u32[]{:S(2)}) collective-permute-start(bf16[192,2048]{1,0:T(8,128)(2,1)S(1)} %collective-permute-done.26.refs_1_.refs_9_), channel_id=1, source_target_pairs={{0,2},{1,5},{2,0},{3,7},{4,6},{5,1},{6,4},{7,3},{8,10},{9,13},{10,... | collective-permute-start | bytes 2359304 | tf_op jit(solution)/shard_map/ppermute | solution.py:48
  258.7 20.8 %collective-permute-start.33 = (bf16[192,1024]{1,0:T(8,128)(2,1)S(1)}, bf16[192,1024]{1,0:T(8,128)(2,1)S(1)}, u32[]{:S(2)}, u32[]{:S(2)}) collective-permute-start(bf16[192,1024]{1,0:T(8,128)(2,1)S(1)} %get-tuple-element.192), channel_id=1, source_target_pairs={{0,16},{8,24},{16,0},{24,8},{1,17},{9,25},{17,1},{25,9},{2,18},{10... | collective-permute-start | bytes 1179656 | tf_op jit(solution)/shard_map/ppermute | solution.py:627
  280.6 275.0 %reduce-scatter.2.cloned.1.call-start = ((), (), s32[]{:S(2)}) async-start(), calls=%async_computation.3 | async-start | bytes 5242880 | tf_op jit(solution)/shard_map/reduce_scatter | solution.py:135
  303.4 16.2 %collective-permute-start.35 = (bf16[768,2048]{1,0:T(8,128)(2,1)}, bf16[768,2048]{1,0:T(8,128)(2,1)}, u32[]{:S(2)}, u32[]{:S(2)}) collective-permute-start(bf16[768,2048]{1,0:T(8,128)(2,1)} %convolution_convert_fusion.1), channel_id=1, source_target_pairs={{0,1},{1,0},{2,3},{3,2},{4,5},{5,4},{6,7},{7,6},{8,9},{9,8},{10,11... | collective-permute-start | bytes 9437192 | tf_op jit(solution)/shard_map/ppermute | solution.py:48
  323.6 13.7 %collective-permute-start.36 = (bf16[192,2048]{1,0:T(8,128)(2,1)S(1)}, bf16[192,2048]{1,0:T(8,128)(2,1)S(1)}, u32[]{:S(2)}, u32[]{:S(2)}) collective-permute-start(bf16[192,2048]{1,0:T(8,128)(2,1)S(1)} %get-tuple-element.366), channel_id=1, source_target_pairs={{0,2},{1,5},{2,0},{3,7},{4,6},{5,1},{6,4},{7,3},{8,10},{9,13},{10,... | collective-permute-start | bytes 2359304 | tf_op jit(solution)/shard_map/ppermute | solution.py:48
  323.8 38.3 %collective-permute-start.38 = (bf16[192,2048]{1,0:T(8,128)(2,1)}, bf16[192,2048]{1,0:T(8,128)(2,1)}, u32[]{:S(2)}, u32[]{:S(2)}) collective-permute-start(bf16[192,2048]{1,0:T(8,128)(2,1)} %get-tuple-element.365), channel_id=1, source_target_pairs={{0,2},{1,5},{2,0},{3,7},{4,6},{5,1},{6,4},{7,3},{8,10},{9,13},{10,... | collective-permute-start | bytes 2359304 | tf_op jit(solution)/shard_map/ppermute | solution.py:48
  339.9 22.1 %collective-permute-start.37 = (bf16[192,2048]{1,0:T(8,128)(2,1)}, bf16[192,2048]{1,0:T(8,128)(2,1)}, u32[]{:S(2)}, u32[]{:S(2)}) collective-permute-start(bf16[192,2048]{1,0:T(8,128)(2,1)} %add_convert_fusion.5), channel_id=1, source_target_pairs={{0,4},{1,3},{2,6},{3,1},{4,0},{5,7},{6,2},{7,5},{8,12},{9,11},{10,... | collective-permute-start | bytes 2359304 | tf_op jit(solution)/shard_map/ppermute | solution.py:48
  370.3 20.1 %collective-permute-start.39 = (bf16[192,2048]{1,0:T(8,128)(2,1)S(1)}, bf16[192,2048]{1,0:T(8,128)(2,1)S(1)}, u32[]{:S(2)}, u32[]{:S(2)}) collective-permute-start(bf16[192,2048]{1,0:T(8,128)(2,1)S(1)} %get-tuple-element.253), channel_id=1, source_target_pairs={{0,4},{1,3},{2,6},{3,1},{4,0},{5,7},{6,2},{7,5},{8,12},{9,11},{10,... | collective-permute-start | bytes 2359304 | tf_op jit(solution)/shard_map/ppermute | solution.py:48
  372.3 19.0 %collective-permute-start.42 = (bf16[192,2048]{1,0:T(8,128)(2,1)S(1)}, bf16[192,2048]{1,0:T(8,128)(2,1)}, u32[]{:S(2)}, u32[]{:S(2)}) collective-permute-start(bf16[192,2048]{1,0:T(8,128)(2,1)S(1)} %get-tuple-element.253), channel_id=1, source_target_pairs={{0,2},{1,5},{2,0},{3,7},{4,6},{5,1},{6,4},{7,3},{8,10},{9,13},{10,... | collective-permute-start | bytes 2359304 | tf_op jit(solution)/shard_map/ppermute | solution.py:48
  372.5 23.1 %collective-permute-start.41 = (bf16[192,2048]{1,0:T(8,128)(2,1)S(1)}, bf16[192,2048]{1,0:T(8,128)(2,1)}, u32[]{:S(2)}, u32[]{:S(2)}) collective-permute-start(bf16[192,2048]{1,0:T(8,128)(2,1)S(1)} %get-tuple-element.253), channel_id=1, source_target_pairs={{0,1},{1,0},{2,3},{3,2},{4,5},{5,4},{6,7},{7,6},{8,9},{9,8},{10,11... | collective-permute-start | bytes 2359304 | tf_op jit(solution)/shard_map/ppermute | solution.py:48
  390.4 12.0 %collective-permute-start.40 = (bf16[192,2048]{1,0:T(8,128)(2,1)S(1)}, bf16[192,2048]{1,0:T(8,128)(2,1)S(1)}, u32[]{:S(2)}, u32[]{:S(2)}) collective-permute-start(bf16[192,2048]{1,0:T(8,128)(2,1)S(1)} %collective-permute-done.39), channel_id=1, source_target_pairs={{0,2},{1,5},{2,0},{3,7},{4,6},{5,1},{6,4},{7,3},{8,10},{9,13},{10,... | collective-permute-start | bytes 2359304 | tf_op jit(solution)/shard_map/ppermute | solution.py:48
  403.8 25.8 %collective-permute-start.46 = (bf16[256,1024]{1,0:T(8,128)(2,1)S(1)}, bf16[256,1024]{1,0:T(8,128)(2,1)S(1)}, u32[]{:S(2)}, u32[]{:S(2)}) collective-permute-start(bf16[256,1024]{1,0:T(8,128)(2,1)S(1)} %get-tuple-element.384), channel_id=1, source_target_pairs={{0,8},{8,0},{16,24},{24,16},{1,9},{9,1},{17,25},{25,17},{2,10},{10... | collective-permute-start | bytes 1572872 | tf_op jit(solution)/shard_map/ppermute | solution.py:741
  403.8 26.6 %collective-permute-start.47 = (bf16[256,1024]{1,0:T(8,128)(2,1)S(1)}, bf16[256,1024]{1,0:T(8,128)(2,1)S(1)}, u32[]{:S(2)}, u32[]{:S(2)}) collective-permute-start(bf16[256,1024]{1,0:T(8,128)(2,1)S(1)} %get-tuple-element.383), channel_id=1, source_target_pairs={{0,8},{8,0},{16,24},{24,16},{1,9},{9,1},{17,25},{25,17},{2,10},{10... | collective-permute-start | bytes 1572872 | tf_op jit(solution)/shard_map/ppermute | solution.py:741
  405.8 35.3 %collective-permute-start.51 = (bf16[256,1024]{1,0:T(8,128)(2,1)}, bf16[256,1024]{1,0:T(8,128)(2,1)}, u32[]{:S(2)}, u32[]{:S(2)}) collective-permute-start(bf16[256,1024]{1,0:T(8,128)(2,1)} %get-tuple-element.376), channel_id=1, source_target_pairs={{0,8},{8,0},{16,24},{24,16},{1,9},{9,1},{17,25},{25,17},{2,10},{10... | collective-permute-start | bytes 1572872 | tf_op jit(solution)/shard_map/ppermute | solution.py:741
  405.8 49.5 %collective-permute-start.55 = (bf16[256,1024]{1,0:T(8,128)(2,1)}, bf16[256,1024]{1,0:T(8,128)(2,1)}, u32[]{:S(2)}, u32[]{:S(2)}) collective-permute-start(bf16[256,1024]{1,0:T(8,128)(2,1)} %get-tuple-element.375), channel_id=1, source_target_pairs={{0,8},{8,0},{16,24},{24,16},{1,9},{9,1},{17,25},{25,17},{2,10},{10... | collective-permute-start | bytes 1572872 | tf_op jit(solution)/shard_map/ppermute | solution.py:741
  407.8 55.2 %collective-permute-start.56 = (bf16[256,1024]{1,0:T(8,128)(2,1)}, bf16[256,1024]{1,0:T(8,128)(2,1)S(1)}, u32[]{:S(2)}, u32[]{:S(2)}) collective-permute-start(bf16[256,1024]{1,0:T(8,128)(2,1)} %get-tuple-element.374), channel_id=1, source_target_pairs={{0,8},{8,0},{16,24},{24,16},{1,9},{9,1},{17,25},{25,17},{2,10},{10... | collective-permute-start | bytes 1572872 | tf_op jit(solution)/shard_map/ppermute | solution.py:741
  469.9 10.3 %collective-permute-start.57 = (bf16[768,2048]{1,0:T(8,128)(2,1)}, bf16[768,2048]{1,0:T(8,128)(2,1)S(1)}, u32[]{:S(2)}, u32[]{:S(2)}) collective-permute-start(bf16[768,2048]{1,0:T(8,128)(2,1)} %convolution_convert_fusion.3), channel_id=1, source_target_pairs={{0,1},{1,0},{2,3},{3,2},{4,5},{5,4},{6,7},{7,6},{8,9},{9,8},{10,11... | collective-permute-start | bytes 9437192 | tf_op jit(solution)/shard_map/ppermute | solution.py:48
  470.0 35.0 %collective-permute-start.61 = (bf16[256,1024]{1,0:T(8,128)(2,1)}, bf16[256,1024]{1,0:T(8,128)(2,1)}, u32[]{:S(2)}, u32[]{:S(2)}) collective-permute-start(bf16[256,1024]{1,0:T(8,128)(2,1)} %get-tuple-element.373), channel_id=1, source_target_pairs={{0,8},{8,0},{16,24},{24,16},{1,9},{9,1},{17,25},{25,17},{2,10},{10... | collective-permute-start | bytes 1572872 | tf_op jit(solution)/shard_map/ppermute | solution.py:741
  470.4 49.6 %collective-permute-start.52 = (f32[8192]{0:T(1024)S(1)}, f32[8192]{0:T(1024)S(1)}, u32[]{:S(2)}, u32[]{:S(2)}) collective-permute-start(f32[8192]{0:T(1024)S(1)} %bitcast.130), channel_id=1, source_target_pairs={{0,8},{8,0},{16,24},{24,16},{1,9},{9,1},{17,25},{25,17},{2,10},{10... | collective-permute-start | bytes 98312 | tf_op jit(solution)/shard_map/ppermute | solution.py:159
  472.2 47.8 %collective-permute-start.53 = (f32[8192]{0:T(1024)S(1)}, f32[8192]{0:T(1024)S(1)}, u32[]{:S(2)}, u32[]{:S(2)}) collective-permute-start(f32[8192]{0:T(1024)S(1)} %bitcast.131), channel_id=1, source_target_pairs={{0,16},{8,24},{16,0},{24,8},{1,17},{9,25},{17,1},{25,9},{2,18},{10... | collective-permute-start | bytes 98312 | tf_op jit(solution)/shard_map/ppermute | solution.py:159
  473.6 46.5 %collective-permute-start.54 = (f32[8192]{0:T(1024)S(1)}, f32[8192]{0:T(1024)S(1)}, u32[]{:S(2)}, u32[]{:S(2)}) collective-permute-start(f32[8192]{0:T(1024)S(1)} %bitcast.132), channel_id=1, source_target_pairs={{0,24},{8,16},{16,8},{24,0},{1,25},{9,17},{17,9},{25,1},{2,26},{10... | collective-permute-start | bytes 98312 | tf_op jit(solution)/shard_map/ppermute | solution.py:159
  482.5 16.4 %collective-permute-start.59 = (bf16[192,2048]{1,0:T(8,128)(2,1)}, bf16[192,2048]{1,0:T(8,128)(2,1)}, u32[]{:S(2)}, u32[]{:S(2)}) collective-permute-start(bf16[192,2048]{1,0:T(8,128)(2,1)} %get-tuple-element.364), channel_id=1, source_target_pairs={{0,2},{1,5},{2,0},{3,7},{4,6},{5,1},{6,4},{7,3},{8,10},{9,13},{10,... | collective-permute-start | bytes 2359304 | tf_op jit(solution)/shard_map/ppermute | solution.py:48
  498.9 18.2 %collective-permute-start.58 = (bf16[192,2048]{1,0:T(8,128)(2,1)S(1)}, bf16[192,2048]{1,0:T(8,128)(2,1)S(1)}, u32[]{:S(2)}, u32[]{:S(2)}) collective-permute-start(bf16[192,2048]{1,0:T(8,128)(2,1)S(1)} %copy-done.113), channel_id=1, source_target_pairs={{0,2},{1,5},{2,0},{3,7},{4,6},{5,1},{6,4},{7,3},{8,10},{9,13},{10,... | collective-permute-start | bytes 2359304 | tf_op jit(solution)/shard_map/ppermute | solution.py:48
  505.0 12.1 %collective-permute-start.60 = (bf16[192,2048]{1,0:T(8,128)(2,1)S(1)}, bf16[192,2048]{1,0:T(8,128)(2,1)S(1)}, u32[]{:S(2)}, u32[]{:S(2)}) collective-permute-start(bf16[192,2048]{1,0:T(8,128)(2,1)S(1)} %add_convert_fusion.2), channel_id=1, source_target_pairs={{0,4},{1,3},{2,6},{3,1},{4,0},{5,7},{6,2},{7,5},{8,12},{9,11},{10,... | collective-permute-start | bytes 2359304 | tf_op jit(solution)/shard_map/ppermute | solution.py:48
  (173 other events, 1184.6 us)
Sparse Core Ops, SparseCore 0:
  165.7 53.9 all-gather.2
  280.7 44.2 all-gather.4
  470.2 85.3 reduce-scatter.1
